TPU v7x, 128 devices: a whole 4x4x4 slice. The times are simulated.
128 devices in a mesh: gx: 8 (over z, core), gy: 16 (over y, x).
Axes of the slice: x: 4, y: 4, z: 4, core: 2. Of those that a mesh axis runs over, the one named last changes fastest.
Arguments:
- old_state: float32 [8, 128, 3, 128, 128], P('gx', 'gy'), as said below
- old_dest: int32 [8, 128], P('gx', 'gy'), may hold values from -1 to 127, as said below
- refine: int32 [8, 128], P('gx', 'gy'), may hold values from 0 to 1, as said below
- parent_block: int32 [8, 128], P('gx', 'gy'), may hold values from 0 to 63, as said below
- coarse_state: float32 [16, 16, 3, 128, 128], P('gx', 'gy'), as said below
- force: float32 [2, 1024, 16384], P(None, 'gx', 'gy'), may hold values from -6 to 6
Outputs:
- depth_out: float32 [1024, 16384], P('gx', 'gy')
- velocity_out: float32 [2, 1024, 16384], P(None, 'gx', 'gy')
Inputs may be any that keep to these rules, and one draw needn't show every extreme that they name: `old_state`: channel 0 of each patch is the water depth, between 0.5 and 2. `coarse_state`: channel 0 of each patch is the water depth, between 0.5 and 2. `old_dest`: A new column is device times 8 plus position within the device, in the same gx row. The slots of one device go to different devices, at most one to each device of its gy row; every position whose refine is 0 receives exactly one slot, a refined one none. In one gx row, the slot at a given position within its device goes the same number of devices onward along gy (modulo 16) on every device, or is -1. `refine`: A device holds at most 2 refined patches; in every gx row some device holds exactly 2. `parent_block`: the parents of all patches of one device lie on one device of its gy column. Quadrant 0 is low first and low second index, 1 low and high, 2 high and low, 3 high and high.
All inputs are finite; a program needn't handle non-finite values.
Results may differ from a plain program's by a relative error of at most 0.0003.
Values sent between devices are 32-bit elements; how exact they have to be, the bound alone decides.
No kernel may reach another device: no remote copies, remote signals or barrier semaphores. Data moves between devices by JAX's collectives and lax.ppermute only.
A program may use at most 64 MiB of HBM per device.

v0:
```python
import functools

import jax
import jax.numpy as jnp
from jax import lax
from jax.experimental import pallas as pl
from jax.experimental.pallas import tpu as pltpu
from jax.sharding import PartitionSpec as P

CELLS = 128
FIELDS = 3
SWEEPS = 6
SLOTS = 8
PEERS = 16
HALO = 8
WIDTH = SLOTS * CELLS
EXT_ROWS = CELLS + 2 * HALO
EXT_COLS = WIDTH + CELLS
OMEGA = 0.8
TIME_STEP = 0.5

VMEM_LIMIT = 40 * 1024 * 1024
in_vmem = pl.BlockSpec(memory_space=pltpu.VMEM)
in_smem = pl.BlockSpec(memory_space=pltpu.SMEM)
in_any = pl.BlockSpec(memory_space=pl.ANY)


def params():
    return pltpu.CompilerParams(vmem_limit_bytes=VMEM_LIMIT)


def stage_kernel(dest, old, out, sems):
    def copy(slot, peer):
        return pltpu.make_async_copy(old.at[slot], out.at[peer], sems.at[slot])

    for slot in range(SLOTS):
        target = dest[slot]

        @pl.when(target >= 0)
        def _(slot=slot, target=target):
            copy(slot, target // SLOTS).start()

    for slot in range(SLOTS):
        target = dest[slot]

        @pl.when(target >= 0)
        def _(slot=slot, target=target):
            copy(slot, target // SLOTS).wait()


def stage(dest, old):
    return pl.pallas_call(
        stage_kernel,
        out_shape=jax.ShapeDtypeStruct((PEERS, FIELDS, CELLS, CELLS), jnp.float32),
        in_specs=[in_smem, in_any],
        out_specs=in_any,
        scratch_shapes=[pltpu.SemaphoreType.DMA((SLOTS,))],
        compiler_params=params(),
        name="stage_outgoing",
    )(dest, old)


def spread(quarter, fine_axis):
    fine = lax.broadcasted_iota(jnp.int32, (CELLS, CELLS), fine_axis)
    coarse = lax.broadcasted_iota(jnp.int32, (CELLS, CELLS), 1 - fine_axis)
    half = CELLS // 2
    middle = lax.shift_right_logical(fine, 1)
    beside = jnp.where((fine & 1) == 0, middle - 1, middle + 1)
    beside = jnp.clip(beside, 0, half - 1)
    base = quarter * half
    near = jnp.where(coarse == base + middle, 0.75, 0.0)
    far = jnp.where(coarse == base + beside, 0.25, 0.0)
    return (near + far).astype(jnp.bfloat16)


def split_two(value):
    high = value.astype(jnp.bfloat16)
    low = (value - high.astype(jnp.float32)).astype(jnp.bfloat16)
    return high, low


def dot(a, b):
    return jnp.dot(a, b, preferred_element_type=jnp.float32)


def assemble_kernel(
    source, refine, code, arrived, pieces, force, depth, rhs, left, right, rows, force_v, sems, force_sem
):
    force_copy = pltpu.make_async_copy(force, force_v, force_sem)
    force_copy.start()

    def copies(origin, index, slot):
        cols = pl.ds(slot * CELLS, CELLS)
        return (
            pltpu.make_async_copy(origin.at[index, 0], depth.at[:, cols], sems.at[slot, 0]),
            pltpu.make_async_copy(origin.at[index, 1], rhs.at[0, :, cols], sems.at[slot, 1]),
            pltpu.make_async_copy(origin.at[index, 2], rhs.at[1, :, cols], sems.at[slot, 2]),
        )

    for slot in range(SLOTS):

        @pl.when(refine[slot] > 0)
        def _(slot=slot):
            for copy in copies(pieces, code[slot] // 4, slot):
                copy.start()

        @pl.when(refine[slot] <= 0)
        def _(slot=slot):
            for copy in copies(arrived, source[slot], slot):
                copy.start()

    force_copy.wait()
    for slot in range(SLOTS):
        for copy in copies(arrived, 0, slot):
            copy.wait()
        cols = slice(slot * CELLS, (slot + 1) * CELLS)

        @pl.when(refine[slot] > 0)
        def _(slot=slot, cols=cols):
            quadrant = code[slot] % 4
            along_rows = spread(quadrant // 2, 0)
            along_cols = spread(quadrant % 2, 1)
            for field in range(FIELDS):
                place = depth if field == 0 else rhs.at[field - 1]
                high, low = split_two(place[:, cols])
                done = dot(along_rows, high) + dot(along_rows, low)
                high, low = split_two(done)
                place[:, cols] = dot(high, along_cols) + dot(low, along_cols)

        for field in range(2):
            rhs[field, :, cols] = rhs[field, :, cols] + TIME_STEP * force_v[field, :, cols]

    for field in range(FIELDS):
        place = depth if field == 0 else rhs.at[field - 1]
        left[field] = place[:, :CELLS].T[:HALO]
        right[field] = place[:, WIDTH - CELLS :].T[CELLS - HALO :]
        rows[0, field] = place[:HALO, :]
        rows[1, field] = place[CELLS - HALO :, :]


def assemble(source, refine, code, arrived, pieces, force):
    f32 = jnp.float32
    return pl.pallas_call(
        assemble_kernel,
        out_shape=(
            jax.ShapeDtypeStruct((CELLS, WIDTH), f32),
            jax.ShapeDtypeStruct((2, CELLS, WIDTH), f32),
            jax.ShapeDtypeStruct((FIELDS, HALO, CELLS), f32),
            jax.ShapeDtypeStruct((FIELDS, HALO, CELLS), f32),
            jax.ShapeDtypeStruct((2, FIELDS, HALO, WIDTH), f32),
        ),
        in_specs=[in_smem] * 3 + [in_any] * 3,
        out_specs=[in_vmem] * 5,
        scratch_shapes=[
            pltpu.VMEM((2, CELLS, WIDTH), f32),
            pltpu.SemaphoreType.DMA((SLOTS, FIELDS)),
            pltpu.SemaphoreType.DMA,
        ],
        compiler_params=params(),
        name="assemble_patches",
    )(source, refine, code, arrived, pieces, force)


def edge_kernel(rows, from_left, from_right, top, bottom, side):
    blank = jnp.zeros((CELLS - 2 * HALO, CELLS), jnp.float32)
    for field in range(FIELDS):
        tile = jnp.concatenate([from_right[field], blank, from_left[field]], axis=0).T
        side[field] = tile
        top[field, :, :WIDTH] = rows[0, field]
        top[field, :, WIDTH:] = tile[:HALO]
        bottom[field, :, :WIDTH] = rows[1, field]
        bottom[field, :, WIDTH:] = tile[CELLS - HALO :]


def edges(rows, from_left, from_right):
    f32 = jnp.float32
    return pl.pallas_call(
        edge_kernel,
        out_shape=(
            jax.ShapeDtypeStruct((FIELDS, HALO, EXT_COLS), f32),
            jax.ShapeDtypeStruct((FIELDS, HALO, EXT_COLS), f32),
            jax.ShapeDtypeStruct((FIELDS, CELLS, CELLS), f32),
        ),
        in_specs=[in_vmem] * 3,
        out_specs=[in_vmem] * 3,
        compiler_params=params(),
        name="edge_rows",
    )(rows, from_left, from_right)


TILES = EXT_ROWS // 8


def sweep_kernel(depth, rhs, side, above, below, out, high, right, velo, north, south, west, east):
    def gather(place, field, own):
        place[:HALO] = above[field]
        place[HALO + CELLS :] = below[field]
        place[HALO : HALO + CELLS, :WIDTH] = own
        place[HALO : HALO + CELLS, WIDTH:] = side[field]

    gather(high, 0, depth[...])
    gather(right.at[0], 1, rhs[0])
    gather(right.at[1], 2, rhs[1])

    row = lax.broadcasted_iota(jnp.int32, (8, EXT_COLS), 0)

    def tile(place, t):
        return place[pl.ds(min(max(t, 0), TILES - 1) * 8, 8), :]

    def around(place, t):
        here, before, after = tile(place, t), tile(place, t - 1), tile(place, t + 1)
        up = jnp.where(row == 0, pltpu.roll(before, 1, 0), pltpu.roll(here, 1, 0))
        down = jnp.where(row == 7, pltpu.roll(after, 7, 0), pltpu.roll(here, 7, 0))
        return here, up, down, pltpu.roll(here, 1, 1), pltpu.roll(here, EXT_COLS - 1, 1)

    def weight(a, b):
        mean = (a + b) * 0.5
        return mean * mean * mean * (1.0 / 3.0)

    for t in range(TILES):
        at = slice(t * 8, t * 8 + 8)
        here, *others = around(high, t)
        faces = [weight(here, other) for other in others]
        diagonal = here + faces[0] + faces[1] + faces[2] + faces[3]
        inside = here > 0.0
        scale = jnp.where(inside, OMEGA / jnp.where(inside, diagonal, 1.0), 0.0)
        for place, face in zip((north, south, west, east), faces):
            place[at, :] = face * scale
        for field in range(2):
            start = right[field, at, :] * scale
            right[field, at, :] = start
            velo[0, field, at, :] = start

    def step(s, _):
        now = s % 2
        for t in range(TILES):
            at = slice(t * 8, t * 8 + 8)
            weights = [place[at, :] for place in (north, south, west, east)]
            for field in range(2):
                here, *others = around(velo.at[now, field], t)
                total = right[field, at, :] + (1.0 - OMEGA) * here
                for w, other in zip(weights, others):
                    total = total + w * other
                velo[1 - now, field, at, :] = total
        return 0

    lax.fori_loop(0, SWEEPS - 1, step, 0)
    last = (SWEEPS - 1) % 2
    out[...] = velo[last, :, HALO : HALO + CELLS, :WIDTH]


def sweeps(depth, rhs, side, above, below):
    f32 = jnp.float32
    ext = (EXT_ROWS, EXT_COLS)
    return pl.pallas_call(
        sweep_kernel,
        out_shape=jax.ShapeDtypeStruct((2, CELLS, WIDTH), f32),
        in_specs=[in_vmem] * 5,
        out_specs=in_vmem,
        scratch_shapes=[
            pltpu.VMEM(ext, f32),
            pltpu.VMEM((2,) + ext, f32),
            pltpu.VMEM((2, 2) + ext, f32),
        ]
        + [pltpu.VMEM(ext, f32)] * 4,
        compiler_params=params(),
        name="jacobi_sweeps",
    )(depth, rhs, side, above, below)


def moved(value, axis, step):
    count = lax.axis_size(axis)
    pairs = [(i, i + step) for i in range(count) if 0 <= i + step < count]
    return lax.ppermute(value, axis, pairs)


def body(old_state, old_dest, refine, parent_block, coarse_state, force):
    dest = old_dest[0]
    table = lax.all_gather(dest, "gy", axis=0)
    pieces = lax.all_gather(coarse_state[:, 0], "gx", axis=0, tiled=True)
    outgoing = stage(dest, old_state[0])
    arrived = lax.all_to_all(outgoing, "gy", split_axis=0, concat_axis=0, tiled=True)
    place = table - lax.axis_index("gy") * SLOTS
    hit = place[None] == jnp.arange(SLOTS, dtype=jnp.int32)[:, None, None]
    peer = jnp.arange(PEERS, dtype=jnp.int32)[None, :, None]
    source = jnp.max(jnp.where(hit, peer, 0), axis=(1, 2))
    depth, rhs, left, right, rows = assemble(
        source, refine[0], parent_block[0], arrived, pieces, force
    )
    from_left = moved(right, "gy", 1)
    from_right = moved(left, "gy", -1)
    top, bottom, side = edges(rows, from_left, from_right)
    above = moved(bottom, "gx", 1)
    below = moved(top, "gx", -1)
    velocity = sweeps(depth, rhs, side, above, below)
    return depth, velocity


def solution(mesh):
    return jax.shard_map(
        body,
        mesh=mesh,
        in_specs=(
            P("gx", "gy", None, None, None),
            P("gx", "gy"),
            P("gx", "gy"),
            P("gx", "gy"),
            P("gx", "gy", None, None, None),
            P(None, "gx", "gy"),
        ),
        out_specs=(P("gx", "gy"), P(None, "gx", "gy")),
        check_vma=False,
    )
```

profile of v0, /device:TPU:7, one launch (start us, length us, event | category | flops | bytes accessed | tf_op | source)
XLA Modules:
  0.0 118.7 jit_solution(3828678199022821733)
XLA Ops:
  7.2 0.0 all-gather.4.cloned.1.call-start
  7.2 0.7 all-gather.4.cloned.1.call-update
  7.9 1.4 %copy-done.1 = f32[1,8,3,128,128]{4,3,2,1,0:T(8,128)S(1)} copy-done((f32[1,8,3,128,128]{4,3,2,1,0:T(8,128)S(1)}, f32[1,8,3,128,128]{4,3,2,1,0:T(8,128)}, u32[]{:S(2)}) %copy-start.1) | copy-done | bytes 1572888
  9.3 0.7 copy-done.4
  10.0 1.6 %stage_outgoing.1 = f32[16,3,128,128]{3,2,1,0:T(8,128)} custom-call(s32[8]{0:T(128)S(1)} %bitcast.10, f32[8,3,128,128]{3,2,1,0:T(8,128)S(1)} %bitcast.9), custom_call_target="tpu_custom_call" | custom-call | tf_op jit(solution)/shard_map/stage_outgoing/pallas_call | solution.py:52
  11.6 0.0 copy-start.6
  11.6 0.0 copy-start.7
  11.6 7.0 %all-to-all-start = ((f32[16,3,128,128]{3,2,1,0:T(8,128)}), f32[16,3,128,128]{3,2,1,0:T(8,128)S(1)}, u32[]{:S(2)}, u32[]{:S(2)}) async-start(f32[16,3,128,128]{3,2,1,0:T(8,128)} %stage_outgoing.1), calls=%async_computation | async-start | bytes 6291456 | tf_op jit(solution)/shard_map/all_to_all | solution.py:282
  18.6 52.0 %all-gather.1 = s32[16,1,8]{2,1,0:T(1,128)S(1)} all-gather(s32[1,1,8]{2,1,0:T(1,128)S(1)} %bitcast.11), channel_id=1, replica_groups=mesh['gx'=8,'gy'=16] {'gy'}, dimensions={0}, use_global_device_ids=true | all-gather | bytes 544 | tf_op jit(solution)/shard_map/all_gather | solution.py:279
  70.6 0.1 copy.13
  70.7 0.2 select_reduce_fusion.source
  70.9 0.0 all-gather.4.cloned.1.call-done
  71.0 1.9 %copy-done = f32[16,1,3,128,128]{4,3,2,1,0:T(8,128)S(1)} copy-done((f32[16,1,3,128,128]{4,3,2,1,0:T(8,128)S(1)}, f32[16,1,3,128,128]{4,3,2,1,0:T(8,128)}, u32[]{:S(2)}) %copy-start) | copy-done | bytes 3145752
  72.9 1.2 %copy-done.2 = f32[2,128,1024]{2,1,0:T(8,128)S(1)} copy-done((f32[2,128,1024]{2,1,0:T(8,128)S(1)}, f32[2,128,1024]{2,1,0:T(8,128)}, u32[]{:S(2)}) %copy-start.2) | copy-done | bytes 1048600
  74.1 3.1 %assemble_patches.1 = (f32[128,1024]{1,0:T(8,128)}, f32[2,128,1024]{2,1,0:T(8,128)S(1)}, f32[3,8,128]{2,1,0:T(8,128)S(1)}, f32[3,8,128]{2,1,0:T(8,128)S(1)}, f32[2,3,8,1024]{3,2,1,0:T(8,128)S(1)}) custom-call(s32[8]{0:T(128)S(1)} %select_reduce_fusion.source, s32[8]{0:T(128)S(1)} %bitcast.12, s32[8]{0:T(128)S(1)} %bitcast.13, ...), custom_call_target="tpu_custom_call" | custom-call | tf_op jit(solution)/shard_map/assemble_patches/pallas_call | solution.py:143
  77.2 3.0 %collective-permute-start = (f32[3,8,128]{2,1,0:T(8,128)S(1)}, f32[3,8,128]{2,1,0:T(8,128)S(1)}, u32[]{:S(2)}, u32[]{:S(2)}) collective-permute-start(f32[3,8,128]{2,1,0:T(8,128)S(1)} %get-tuple-element.13), channel_id=1, source_target_pairs={{0,1},{1,2},{2,3},{3,4},{4,5},{5,6},{6,7},{7,8},{8,9},{9,10},{10,1... | collective-permute-start | bytes 36872 | tf_op jit(solution)/shard_map/ppermute | solution.py:274
  80.2 2.3 %collective-permute-start.1 = (f32[3,8,128]{2,1,0:T(8,128)S(1)}, f32[3,8,128]{2,1,0:T(8,128)S(1)}, u32[]{:S(2)}, u32[]{:S(2)}) collective-permute-start(f32[3,8,128]{2,1,0:T(8,128)S(1)} %get-tuple-element.14), channel_id=1, source_target_pairs={{1,0},{2,1},{3,2},{4,3},{5,4},{6,5},{7,6},{8,7},{9,8},{10,9},{11,1... | collective-permute-start | bytes 36872 | tf_op jit(solution)/shard_map/ppermute | solution.py:274
  82.5 4.3 %collective-permute-done.1.from_right = f32[3,8,128]{2,1,0:T(8,128)S(1)} collective-permute-done((f32[3,8,128]{2,1,0:T(8,128)S(1)}, f32[3,8,128]{2,1,0:T(8,128)S(1)}, u32[]{:S(2)}, u32[]{:S(2)}) %collective-permute-start.1) | collective-permute-done | bytes 12320 | tf_op jit(solution)/shard_map/ppermute | solution.py:274
  86.7 0.1 edge_rows.1
  86.9 10.2 %collective-permute-start.2 = (f32[3,8,1152]{2,1,0:T(8,128)S(1)}, f32[3,8,1152]{2,1,0:T(8,128)S(1)}, u32[]{:S(2)}, u32[]{:S(2)}) collective-permute-start(f32[3,8,1152]{2,1,0:T(8,128)S(1)} %get-tuple-element.16), channel_id=1, source_target_pairs={{0,16},{16,32},{32,48},{48,64},{64,80},{80,96},{96,112},{1,17},{17... | collective-permute-start | bytes 331784 | tf_op jit(solution)/shard_map/ppermute | solution.py:274
  97.1 1.9 %collective-permute-start.3 = (f32[3,8,1152]{2,1,0:T(8,128)S(1)}, f32[3,8,1152]{2,1,0:T(8,128)S(1)}, u32[]{:S(2)}, u32[]{:S(2)}) collective-permute-start(f32[3,8,1152]{2,1,0:T(8,128)S(1)} %get-tuple-element.17), channel_id=1, source_target_pairs={{16,0},{32,16},{48,32},{64,48},{80,64},{96,80},{112,96},{17,1},{33... | collective-permute-start | bytes 331784 | tf_op jit(solution)/shard_map/ppermute | solution.py:274
  99.1 4.1 %collective-permute-done.3.below = f32[3,8,1152]{2,1,0:T(8,128)S(1)} collective-permute-done((f32[3,8,1152]{2,1,0:T(8,128)S(1)}, f32[3,8,1152]{2,1,0:T(8,128)S(1)}, u32[]{:S(2)}, u32[]{:S(2)}) %collective-permute-start.3) | collective-permute-done | bytes 110624 | tf_op jit(solution)/shard_map/ppermute | solution.py:274
  103.2 1.0 copy-done.3
  104.2 7.7 %jacobi_sweeps.1 = f32[2,128,1024]{2,1,0:T(8,128)} custom-call(f32[128,1024]{1,0:T(8,128)S(1)} %copy-done.3, f32[2,128,1024]{2,1,0:T(8,128)S(1)} %get-tuple-element.11.rhs, f32[3,128,128]{2,1,0:T(8,128)S(1)} %get-tuple-element.15.side, f32[3,8,1152]{2,1,0:T(8,128)S(1)} %collective-permute-done.2.above, f32[3,8,1152]{2,1,0:T(8,128)S(1)} %collective-permute-done.3.below), custom_call_target="tpu_custom_call" | custom-call | tf_op jit(solution)/shard_map/jacobi_sweeps/pallas_call | solution.py:255
  (13 shorter events, 0.0 us)
Async XLA Ops:
  7.2 63.8 %all-gather.4.cloned.1.call-start = ((), (), s32[]{:S(2)}) async-start(), calls=%async_computation.1 | async-start | bytes 3538944 | tf_op jit(solution)/shard_map/all_gather | solution.py:280
  7.9 1.4 %copy-start.1 = (f32[1,8,3,128,128]{4,3,2,1,0:T(8,128)S(1)}, f32[1,8,3,128,128]{4,3,2,1,0:T(8,128)}, u32[]{:S(2)}) copy-start(f32[1,8,3,128,128]{4,3,2,1,0:T(8,128)} %param.6) | copy-start | bytes 4718596
  9.3 0.7 copy-start.4
  11.6 7.0 %copy-start.5 = (s32[1,8]{1,0:T(1,128)S(1)}, s32[1,8]{1,0:T(1,128)}, u32[]{:S(2)}) copy-start(s32[1,8]{1,0:T(1,128)} %param.7) | copy-start | bytes 100
  11.6 59.4 %copy-start.6 = (s32[1,8]{1,0:T(1,128)S(1)}, s32[1,8]{1,0:T(1,128)}, u32[]{:S(2)}) copy-start(s32[1,8]{1,0:T(1,128)} %param.8) | copy-start | bytes 100
  11.6 59.4 %copy-start.7 = (s32[1,8]{1,0:T(1,128)S(1)}, s32[1,8]{1,0:T(1,128)}, u32[]{:S(2)}) copy-start(s32[1,8]{1,0:T(1,128)} %param.9) | copy-start | bytes 100
  11.6 59.3 %all-to-all-start = ((f32[16,3,128,128]{3,2,1,0:T(8,128)}), f32[16,3,128,128]{3,2,1,0:T(8,128)S(1)}, u32[]{:S(2)}, u32[]{:S(2)}) async-start(f32[16,3,128,128]{3,2,1,0:T(8,128)} %stage_outgoing.1), calls=%async_computation | async-start | bytes 6291456 | tf_op jit(solution)/shard_map/all_to_all | solution.py:282
  71.0 1.9 %copy-start = (f32[16,1,3,128,128]{4,3,2,1,0:T(8,128)S(1)}, f32[16,1,3,128,128]{4,3,2,1,0:T(8,128)}, u32[]{:S(2)}) copy-start(f32[16,1,3,128,128]{4,3,2,1,0:T(8,128)} %all-gather.4.cloned.1.call-done) | copy-start | bytes 9437188
  72.9 1.2 %copy-start.2 = (f32[2,128,1024]{2,1,0:T(8,128)S(1)}, f32[2,128,1024]{2,1,0:T(8,128)}, u32[]{:S(2)}) copy-start(f32[2,128,1024]{2,1,0:T(8,128)} %force.1) | copy-start | bytes 3145732
  77.2 5.3 %collective-permute-start = (f32[3,8,128]{2,1,0:T(8,128)S(1)}, f32[3,8,128]{2,1,0:T(8,128)S(1)}, u32[]{:S(2)}, u32[]{:S(2)}) collective-permute-start(f32[3,8,128]{2,1,0:T(8,128)S(1)} %get-tuple-element.13), channel_id=1, source_target_pairs={{0,1},{1,2},{2,3},{3,4},{4,5},{5,6},{6,7},{7,8},{8,9},{9,10},{10,1... | collective-permute-start | bytes 36872 | tf_op jit(solution)/shard_map/ppermute | solution.py:274
  80.2 6.5 %collective-permute-start.1 = (f32[3,8,128]{2,1,0:T(8,128)S(1)}, f32[3,8,128]{2,1,0:T(8,128)S(1)}, u32[]{:S(2)}, u32[]{:S(2)}) collective-permute-start(f32[3,8,128]{2,1,0:T(8,128)S(1)} %get-tuple-element.14), channel_id=1, source_target_pairs={{1,0},{2,1},{3,2},{4,3},{5,4},{6,5},{7,6},{8,7},{9,8},{10,9},{11,1... | collective-permute-start | bytes 36872 | tf_op jit(solution)/shard_map/ppermute | solution.py:274
  86.9 12.2 %collective-permute-start.2 = (f32[3,8,1152]{2,1,0:T(8,128)S(1)}, f32[3,8,1152]{2,1,0:T(8,128)S(1)}, u32[]{:S(2)}, u32[]{:S(2)}) collective-permute-start(f32[3,8,1152]{2,1,0:T(8,128)S(1)} %get-tuple-element.16), channel_id=1, source_target_pairs={{0,16},{16,32},{32,48},{48,64},{64,80},{80,96},{96,112},{1,17},{17... | collective-permute-start | bytes 331784 | tf_op jit(solution)/shard_map/ppermute | solution.py:274
  97.1 6.1 %collective-permute-start.3 = (f32[3,8,1152]{2,1,0:T(8,128)S(1)}, f32[3,8,1152]{2,1,0:T(8,128)S(1)}, u32[]{:S(2)}, u32[]{:S(2)}) collective-permute-start(f32[3,8,1152]{2,1,0:T(8,128)S(1)} %get-tuple-element.17), channel_id=1, source_target_pairs={{16,0},{32,16},{48,32},{64,48},{80,64},{96,80},{112,96},{17,1},{33... | collective-permute-start | bytes 331784 | tf_op jit(solution)/shard_map/ppermute | solution.py:274
  103.2 1.0 copy-start.3
Sparse Core Ops, SparseCore 0:
  9.7 30.6 all-gather.3
where the time goes:
time: 120 us; the launch traced here: 119 us
  blocking collectives  52 us (43%)
  starting transfers between devices  24.4 us (20%)
  between operations  14.2 us (12%)
  Pallas kernels  12.5 us (10%)
  waiting for transfers between devices  9.09 us (8%)
  local copies, waits for them, and re-layouts  6.29 us (5%)
    all_gather x1, blocking collectives, body(): table = lax.all_gather(dest, 'gy', axis=0)  52 us
    ppermute x4, starting transfers between devices, moved(): return lax.ppermute(value, axis, pairs)  17.4 us
    ppermute x4, waiting for transfers between devices, moved(): return lax.ppermute(value, axis, pairs)  8.39 us
    pallas_call x1, Pallas kernels, sweeps(): pl.pallas_call(sweep_kernel, out_shape=jax.ShapeDtypeStruct((2, CELLS, WI...  7.67 us
    all_to_all x1, starting transfers between devices, body(): lax.all_to_all(outgoing, 'gy', split_axis=0, concat_axis=0, tiled=True)  6.97 us
    unnamed x16, local copies, waits for them, and re-layouts  6.22 us
    pallas_call x1, Pallas kernels, assemble(): pl.pallas_call(assemble_kernel, out_shape=(jax.ShapeDtypeStruct((CELLS, W...  3.07 us
  transfers between devices with their start and end apart: 6, of which 2 were waited for; matrix products, arithmetic and copies ran while one was open for 0% of the time, Pallas kernels for 1%

commit v1 on v0

v1 whole, which is shorter than its diff:
```python
import functools

import jax
import jax.numpy as jnp
from jax import lax
from jax.experimental import pallas as pl
from jax.experimental.pallas import tpu as pltpu
from jax.sharding import PartitionSpec as P

CELLS = 128
FIELDS = 3
SWEEPS = 6
SLOTS = 8
PEERS = 16
OWNERS = 8
HALO = 8
WIDTH = SLOTS * CELLS
PATCH_ROWS = FIELDS * CELLS
CHUNK_ROWS = PATCH_ROWS + HALO
EXT_ROWS = CELLS + 2 * HALO
TILES = EXT_ROWS // 8
BLOCKS = SLOTS + 1
EXT_COLS = BLOCKS * CELLS
OMEGA = 0.8
TIME_STEP = 0.5

MIB = 1024 * 1024
in_vmem = pl.BlockSpec(memory_space=pltpu.VMEM)
in_smem = pl.BlockSpec(memory_space=pltpu.SMEM)
in_any = pl.BlockSpec(memory_space=pl.ANY)


def params(mib):
    return pltpu.CompilerParams(vmem_limit_bytes=mib * MIB)


def stage_kernel(dest, old, out, patch_v, note_v, in_sems, out_sems, note_sem):
    for slot in range(SLOTS):
        pltpu.make_async_copy(old.at[slot], patch_v.at[slot], in_sems.at[slot]).start()
    note_v[...] = jnp.full(note_v.shape, -1.0, jnp.float32)
    for slot in range(SLOTS):
        target = dest[slot]

        @pl.when(target >= 0)
        def _(target=target):
            where = lax.convert_element_type(target & (SLOTS - 1), jnp.float32)
            note_v[target >> 3] = jnp.full((HALO, CELLS), where, jnp.float32)

    notes = pltpu.make_async_copy(note_v, out.at[:, pl.ds(PATCH_ROWS, HALO)], note_sem)
    notes.start()

    def send(slot):
        rows = out.at[dest[slot] >> 3, pl.ds(0, PATCH_ROWS)]
        return pltpu.make_async_copy(patch_v.at[slot], rows, out_sems.at[slot])

    for slot in range(SLOTS):
        pltpu.make_async_copy(old.at[slot], patch_v.at[slot], in_sems.at[slot]).wait()

        @pl.when(dest[slot] >= 0)
        def _(slot=slot):
            send(slot).start()

    for slot in range(SLOTS):

        @pl.when(dest[slot] >= 0)
        def _(slot=slot):
            send(slot).wait()

    notes.wait()


def stage(dest, old):
    return pl.pallas_call(
        stage_kernel,
        out_shape=jax.ShapeDtypeStruct((PEERS, CHUNK_ROWS, CELLS), jnp.float32),
        in_specs=[in_smem, in_any],
        out_specs=in_any,
        scratch_shapes=[
            pltpu.VMEM((SLOTS, PATCH_ROWS, CELLS), jnp.float32),
            pltpu.VMEM((PEERS, HALO, CELLS), jnp.float32),
            pltpu.SemaphoreType.DMA((SLOTS,)),
            pltpu.SemaphoreType.DMA((SLOTS,)),
            pltpu.SemaphoreType.DMA,
        ],
        compiler_params=params(60),
        name="stage_outgoing",
    )(dest, old)


def spread(quarter, fine_axis):
    fine = lax.broadcasted_iota(jnp.int32, (CELLS, CELLS), fine_axis)
    coarse = lax.broadcasted_iota(jnp.int32, (CELLS, CELLS), 1 - fine_axis)
    half = CELLS // 2
    middle = lax.shift_right_logical(fine, 1)
    beside = jnp.where((fine & 1) == 0, middle - 1, middle + 1)
    beside = jnp.clip(beside, 0, half - 1)
    base = quarter * half
    near = jnp.where(coarse == base + middle, 0.75, 0.0)
    far = jnp.where(coarse == base + beside, 0.25, 0.0)
    return (near + far).astype(jnp.bfloat16)


def split_two(value):
    high = value.astype(jnp.bfloat16)
    low = (value - high.astype(jnp.float32)).astype(jnp.bfloat16)
    return high, low


def dot(a, b):
    return jnp.dot(a, b, preferred_element_type=jnp.float32)


def assemble_kernel(refine, code, owner, arrived, force, *refs):
    pieces, refs = refs[:OWNERS], refs[OWNERS:]
    depth, state, left, right, rows, note_v, note_i, force_v, sems, note_sem, force_sem, depth_sem = refs
    notes = pltpu.make_async_copy(arrived.at[:, pl.ds(PATCH_ROWS, HALO)], note_v, note_sem)
    notes.start()

    def force_copy(slot):
        cols = pl.ds(slot * CELLS, CELLS)
        return pltpu.make_async_copy(force.at[:, :, cols], force_v.at[slot], force_sem.at[slot])

    for slot in range(SLOTS):
        force_copy(slot).start()

    def place(origin, slot):
        return pltpu.make_async_copy(origin, state.at[slot], sems.at[slot])

    for number, piece in enumerate(pieces):

        @pl.when(owner[0] == number)
        def _(piece=piece):
            for slot in range(SLOTS):

                @pl.when(refine[slot] > 0)
                def _(slot=slot):
                    place(piece.at[(code[slot] >> 2) & 1], slot).start()

    notes.wait()
    note_i[...] = note_v[:, 0, :].astype(jnp.int32)
    for peer in range(PEERS):
        slot = note_i[peer, 0]

        @pl.when(slot >= 0)
        def _(slot=slot, peer=peer):
            place(arrived.at[peer, pl.ds(0, PATCH_ROWS)], slot).start()

    def depth_copy(slot):
        cols = pl.ds(slot * CELLS, CELLS)
        source = state.at[slot, pl.ds(0, CELLS)]
        return pltpu.make_async_copy(source, depth.at[:, cols], depth_sem.at[slot])

    for slot in range(SLOTS):
        place(arrived.at[0, pl.ds(0, PATCH_ROWS)], slot).wait()

        @pl.when(refine[slot] > 0)
        def _(slot=slot):
            quadrant = code[slot] & 3
            along_rows = spread(quadrant >> 1, 0)
            along_cols = spread(quadrant & 1, 1)
            for field in range(FIELDS):
                at = slice(field * CELLS, (field + 1) * CELLS)
                high, low = split_two(state[slot, at])
                done = dot(along_rows, high) + dot(along_rows, low)
                high, low = split_two(done)
                state[slot, at] = dot(high, along_cols) + dot(low, along_cols)

        depth_copy(slot).start()
        force_copy(slot).wait()
        for field in range(2):
            at = slice((field + 1) * CELLS, (field + 2) * CELLS)
            state[slot, at] = state[slot, at] + TIME_STEP * force_v[slot, field]
        for field in range(FIELDS):
            low = field * CELLS
            rows[0, field, slot] = state[slot, low : low + HALO]
            rows[1, field, slot] = state[slot, low + CELLS - HALO : low + CELLS]

    for field in range(FIELDS):
        at = slice(field * CELLS, (field + 1) * CELLS)
        left[field] = state[0, at].T[:HALO]
        right[field] = state[SLOTS - 1, at].T[CELLS - HALO :]
    for slot in range(SLOTS):
        depth_copy(slot).wait()


def assemble(refine, code, owner, arrived, force, pieces):
    f32 = jnp.float32
    return pl.pallas_call(
        assemble_kernel,
        out_shape=(
            jax.ShapeDtypeStruct((CELLS, WIDTH), f32),
            jax.ShapeDtypeStruct((SLOTS, PATCH_ROWS, CELLS), f32),
            jax.ShapeDtypeStruct((FIELDS, HALO, CELLS), f32),
            jax.ShapeDtypeStruct((FIELDS, HALO, CELLS), f32),
            jax.ShapeDtypeStruct((2, FIELDS, SLOTS, HALO, CELLS), f32),
        ),
        in_specs=[in_smem] * 3 + [in_any] * (2 + OWNERS),
        out_specs=[in_any] + [in_vmem] * 4,
        scratch_shapes=[
            pltpu.VMEM((PEERS, HALO, CELLS), f32),
            pltpu.VMEM((PEERS, CELLS), jnp.int32),
            pltpu.VMEM((SLOTS, 2, CELLS, CELLS), f32),
            pltpu.SemaphoreType.DMA((SLOTS,)),
            pltpu.SemaphoreType.DMA,
            pltpu.SemaphoreType.DMA((SLOTS,)),
            pltpu.SemaphoreType.DMA((SLOTS,)),
        ],
        compiler_params=params(40),
        name="assemble_patches",
    )(refine, code, owner, arrived, force, *pieces)


def edge_kernel(rows, from_left, from_right, top, bottom, side):
    blank = jnp.zeros((CELLS - 2 * HALO, CELLS), jnp.float32)
    for field in range(FIELDS):
        tile = jnp.concatenate([from_right[field], blank, from_left[field]], axis=0).T
        side[field] = tile
        top[field, :SLOTS] = rows[0, field]
        top[field, SLOTS] = tile[:HALO]
        bottom[field, :SLOTS] = rows[1, field]
        bottom[field, SLOTS] = tile[CELLS - HALO :]


def edges(rows, from_left, from_right):
    f32 = jnp.float32
    return pl.pallas_call(
        edge_kernel,
        out_shape=(
            jax.ShapeDtypeStruct((FIELDS, BLOCKS, HALO, CELLS), f32),
            jax.ShapeDtypeStruct((FIELDS, BLOCKS, HALO, CELLS), f32),
            jax.ShapeDtypeStruct((FIELDS, CELLS, CELLS), f32),
        ),
        in_specs=[in_vmem] * 3,
        out_specs=[in_vmem] * 3,
        compiler_params=params(16),
        name="edge_rows",
    )(rows, from_left, from_right)


def sweep_kernel(state, side, above, below, out, wide, right, velo, faces, out_sems):
    for field in range(FIELDS):
        at = slice(field * CELLS, (field + 1) * CELLS)
        for block in range(BLOCKS):
            wide[field, block, :HALO] = above[field, block]
            wide[field, block, HALO + CELLS :] = below[field, block]
            wide[field, block, HALO : HALO + CELLS] = side[field] if block == SLOTS else state[block, at]

    def rows_of(t):
        return pl.ds(t, 8, stride=TILES)

    def spaced(field, t):
        return jnp.concatenate([wide[field, block, rows_of(t), :] for block in range(BLOCKS)], axis=1)

    def each_tile(load):
        first, last = load(0), load(TILES - 1)
        before, here = pltpu.roll(last, 1, 0), first
        for t in range(TILES):
            after = load(t + 1) if t < TILES - 1 else pltpu.roll(load(0), 7, 0)
            yield t, here, (before, after, pltpu.roll(here, 1, 1), pltpu.roll(here, EXT_COLS - 1, 1))
            before, here = here, after

    def weight(a, b):
        mean = (a + b) * 0.5
        return mean * mean * mean * (1.0 / 3.0)

    for t, here, others in each_tile(lambda t: spaced(0, t)):
        weights = [weight(here, other) for other in others]
        diagonal = here + weights[0] + weights[1] + weights[2] + weights[3]
        inside = here > 0.0
        scale = jnp.where(inside, OMEGA / jnp.where(inside, diagonal, 1.0), 0.0)
        for number, w in enumerate(weights):
            faces[number, t] = w * scale
        for field in range(2):
            start = spaced(field + 1, t) * scale
            right[field, t] = start
            velo[0, field, t] = start

    def relaxed(now, field, t, here, others):
        total = right[field, t] + (1.0 - OMEGA) * here
        for number, other in enumerate(others):
            total = total + faces[number, t] * other
        return total

    def step(s, _):
        now = s & 1
        for field in range(2):
            for t, here, others in each_tile(lambda t: velo[now, field, t]):
                velo[1 - now, field, t] = relaxed(now, field, t, here, others)
        return 0

    lax.fori_loop(0, SWEEPS - 2, step, 0)

    def out_copy(field, block):
        cols = pl.ds(block * CELLS, CELLS)
        source = wide.at[field, block, pl.ds(HALO, CELLS)]
        return pltpu.make_async_copy(source, out.at[field, :, cols], out_sems.at[field, block])

    now = (SWEEPS - 2) % 2
    for field in range(2):
        for t, here, others in each_tile(lambda t: velo[now, field, t]):
            done = relaxed(now, field, t, here, others)
            for block in range(SLOTS):
                wide[field, block, rows_of(t), :] = done[:, block * CELLS : (block + 1) * CELLS]
        for block in range(SLOTS):
            out_copy(field, block).start()
    for field in range(2):
        for block in range(SLOTS):
            out_copy(field, block).wait()


def sweeps(state, side, above, below):
    f32 = jnp.float32
    tiles = (TILES, 8, EXT_COLS)
    return pl.pallas_call(
        sweep_kernel,
        out_shape=jax.ShapeDtypeStruct((2, CELLS, WIDTH), f32),
        in_specs=[in_vmem] * 4,
        out_specs=in_any,
        scratch_shapes=[
            pltpu.VMEM((FIELDS, BLOCKS, EXT_ROWS, CELLS), f32),
            pltpu.VMEM((2,) + tiles, f32),
            pltpu.VMEM((2, 2) + tiles, f32),
            pltpu.VMEM((4,) + tiles, f32),
            pltpu.SemaphoreType.DMA((2, SLOTS)),
        ],
        compiler_params=params(40),
        name="jacobi_sweeps",
    )(state, side, above, below)


def moved(value, axis, step):
    count = lax.axis_size(axis)
    pairs = [(i, i + step) for i in range(count) if 0 <= i + step < count]
    return lax.ppermute(value, axis, pairs)


def around_ring(value, axis, step):
    count = lax.axis_size(axis)
    return lax.ppermute(value, axis, [(i, (i + step) % count) for i in range(count)])


def swapped(value, axis, bit):
    count = lax.axis_size(axis)
    return lax.ppermute(value, axis, [(i, i ^ bit) for i in range(count)])


def column_pieces(coarse):
    own = [
        coarse,
        around_ring(coarse, "gx", -2),
        around_ring(coarse, "gx", 4),
        around_ring(coarse, "gx", 2),
    ]
    return own + [swapped(piece, "gx", 1) for piece in own]


def body(old_state, old_dest, refine, parent_block, coarse_state, force):
    gx = lax.axis_index("gx")
    outgoing = stage(old_dest[0], old_state.reshape(SLOTS, PATCH_ROWS, CELLS))
    arrived = lax.all_to_all(outgoing, "gy", split_axis=0, concat_axis=0, tiled=True)
    pieces = column_pieces(coarse_state.reshape(2, PATCH_ROWS, CELLS))
    holder = parent_block[0, :1] >> 3
    owner = (((holder >> 1) - (gx >> 1)) & 3) + 4 * ((holder ^ gx) & 1)
    depth, state, left, right, rows = assemble(
        refine[0], parent_block[0], owner, arrived, force, pieces
    )
    from_left = moved(right, "gy", 1)
    from_right = moved(left, "gy", -1)
    top, bottom, side = edges(rows, from_left, from_right)
    above = moved(bottom, "gx", 1)
    below = moved(top, "gx", -1)
    velocity = sweeps(state, side, above, below)
    return depth, velocity


def solution(mesh):
    return jax.shard_map(
        body,
        mesh=mesh,
        in_specs=(
            P("gx", "gy", None, None, None),
            P("gx", "gy"),
            P("gx", "gy"),
            P("gx", "gy"),
            P("gx", "gy", None, None, None),
            P(None, "gx", "gy"),
        ),
        out_specs=(P("gx", "gy"), P(None, "gx", "gy")),
        check_vma=False,
    )
```

time: 120 us -> 93.2 us (0.78)
  blocking collectives: 52 us -> 0 us
  waiting for transfers between devices: 9.09 us -> 44.3 us
  between operations: 14.2 us -> 0.8 us
  starting transfers between devices: 24.4 us -> 31.1 us
  local copies, waits for them, and re-layouts: 6.29 us -> 2.23 us
  Pallas kernels: 12.5 us -> 14 us
    all_gather x1 -> x0, blocking collectives: 52 us -> none  [body(): table = lax.all_gather(dest, 'gy', axis=0)]
    all_to_all x1, waiting for transfers between devices: 0.01 us -> 18.4 us  [body(): lax.all_to_all(outgoing, 'gy', split_axis=0, concat_axis=0, tiled=True)]
    ppermute x0 -> x7, waiting for transfers between devices: none -> 17.2 us  [the longest x3 15.6 us: around_ring(): lax.ppermute(value, axis, [(i, (i + step) % count) for i in range(count)])]
    ppermute x0 -> x7, starting transfers between devices: none -> 9.71 us  [the longest x4 5.26 us: swapped(): return lax.ppermute(value, axis, [(i, i ^ bit) for i in range(count)])]
    unnamed x16 -> x8, local copies, waits for them, and re-layouts: 6.22 us -> 2.23 us
    ppermute x4, starting transfers between devices: 17.4 us -> 14.5 us  [moved(): return lax.ppermute(value, axis, pairs)]
    pallas_call x1, Pallas kernels: 3.07 us -> 4.94 us  [assemble(): pl.pallas_call(assemble_kernel, out_shape=(jax.ShapeDtypeStruct((CELLS, W...]
    pallas_call x1, Pallas kernels: 7.67 us -> 5.93 us  [sweeps(): pl.pallas_call(sweep_kernel, out_shape=jax.ShapeDtypeStruct((2, CELLS, WI...]
  transfers between devices with their start and end apart: 6 -> 12, of which waited for: 2 -> 6; matrix products, arithmetic and copies ran while one was open for 0% -> 0% of each run, Pallas kernels for 1% -> 0%
where the time goes in v1:
time: 93.2 us; the launch traced here: 92.5 us
  waiting for transfers between devices  44.3 us (48%)
  starting transfers between devices  31.1 us (33%)
  Pallas kernels  14 us (15%)
  local copies, waits for them, and re-layouts  2.23 us (2%)
    all_to_all x1, waiting for transfers between devices, body(): lax.all_to_all(outgoing, 'gy', split_axis=0, concat_axis=0, tiled=True)  18.4 us
    ppermute x3, waiting for transfers between devices, around_ring(): lax.ppermute(value, axis, [(i, (i + step) % count) for i in range(count)])  15.6 us
    ppermute x4, starting transfers between devices, moved(): return lax.ppermute(value, axis, pairs)  14.5 us
    ppermute x4, waiting for transfers between devices, moved(): return lax.ppermute(value, axis, pairs)  8.74 us
    all_to_all x1, starting transfers between devices, body(): lax.all_to_all(outgoing, 'gy', split_axis=0, concat_axis=0, tiled=True)  6.85 us
    pallas_call x1, Pallas kernels, sweeps(): pl.pallas_call(sweep_kernel, out_shape=jax.ShapeDtypeStruct((2, CELLS, WI...  5.93 us
    ppermute x4, starting transfers between devices, swapped(): return lax.ppermute(value, axis, [(i, i ^ bit) for i in range(count)])  5.26 us
    pallas_call x1, Pallas kernels, assemble(): pl.pallas_call(assemble_kernel, out_shape=(jax.ShapeDtypeStruct((CELLS, W...  4.94 us
  transfers between devices with their start and end apart: 12, of which 6 were waited for; matrix products, arithmetic and copies ran while one was open for 0% of the time, Pallas kernels for 0%

profile of v1, /device:TPU:7, one launch (start us, length us, event | category | flops | bytes accessed | tf_op | source)
XLA Modules:
  0.0 92.5 jit_solution(10540554397431763323)
XLA Ops:
  0.6 3.0 %stage_outgoing.1 = f32[16,392,128]{2,1,0:T(8,128)} custom-call(s32[8]{0:T(128)} %bitcast.18, f32[8,384,128]{2,1,0:T(8,128)} %bitcast.17), custom_call_target="tpu_custom_call" | custom-call | tf_op jit(solution)/shard_map/stage_outgoing/pallas_call | solution.py:73
  3.7 0.0 copy-start.3
  3.7 0.0 copy-start.2
  3.7 6.9 %all-to-all-start = ((f32[16,392,128]{2,1,0:T(8,128)}), f32[16,392,128]{2,1,0:T(8,128)S(1)}, u32[]{:S(2)}, u32[]{:S(2)}) async-start(f32[16,392,128]{2,1,0:T(8,128)} %stage_outgoing.1), calls=%async_computation | async-start | bytes 6422528 | tf_op jit(solution)/shard_map/all_to_all | solution.py:360
  10.5 3.8 %collective-permute-start = (f32[2,384,128]{2,1,0:T(8,128)}, f32[2,384,128]{2,1,0:T(8,128)}, u32[]{:S(2)}, u32[]{:S(2)}) collective-permute-start(f32[2,384,128]{2,1,0:T(8,128)} %bitcast.9), channel_id=1, source_target_pairs={{0,96},{16,112},{32,0},{48,16},{64,32},{80,48},{96,64},{112,80},{1... | collective-permute-start | bytes 1179656 | tf_op jit(solution)/shard_map/ppermute | solution.py:339
  14.3 0.7 collective-permute-start.2
  15.0 2.1 %collective-permute-start.3 = (f32[2,384,128]{2,1,0:T(8,128)}, f32[2,384,128]{2,1,0:T(8,128)}, u32[]{:S(2)}, u32[]{:S(2)}) collective-permute-start(f32[2,384,128]{2,1,0:T(8,128)} %bitcast.12), channel_id=1, source_target_pairs={{0,16},{16,0},{32,48},{48,32},{64,80},{80,64},{96,112},{112,96},{1... | collective-permute-start | bytes 1179656 | tf_op jit(solution)/shard_map/ppermute | solution.py:344
  17.1 13.0 %collective-permute-done.refs_1_ = f32[2,384,128]{2,1,0:T(8,128)} collective-permute-done((f32[2,384,128]{2,1,0:T(8,128)}, f32[2,384,128]{2,1,0:T(8,128)}, u32[]{:S(2)}, u32[]{:S(2)}) %collective-permute-start) | collective-permute-done | bytes 393248 | tf_op jit(solution)/shard_map/ppermute | solution.py:339
  30.1 2.3 %collective-permute-start.4 = (f32[2,384,128]{2,1,0:T(8,128)}, f32[2,384,128]{2,1,0:T(8,128)}, u32[]{:S(2)}, u32[]{:S(2)}) collective-permute-start(f32[2,384,128]{2,1,0:T(8,128)} %collective-permute-done.refs_1_), channel_id=1, source_target_pairs={{0,16},{16,0},{32,48},{48,32},{64,80},{80,64},{96,112},{112,96},{1... | collective-permute-start | bytes 1179656 | tf_op jit(solution)/shard_map/ppermute | solution.py:344
  32.4 2.6 %collective-permute-done.2.refs_3_ = f32[2,384,128]{2,1,0:T(8,128)} collective-permute-done((f32[2,384,128]{2,1,0:T(8,128)}, f32[2,384,128]{2,1,0:T(8,128)}, u32[]{:S(2)}, u32[]{:S(2)}) %collective-permute-start.2) | collective-permute-done | bytes 393248 | tf_op jit(solution)/shard_map/ppermute | solution.py:339
  35.0 0.8 collective-permute-start.6
  35.9 1.6 %collective-permute-done.6.refs_7_ = f32[2,384,128]{2,1,0:T(8,128)} collective-permute-done((f32[2,384,128]{2,1,0:T(8,128)}, f32[2,384,128]{2,1,0:T(8,128)}, u32[]{:S(2)}, u32[]{:S(2)}) %collective-permute-start.6) | collective-permute-done | bytes 393248 | tf_op jit(solution)/shard_map/ppermute | solution.py:344
  37.5 18.4 %all-to-all-done.arrived = f32[16,392,128]{2,1,0:T(8,128)S(1)} async-done(((f32[16,392,128]{2,1,0:T(8,128)}), f32[16,392,128]{2,1,0:T(8,128)S(1)}, u32[]{:S(2)}, u32[]{:S(2)}) %all-to-all-start) | async-done | bytes 3211296 | tf_op jit(solution)/shard_map/all_to_all | solution.py:360
  55.9 1.2 %copy-done = f32[2,128,1024]{2,1,0:T(8,128)S(1)} copy-done((f32[2,128,1024]{2,1,0:T(8,128)S(1)}, f32[2,128,1024]{2,1,0:T(8,128)}, u32[]{:S(2)}) %copy-start) | copy-done | bytes 1048600
  57.2 1.0 %copy-done.1 = f32[2,1,3,128,128]{4,3,2,1,0:T(8,128)S(1)} copy-done((f32[2,1,3,128,128]{4,3,2,1,0:T(8,128)S(1)}, f32[2,1,3,128,128]{4,3,2,1,0:T(8,128)}, u32[]{:S(2)}) %copy-start.1) | copy-done | bytes 393240
  58.1 4.9 %assemble_patches.1 = (f32[128,1024]{1,0:T(8,128)}, f32[8,384,128]{2,1,0:T(8,128)S(1)}, f32[3,8,128]{2,1,0:T(8,128)S(1)}, f32[3,8,128]{2,1,0:T(8,128)S(1)}, f32[2,3,8,8,128]{4,3,2,1,0:T(8,128)S(1)}) custom-call(s32[8]{0:T(128)S(1)} %bitcast.14, s32[8]{0:T(128)S(1)} %bitcast.16, s32[1]{0:T(128)S(6)} %add.3.owner, f32[16,392,128]{2,1,0:T(8,128)S(1)} %all-to-all-done.arrived, ...), custom_call_target="tpu_custom_call" | custom-call | tf_op jit(solution)/shard_map/assemble_patches/pallas_call | solution.py:188
  63.1 4.6 %collective-permute-start.7 = (f32[3,8,128]{2,1,0:T(8,128)S(1)}, f32[3,8,128]{2,1,0:T(8,128)S(1)}, u32[]{:S(2)}, u32[]{:S(2)}) collective-permute-start(f32[3,8,128]{2,1,0:T(8,128)S(1)} %get-tuple-element.13), channel_id=1, source_target_pairs={{0,1},{1,2},{2,3},{3,4},{4,5},{5,6},{6,7},{7,8},{8,9},{9,10},{10,1... | collective-permute-start | bytes 36872 | tf_op jit(solution)/shard_map/ppermute | solution.py:334
  67.7 1.9 %collective-permute-start.8 = (f32[3,8,128]{2,1,0:T(8,128)S(1)}, f32[3,8,128]{2,1,0:T(8,128)S(1)}, u32[]{:S(2)}, u32[]{:S(2)}) collective-permute-start(f32[3,8,128]{2,1,0:T(8,128)S(1)} %get-tuple-element.14), channel_id=1, source_target_pairs={{1,0},{2,1},{3,2},{4,3},{5,4},{6,5},{7,6},{8,7},{9,8},{10,9},{11,1... | collective-permute-start | bytes 36872 | tf_op jit(solution)/shard_map/ppermute | solution.py:334
  69.6 4.6 %collective-permute-done.8.from_right = f32[3,8,128]{2,1,0:T(8,128)S(1)} collective-permute-done((f32[3,8,128]{2,1,0:T(8,128)S(1)}, f32[3,8,128]{2,1,0:T(8,128)S(1)}, u32[]{:S(2)}, u32[]{:S(2)}) %collective-permute-start.8) | collective-permute-done | bytes 12320 | tf_op jit(solution)/shard_map/ppermute | solution.py:334
  74.2 0.1 edge_rows.1
  74.3 6.1 %collective-permute-start.9 = (f32[3,9,8,128]{3,2,1,0:T(8,128)S(1)}, f32[3,9,8,128]{3,2,1,0:T(8,128)S(1)}, u32[]{:S(2)}, u32[]{:S(2)}) collective-permute-start(f32[3,9,8,128]{3,2,1,0:T(8,128)S(1)} %get-tuple-element.16), channel_id=1, source_target_pairs={{0,16},{16,32},{32,48},{48,64},{64,80},{80,96},{96,112},{1,17},{17... | collective-permute-start | bytes 331784 | tf_op jit(solution)/shard_map/ppermute | solution.py:334
  80.5 1.9 %collective-permute-start.10 = (f32[3,9,8,128]{3,2,1,0:T(8,128)S(1)}, f32[3,9,8,128]{3,2,1,0:T(8,128)S(1)}, u32[]{:S(2)}, u32[]{:S(2)}) collective-permute-start(f32[3,9,8,128]{3,2,1,0:T(8,128)S(1)} %get-tuple-element.17), channel_id=1, source_target_pairs={{16,0},{32,16},{48,32},{64,48},{80,64},{96,80},{112,96},{17,1},{33... | collective-permute-start | bytes 331784 | tf_op jit(solution)/shard_map/ppermute | solution.py:334
  82.4 4.1 %collective-permute-done.10.below = f32[3,9,8,128]{3,2,1,0:T(8,128)S(1)} collective-permute-done((f32[3,9,8,128]{3,2,1,0:T(8,128)S(1)}, f32[3,9,8,128]{3,2,1,0:T(8,128)S(1)}, u32[]{:S(2)}, u32[]{:S(2)}) %collective-permute-start.10) | collective-permute-done | bytes 110624 | tf_op jit(solution)/shard_map/ppermute | solution.py:334
  86.5 5.9 %jacobi_sweeps.1 = f32[2,128,1024]{2,1,0:T(8,128)} custom-call(f32[8,384,128]{2,1,0:T(8,128)S(1)} %get-tuple-element.11.state, f32[3,128,128]{2,1,0:T(8,128)S(1)} %get-tuple-element.15.side, f32[3,9,8,128]{3,2,1,0:T(8,128)S(1)} %collective-permute-done.9.above, f32[3,9,8,128]{3,2,1,0:T(8,128)S(1)} %collective-permute-done.10.below), custom_call_target="tpu_custom_call" | custom-call | tf_op jit(solution)/shard_map/jacobi_sweeps/pallas_call | solution.py:314
  (12 shorter events, 0.0 us)
Async XLA Ops:
  3.7 32.1 %copy-start.3 = (s32[1,8]{1,0:T(1,128)S(1)}, s32[1,8]{1,0:T(1,128)}, u32[]{:S(2)}) copy-start(s32[1,8]{1,0:T(1,128)} %param.9) | copy-start | bytes 100
  3.7 52.3 %copy-start.2 = (s32[1,8]{1,0:T(1,128)S(1)}, s32[1,8]{1,0:T(1,128)}, u32[]{:S(2)}) copy-start(s32[1,8]{1,0:T(1,128)} %param.8) | copy-start | bytes 100
  3.7 52.2 %all-to-all-start = ((f32[16,392,128]{2,1,0:T(8,128)}), f32[16,392,128]{2,1,0:T(8,128)S(1)}, u32[]{:S(2)}, u32[]{:S(2)}) async-start(f32[16,392,128]{2,1,0:T(8,128)} %stage_outgoing.1), calls=%async_computation | async-start | bytes 6422528 | tf_op jit(solution)/shard_map/all_to_all | solution.py:360
  10.5 19.6 %collective-permute-start = (f32[2,384,128]{2,1,0:T(8,128)}, f32[2,384,128]{2,1,0:T(8,128)}, u32[]{:S(2)}, u32[]{:S(2)}) collective-permute-start(f32[2,384,128]{2,1,0:T(8,128)} %bitcast.9), channel_id=1, source_target_pairs={{0,96},{16,112},{32,0},{48,16},{64,32},{80,48},{96,64},{112,80},{1... | collective-permute-start | bytes 1179656 | tf_op jit(solution)/shard_map/ppermute | solution.py:339
  14.3 18.1 %collective-permute-start.1 = (f32[2,384,128]{2,1,0:T(8,128)}, f32[2,384,128]{2,1,0:T(8,128)}, u32[]{:S(2)}, u32[]{:S(2)}) collective-permute-start(f32[2,384,128]{2,1,0:T(8,128)} %bitcast.10), channel_id=1, source_target_pairs={{0,64},{16,80},{32,96},{48,112},{64,0},{80,16},{96,32},{112,48},{1... | collective-permute-start | bytes 1179656 | tf_op jit(solution)/shard_map/ppermute | solution.py:339
  14.3 20.6 %collective-permute-start.2 = (f32[2,384,128]{2,1,0:T(8,128)}, f32[2,384,128]{2,1,0:T(8,128)}, u32[]{:S(2)}, u32[]{:S(2)}) collective-permute-start(f32[2,384,128]{2,1,0:T(8,128)} %bitcast.11), channel_id=1, source_target_pairs={{0,32},{16,48},{32,64},{48,80},{64,96},{80,112},{96,0},{112,16},{1... | collective-permute-start | bytes 1179656 | tf_op jit(solution)/shard_map/ppermute | solution.py:339
  15.0 20.9 %collective-permute-start.3 = (f32[2,384,128]{2,1,0:T(8,128)}, f32[2,384,128]{2,1,0:T(8,128)}, u32[]{:S(2)}, u32[]{:S(2)}) collective-permute-start(f32[2,384,128]{2,1,0:T(8,128)} %bitcast.12), channel_id=1, source_target_pairs={{0,16},{16,0},{32,48},{48,32},{64,80},{80,64},{96,112},{112,96},{1... | collective-permute-start | bytes 1179656 | tf_op jit(solution)/shard_map/ppermute | solution.py:344
  30.1 5.8 %collective-permute-start.4 = (f32[2,384,128]{2,1,0:T(8,128)}, f32[2,384,128]{2,1,0:T(8,128)}, u32[]{:S(2)}, u32[]{:S(2)}) collective-permute-start(f32[2,384,128]{2,1,0:T(8,128)} %collective-permute-done.refs_1_), channel_id=1, source_target_pairs={{0,16},{16,0},{32,48},{48,32},{64,80},{80,64},{96,112},{112,96},{1... | collective-permute-start | bytes 1179656 | tf_op jit(solution)/shard_map/ppermute | solution.py:344
  32.4 3.5 %collective-permute-start.5 = (f32[2,384,128]{2,1,0:T(8,128)}, f32[2,384,128]{2,1,0:T(8,128)}, u32[]{:S(2)}, u32[]{:S(2)}) collective-permute-start(f32[2,384,128]{2,1,0:T(8,128)} %collective-permute-done.1.refs_2_), channel_id=1, source_target_pairs={{0,16},{16,0},{32,48},{48,32},{64,80},{80,64},{96,112},{112,96},{1... | collective-permute-start | bytes 1179656 | tf_op jit(solution)/shard_map/ppermute | solution.py:344
  35.0 2.5 %collective-permute-start.6 = (f32[2,384,128]{2,1,0:T(8,128)}, f32[2,384,128]{2,1,0:T(8,128)}, u32[]{:S(2)}, u32[]{:S(2)}) collective-permute-start(f32[2,384,128]{2,1,0:T(8,128)} %collective-permute-done.2.refs_3_), channel_id=1, source_target_pairs={{0,16},{16,0},{32,48},{48,32},{64,80},{80,64},{96,112},{112,96},{1... | collective-permute-start | bytes 1179656 | tf_op jit(solution)/shard_map/ppermute | solution.py:344
  55.9 1.2 %copy-start = (f32[2,128,1024]{2,1,0:T(8,128)S(1)}, f32[2,128,1024]{2,1,0:T(8,128)}, u32[]{:S(2)}) copy-start(f32[2,128,1024]{2,1,0:T(8,128)} %force.1) | copy-start | bytes 3145732
  57.2 1.0 %copy-start.1 = (f32[2,1,3,128,128]{4,3,2,1,0:T(8,128)S(1)}, f32[2,1,3,128,128]{4,3,2,1,0:T(8,128)}, u32[]{:S(2)}) copy-start(f32[2,1,3,128,128]{4,3,2,1,0:T(8,128)} %param.10) | copy-start | bytes 1179652
  63.1 6.5 %collective-permute-start.7 = (f32[3,8,128]{2,1,0:T(8,128)S(1)}, f32[3,8,128]{2,1,0:T(8,128)S(1)}, u32[]{:S(2)}, u32[]{:S(2)}) collective-permute-start(f32[3,8,128]{2,1,0:T(8,128)S(1)} %get-tuple-element.13), channel_id=1, source_target_pairs={{0,1},{1,2},{2,3},{3,4},{4,5},{5,6},{6,7},{7,8},{8,9},{9,10},{10,1... | collective-permute-start | bytes 36872 | tf_op jit(solution)/shard_map/ppermute | solution.py:334
  67.7 6.5 %collective-permute-start.8 = (f32[3,8,128]{2,1,0:T(8,128)S(1)}, f32[3,8,128]{2,1,0:T(8,128)S(1)}, u32[]{:S(2)}, u32[]{:S(2)}) collective-permute-start(f32[3,8,128]{2,1,0:T(8,128)S(1)} %get-tuple-element.14), channel_id=1, source_target_pairs={{1,0},{2,1},{3,2},{4,3},{5,4},{6,5},{7,6},{8,7},{9,8},{10,9},{11,1... | collective-permute-start | bytes 36872 | tf_op jit(solution)/shard_map/ppermute | solution.py:334
  74.3 8.1 %collective-permute-start.9 = (f32[3,9,8,128]{3,2,1,0:T(8,128)S(1)}, f32[3,9,8,128]{3,2,1,0:T(8,128)S(1)}, u32[]{:S(2)}, u32[]{:S(2)}) collective-permute-start(f32[3,9,8,128]{3,2,1,0:T(8,128)S(1)} %get-tuple-element.16), channel_id=1, source_target_pairs={{0,16},{16,32},{32,48},{48,64},{64,80},{80,96},{96,112},{1,17},{17... | collective-permute-start | bytes 331784 | tf_op jit(solution)/shard_map/ppermute | solution.py:334
  80.5 6.1 %collective-permute-start.10 = (f32[3,9,8,128]{3,2,1,0:T(8,128)S(1)}, f32[3,9,8,128]{3,2,1,0:T(8,128)S(1)}, u32[]{:S(2)}, u32[]{:S(2)}) collective-permute-start(f32[3,9,8,128]{3,2,1,0:T(8,128)S(1)} %get-tuple-element.17), channel_id=1, source_target_pairs={{16,0},{32,16},{48,32},{64,48},{80,64},{96,80},{112,96},{17,1},{33... | collective-permute-start | bytes 331784 | tf_op jit(solution)/shard_map/ppermute | solution.py:334

commit v2 on v1

--- a/solution.py
+++ b/solution.py
@@ -13,6 +13,7 @@
 SLOTS = 8
 PEERS = 16
 OWNERS = 8
+REFINED = 2
 HALO = 8
 WIDTH = SLOTS * CELLS
 PATCH_ROWS = FIELDS * CELLS
@@ -27,6 +28,7 @@
 MIB = 1024 * 1024
 in_vmem = pl.BlockSpec(memory_space=pltpu.VMEM)
 in_smem = pl.BlockSpec(memory_space=pltpu.SMEM)
+in_hbm = pl.BlockSpec(memory_space=pltpu.HBM)
 in_any = pl.BlockSpec(memory_space=pl.ANY)
 
 
@@ -73,7 +75,7 @@
     return pl.pallas_call(
         stage_kernel,
         out_shape=jax.ShapeDtypeStruct((PEERS, CHUNK_ROWS, CELLS), jnp.float32),
-        in_specs=[in_smem, in_any],
+        in_specs=[in_smem, in_hbm],
         out_specs=in_any,
         scratch_shapes=[
             pltpu.VMEM((SLOTS, PATCH_ROWS, CELLS), jnp.float32),
@@ -87,6 +89,52 @@
     )(dest, old)
 
 
+KEPT = 4
+COLS_AT = 2 * PATCH_ROWS
+ROWS_AT = COLS_AT + 4 * CELLS
+
+
+def keep_kernel(force, coarse, out, kept_v, sems, out_sem):
+    copies = [(coarse.at[0], 0, PATCH_ROWS), (coarse.at[1], PATCH_ROWS, PATCH_ROWS)]
+    for field in range(2):
+        for edge in range(2):
+            number = field * 2 + edge
+            cols = pl.ds(edge * (WIDTH - CELLS), CELLS)
+            copies.append((force.at[field, :, cols], COLS_AT + number * CELLS, CELLS))
+            for slot in range(SLOTS):
+                part = force.at[field, pl.ds(edge * (CELLS - HALO), HALO), pl.ds(slot * CELLS, CELLS)]
+                copies.append((part, ROWS_AT + (number * SLOTS + slot) * HALO, HALO))
+    copies = [
+        pltpu.make_async_copy(part, kept_v.at[pl.ds(first, size)], sems.at[number])
+        for number, (part, first, size) in enumerate(copies)
+    ]
+    for copy in copies:
+        copy.start()
+    for copy in copies:
+        copy.wait()
+    last = pltpu.make_async_copy(kept_v, out, out_sem)
+    last.start()
+    last.wait()
+
+
+def keep(force, coarse):
+    shape = (KEPT * PATCH_ROWS, CELLS)
+    return pl.pallas_call(
+        keep_kernel,
+        out_shape=jax.ShapeDtypeStruct(shape, jnp.float32),
+        in_specs=[in_any] * 2,
+        out_specs=in_any,
+        scratch_shapes=[
+            pltpu.VMEM(shape, jnp.float32),
+            pltpu.SemaphoreType.DMA((6 + 4 * SLOTS,)),
+            pltpu.SemaphoreType.DMA,
+        ],
+        compiler_params=params(24),
+        cost_estimate=pl.CostEstimate(flops=1 << 18, bytes_accessed=3 << 20, transcendentals=0),
+        name="keep_own",
+    )(force, coarse)
+
+
 def spread(quarter, fine_axis):
     fine = lax.broadcasted_iota(jnp.int32, (CELLS, CELLS), fine_axis)
     coarse = lax.broadcasted_iota(jnp.int32, (CELLS, CELLS), 1 - fine_axis)
@@ -110,115 +158,188 @@
     return jnp.dot(a, b, preferred_element_type=jnp.float32)
 
 
-def assemble_kernel(refine, code, owner, arrived, force, *refs):
+def outline_kernel(refine, code, owner, arrived, *refs):
     pieces, refs = refs[:OWNERS], refs[OWNERS:]
-    depth, state, left, right, rows, note_v, note_i, force_v, sems, note_sem, force_sem, depth_sem = refs
-    notes = pltpu.make_async_copy(arrived.at[:, pl.ds(PATCH_ROWS, HALO)], note_v, note_sem)
-    notes.start()
-
-    def force_copy(slot):
-        cols = pl.ds(slot * CELLS, CELLS)
-        return pltpu.make_async_copy(force.at[:, :, cols], force_v.at[slot], force_sem.at[slot])
-
+    source, fresh, left, right, rows, parent_v, note_i, force_v, picks, sems, force_sem = refs
+    force_copy = pltpu.make_async_copy(pieces[0].at[pl.ds(2, 2)], force_v, force_sem)
+    force_copy.start()
+
+    picks[0] = -1
+    picks[1] = -1
+    count = jnp.int32(0)
     for slot in range(SLOTS):
-        force_copy(slot).start()
-
-    def place(origin, slot):
-        return pltpu.make_async_copy(origin, state.at[slot], sems.at[slot])
-
-    for number, piece in enumerate(pieces):
-
-        @pl.when(owner[0] == number)
+        here = refine[slot] > 0
+        source[slot] = jnp.where(here, PEERS + count, 0)
+
+        @pl.when(here)
+        def _(slot=slot, count=count):
+            picks[jnp.minimum(count, REFINED - 1)] = slot
+
+        count = count + here.astype(jnp.int32)
+
+    def quarter(piece, number, field):
+        slot = picks[number]
+        first = pl.multiple_of(field * CELLS + ((code[slot] >> 1) & 1) * (CELLS // 2), CELLS // 2)
+        return pltpu.make_async_copy(
+            piece.at[(code[slot] >> 2) & 1, pl.ds(first, CELLS // 2)],
+            parent_v.at[number, field],
+            sems.at[number],
+        )
+
+    for place, piece in enumerate(pieces):
+
+        @pl.when(owner[0] == place)
         def _(piece=piece):
-            for slot in range(SLOTS):
-
-                @pl.when(refine[slot] > 0)
-                def _(slot=slot):
-                    place(piece.at[(code[slot] >> 2) & 1], slot).start()
-
-    notes.wait()
-    note_i[...] = note_v[:, 0, :].astype(jnp.int32)
+            for number in range(REFINED):
+
+                @pl.when(picks[number] >= 0)
+                def _(number=number):
+                    for field in range(FIELDS):
+                        quarter(piece, number, field).start()
+
+    note_i[...] = arrived[:, PATCH_ROWS, :].astype(jnp.int32)
     for peer in range(PEERS):
         slot = note_i[peer, 0]
 
         @pl.when(slot >= 0)
         def _(slot=slot, peer=peer):
-            place(arrived.at[peer, pl.ds(0, PATCH_ROWS)], slot).start()
-
-    def depth_copy(slot):
-        cols = pl.ds(slot * CELLS, CELLS)
-        source = state.at[slot, pl.ds(0, CELLS)]
-        return pltpu.make_async_copy(source, depth.at[:, cols], depth_sem.at[slot])
-
-    for slot in range(SLOTS):
-        place(arrived.at[0, pl.ds(0, PATCH_ROWS)], slot).wait()
-
-        @pl.when(refine[slot] > 0)
-        def _(slot=slot):
-            quadrant = code[slot] & 3
-            along_rows = spread(quadrant >> 1, 0)
-            along_cols = spread(quadrant & 1, 1)
+            source[slot] = peer
+
+    def refined(number, _):
+        @pl.when(picks[number] >= 0)
+        def _():
             for field in range(FIELDS):
-                at = slice(field * CELLS, (field + 1) * CELLS)
-                high, low = split_two(state[slot, at])
+                quarter(pieces[0], number, field).wait()
+            along_rows = spread(0, 0)[:, : CELLS // 2]
+            along_cols = spread(code[picks[number]] & 1, 1)
+            for field in range(FIELDS):
+                high, low = split_two(parent_v[number, field])
                 done = dot(along_rows, high) + dot(along_rows, low)
                 high, low = split_two(done)
-                state[slot, at] = dot(high, along_cols) + dot(low, along_cols)
-
-        depth_copy(slot).start()
-        force_copy(slot).wait()
-        for field in range(2):
-            at = slice((field + 1) * CELLS, (field + 2) * CELLS)
-            state[slot, at] = state[slot, at] + TIME_STEP * force_v[slot, field]
-        for field in range(FIELDS):
-            low = field * CELLS
-            rows[0, field, slot] = state[slot, low : low + HALO]
-            rows[1, field, slot] = state[slot, low + CELLS - HALO : low + CELLS]
-
+                at = slice(field * CELLS, (field + 1) * CELLS)
+                fresh[number, at] = dot(high, along_cols) + dot(low, along_cols)
+
+        return 0
+
+    lax.fori_loop(0, REFINED, refined, 0)
+
+    def taken(slot, first, size):
+        origin = source[slot]
+        kept = arrived[jnp.minimum(origin, PEERS - 1), first : first + size]
+        new = fresh[jnp.clip(origin - PEERS, 0, REFINED - 1), first : first + size]
+        return jnp.where(origin >= PEERS, new, kept)
+
+    def forcing(first, size):
+        part, first = divmod(first - COLS_AT, PATCH_ROWS)
+        return TIME_STEP * force_v[part, first : first + size]
+
+    force_copy.wait()
     for field in range(FIELDS):
-        at = slice(field * CELLS, (field + 1) * CELLS)
-        left[field] = state[0, at].T[:HALO]
-        right[field] = state[SLOTS - 1, at].T[CELLS - HALO :]
-    for slot in range(SLOTS):
-        depth_copy(slot).wait()
-
-
-def assemble(refine, code, owner, arrived, force, pieces):
+        low = field * CELLS
+        first = taken(0, low, CELLS)
+        last = taken(SLOTS - 1, low, CELLS)
+        if field > 0:
+            first = first + forcing(COLS_AT + (2 * field - 2) * CELLS, CELLS)
+            last = last + forcing(COLS_AT + (2 * field - 1) * CELLS, CELLS)
+        left[field] = first.T[:HALO]
+        right[field] = last.T[CELLS - HALO :]
+        for slot in range(SLOTS):
+            for edge, first in enumerate((low, low + CELLS - HALO)):
+                value = taken(slot, first, HALO)
+                if field > 0:
+                    number = 2 * field - 2 + edge
+                    value = value + forcing(ROWS_AT + (number * SLOTS + slot) * HALO, HALO)
+                rows[edge, field, slot] = value
+
+
+def outline(refine, code, owner, arrived, pieces):
     f32 = jnp.float32
     return pl.pallas_call(
-        assemble_kernel,
+        outline_kernel,
         out_shape=(
-            jax.ShapeDtypeStruct((CELLS, WIDTH), f32),
-            jax.ShapeDtypeStruct((SLOTS, PATCH_ROWS, CELLS), f32),
+            jax.ShapeDtypeStruct((SLOTS,), jnp.int32),
+            jax.ShapeDtypeStruct((REFINED, PATCH_ROWS, CELLS), f32),
             jax.ShapeDtypeStruct((FIELDS, HALO, CELLS), f32),
             jax.ShapeDtypeStruct((FIELDS, HALO, CELLS), f32),
             jax.ShapeDtypeStruct((2, FIELDS, SLOTS, HALO, CELLS), f32),
         ),
-        in_specs=[in_smem] * 3 + [in_any] * (2 + OWNERS),
-        out_specs=[in_any] + [in_vmem] * 4,
+        in_specs=[in_smem] * 3 + [in_vmem] + [in_any] * OWNERS,
+        out_specs=[in_smem] + [in_vmem] * 4,
         scratch_shapes=[
-            pltpu.VMEM((PEERS, HALO, CELLS), f32),
+            pltpu.VMEM((REFINED, FIELDS, CELLS // 2, CELLS), f32),
             pltpu.VMEM((PEERS, CELLS), jnp.int32),
-            pltpu.VMEM((SLOTS, 2, CELLS, CELLS), f32),
-            pltpu.SemaphoreType.DMA((SLOTS,)),
+            pltpu.VMEM((2, PATCH_ROWS, CELLS), f32),
+            pltpu.SMEM((REFINED,), jnp.int32),
+            pltpu.SemaphoreType.DMA((REFINED,)),
             pltpu.SemaphoreType.DMA,
-            pltpu.SemaphoreType.DMA((SLOTS,)),
+        ],
+        compiler_params=params(40),
+        name="block_outline",
+    )(refine, code, owner, arrived, *pieces)
+
+
+def interior_kernel(source, arrived, fresh, force, depth, wide, force_v, force_sems, depth_sems):
+    force_copies = [pltpu.make_async_copy(force.at[i], force_v.at[i], force_sems.at[i]) for i in range(2)]
+    for copy in force_copies:
+        copy.start()
+
+    def depth_copy(slot):
+        inner = wide.at[0, slot, pl.ds(HALO, CELLS)]
+        cols = pl.ds(slot * CELLS, CELLS)
+        return pltpu.make_async_copy(inner, depth.at[:, cols], depth_sems.at[slot])
+
+    for field in range(FIELDS):
+        if field > 0:
+            force_copies[field - 1].wait()
+        for slot in range(SLOTS):
+            origin = source[slot]
+            at = slice(field * CELLS, (field + 1) * CELLS)
+            kept = arrived[jnp.minimum(origin, PEERS - 1), at]
+            new = fresh[jnp.clip(origin - PEERS, 0, REFINED - 1), at]
+            value = jnp.where(origin >= PEERS, new, kept)
+            if field > 0:
+                value = value + TIME_STEP * force_v[field - 1, :, slot * CELLS : (slot + 1) * CELLS]
+            wide[field, slot, HALO : HALO + CELLS] = value
+            if field == 0:
+                depth_copy(slot).start()
+    for slot in range(SLOTS):
+        depth_copy(slot).wait()
+
+
+def interior(source, arrived, fresh, force):
+    f32 = jnp.float32
+    return pl.pallas_call(
+        interior_kernel,
+        out_shape=(
+            jax.ShapeDtypeStruct((CELLS, WIDTH), f32),
+            jax.ShapeDtypeStruct((FIELDS, SLOTS, EXT_ROWS, CELLS), f32),
+        ),
+        in_specs=[in_smem] + [in_vmem] * 2 + [in_hbm],
+        out_specs=[in_hbm, in_vmem],
+        scratch_shapes=[
+            pltpu.VMEM((2, CELLS, WIDTH), f32),
+            pltpu.SemaphoreType.DMA((2,)),
             pltpu.SemaphoreType.DMA((SLOTS,)),
         ],
-        compiler_params=params(40),
-        name="assemble_patches",
-    )(refine, code, owner, arrived, force, *pieces)
+        compiler_params=params(24),
+        cost_estimate=pl.CostEstimate(flops=1 << 20, bytes_accessed=6 << 20, transcendentals=0),
+        name="block_interior",
+    )(source, arrived, fresh, force)
 
 
 def edge_kernel(rows, from_left, from_right, top, bottom, side):
     blank = jnp.zeros((CELLS - 2 * HALO, CELLS), jnp.float32)
     for field in range(FIELDS):
         tile = jnp.concatenate([from_right[field], blank, from_left[field]], axis=0).T
-        side[field] = tile
-        top[field, :SLOTS] = rows[0, field]
-        top[field, SLOTS] = tile[:HALO]
-        bottom[field, :SLOTS] = rows[1, field]
-        bottom[field, SLOTS] = tile[CELLS - HALO :]
+        side[field, :HALO] = tile[:HALO]
+        side[field, HALO : HALO + CELLS] = tile
+        side[field, HALO + CELLS :] = tile[:HALO]
+        for block in range(SLOTS):
+            at = slice(block * CELLS, (block + 1) * CELLS)
+            top[field, :, at] = rows[0, field, block]
+            bottom[field, :, at] = rows[1, field, block]
+        top[field, :, WIDTH:] = tile[:HALO]
+        bottom[field, :, WIDTH:] = tile[CELLS - HALO :]
 
 
 def edges(rows, from_left, from_right):
@@ -226,9 +347,9 @@
     return pl.pallas_call(
         edge_kernel,
         out_shape=(
-            jax.ShapeDtypeStruct((FIELDS, BLOCKS, HALO, CELLS), f32),
-            jax.ShapeDtypeStruct((FIELDS, BLOCKS, HALO, CELLS), f32),
-            jax.ShapeDtypeStruct((FIELDS, CELLS, CELLS), f32),
+            jax.ShapeDtypeStruct((FIELDS, HALO, EXT_COLS), f32),
+            jax.ShapeDtypeStruct((FIELDS, HALO, EXT_COLS), f32),
+            jax.ShapeDtypeStruct((FIELDS, EXT_ROWS, CELLS), f32),
         ),
         in_specs=[in_vmem] * 3,
         out_specs=[in_vmem] * 3,
@@ -237,19 +358,21 @@
     )(rows, from_left, from_right)
 
 
-def sweep_kernel(state, side, above, below, out, wide, right, velo, faces, out_sems):
-    for field in range(FIELDS):
-        at = slice(field * CELLS, (field + 1) * CELLS)
-        for block in range(BLOCKS):
-            wide[field, block, :HALO] = above[field, block]
-            wide[field, block, HALO + CELLS :] = below[field, block]
-            wide[field, block, HALO : HALO + CELLS] = side[field] if block == SLOTS else state[block, at]
+def sweep_kernel(inner, side, above, below, out, done_v, right, velo, faces, out_sems):
+    row = lax.broadcasted_iota(jnp.int32, (8, EXT_COLS), 0)
 
     def rows_of(t):
         return pl.ds(t, 8, stride=TILES)
 
     def spaced(field, t):
-        return jnp.concatenate([wide[field, block, rows_of(t), :] for block in range(BLOCKS)], axis=1)
+        parts = [inner[field, block, rows_of(t), :] for block in range(SLOTS)]
+        value = jnp.concatenate(parts + [side[field, rows_of(t), :]], axis=1)
+        if t < HALO:
+            value = jnp.where(row == 0, above[field, t : t + 1, :], value)
+        if t >= TILES - HALO:
+            first = t - (TILES - HALO)
+            value = jnp.where(row == 7, below[field, first : first + 1, :], value)
+        return value
 
     def each_tile(load):
         first, last = load(0), load(TILES - 1)
@@ -292,7 +415,7 @@
 
     def out_copy(field, block):
         cols = pl.ds(block * CELLS, CELLS)
-        source = wide.at[field, block, pl.ds(HALO, CELLS)]
+        source = done_v.at[field, block, pl.ds(HALO, CELLS)]
         return pltpu.make_async_copy(source, out.at[field, :, cols], out_sems.at[field, block])
 
     now = (SWEEPS - 2) % 2
@@ -300,7 +423,7 @@
         for t, here, others in each_tile(lambda t: velo[now, field, t]):
             done = relaxed(now, field, t, here, others)
             for block in range(SLOTS):
-                wide[field, block, rows_of(t), :] = done[:, block * CELLS : (block + 1) * CELLS]
+                done_v[field, block, rows_of(t), :] = done[:, block * CELLS : (block + 1) * CELLS]
         for block in range(SLOTS):
             out_copy(field, block).start()
     for field in range(2):
@@ -308,7 +431,7 @@
             out_copy(field, block).wait()
 
 
-def sweeps(state, side, above, below):
+def sweeps(inner, side, above, below):
     f32 = jnp.float32
     tiles = (TILES, 8, EXT_COLS)
     return pl.pallas_call(
@@ -317,7 +440,7 @@
         in_specs=[in_vmem] * 4,
         out_specs=in_any,
         scratch_shapes=[
-            pltpu.VMEM((FIELDS, BLOCKS, EXT_ROWS, CELLS), f32),
+            pltpu.VMEM((2, SLOTS, EXT_ROWS, CELLS), f32),
             pltpu.VMEM((2,) + tiles, f32),
             pltpu.VMEM((2, 2) + tiles, f32),
             pltpu.VMEM((4,) + tiles, f32),
@@ -325,7 +448,7 @@
         ],
         compiler_params=params(40),
         name="jacobi_sweeps",
-    )(state, side, above, below)
+    )(inner, side, above, below)
 
 
 def moved(value, axis, step):
@@ -358,18 +481,21 @@
     gx = lax.axis_index("gx")
     outgoing = stage(old_dest[0], old_state.reshape(SLOTS, PATCH_ROWS, CELLS))
     arrived = lax.all_to_all(outgoing, "gy", split_axis=0, concat_axis=0, tiled=True)
-    pieces = column_pieces(coarse_state.reshape(2, PATCH_ROWS, CELLS))
+    coarse = coarse_state.reshape(2, PATCH_ROWS, CELLS)
+    kept = swapped(swapped(keep(force, coarse), "gx", 1), "gx", 1)
+    pieces = [kept.reshape(KEPT, PATCH_ROWS, CELLS)] + column_pieces(coarse)[1:]
     holder = parent_block[0, :1] >> 3
     owner = (((holder >> 1) - (gx >> 1)) & 3) + 4 * ((holder ^ gx) & 1)
-    depth, state, left, right, rows = assemble(
-        refine[0], parent_block[0], owner, arrived, force, pieces
+    source, fresh, left, right, rows = outline(
+        refine[0], parent_block[0], owner, arrived, pieces
     )
+    depth, inner = interior(source, arrived, fresh, force)
     from_left = moved(right, "gy", 1)
     from_right = moved(left, "gy", -1)
     top, bottom, side = edges(rows, from_left, from_right)
     above = moved(bottom, "gx", 1)
     below = moved(top, "gx", -1)
-    velocity = sweeps(state, side, above, below)
+    velocity = sweeps(inner, side, above, below)
     return depth, velocity
 
 

time: 93.2 us -> 88.4 us (0.948)
  waiting for transfers between devices: 44.3 us -> 41.6 us
  starting transfers between devices: 31.1 us -> 29.5 us
  local copies, waits for them, and re-layouts: 2.23 us -> 1.24 us
    all_to_all x1, waiting for transfers between devices: 18.4 us -> 14.5 us  [body(): lax.all_to_all(outgoing, 'gy', split_axis=0, concat_axis=0, tiled=True)]
    ppermute x3, waiting for transfers between devices: 15.6 us -> 18.2 us  [around_ring(): lax.ppermute(value, axis, [(i, (i + step) % count) for i in range(count)])]
    ppermute x4, waiting for transfers between devices: 8.74 us -> 7.23 us  [moved(): return lax.ppermute(value, axis, pairs)]
    ppermute x4 -> x6, starting transfers between devices: 5.26 us -> 3.84 us  [swapped(): return lax.ppermute(value, axis, [(i, i ^ bit) for i in range(count)])]
    unnamed x8, local copies, waits for them, and re-layouts: 2.23 us -> 1.24 us
    pallas_call x2 -> x4, Pallas kernels: 5.06 us -> 5.65 us  [the longest x1 2.55 us: outline(): pl.pallas_call(outline_kernel, out_shape=(jax.ShapeDtypeStruct((SLOTS,),...]
  transfers between devices with their start and end apart: 12 -> 14, of which waited for: 6 -> 6; matrix products, arithmetic and copies ran while one was open for 0% -> 0% of each run, Pallas kernels for 0% -> 3%
where the time goes in v2:
time: 88.4 us; the launch traced here: 87.7 us
  waiting for transfers between devices  41.6 us (47%)
  starting transfers between devices  29.5 us (33%)
  Pallas kernels  14.6 us (17%)
  local copies, waits for them, and re-layouts  1.24 us (1%)
    ppermute x3, waiting for transfers between devices, around_ring(): lax.ppermute(value, axis, [(i, (i + step) % count) for i in range(count)])  18.2 us
    all_to_all x1, waiting for transfers between devices, body(): lax.all_to_all(outgoing, 'gy', split_axis=0, concat_axis=0, tiled=True)  14.5 us
    ppermute x4, starting transfers between devices, moved(): return lax.ppermute(value, axis, pairs)  14.3 us
    ppermute x4, waiting for transfers between devices, moved(): return lax.ppermute(value, axis, pairs)  7.23 us
    all_to_all x1, starting transfers between devices, body(): lax.all_to_all(outgoing, 'gy', split_axis=0, concat_axis=0, tiled=True)  6.89 us
    pallas_call x1, Pallas kernels, sweeps(): pl.pallas_call(sweep_kernel, out_shape=jax.ShapeDtypeStruct((2, CELLS, WI...  5.94 us
    ppermute x3, starting transfers between devices, around_ring(): lax.ppermute(value, axis, [(i, (i + step) % count) for i in range(count)])  4.49 us
    ppermute x6, starting transfers between devices, swapped(): return lax.ppermute(value, axis, [(i, i ^ bit) for i in range(count)])  3.84 us
  transfers between devices with their start and end apart: 14, of which 6 were waited for; matrix products, arithmetic and copies ran while one was open for 0% of the time, Pallas kernels for 3%

profile of v2, /device:TPU:7, one launch (start us, length us, event | category | flops | bytes accessed | tf_op | source)
XLA Modules:
  0.0 87.7 jit_solution(13388565269075238734)
XLA Ops:
  0.6 3.0 %stage_outgoing.1 = f32[16,392,128]{2,1,0:T(8,128)} custom-call(s32[8]{0:T(128)} %bitcast.14, f32[8,384,128]{2,1,0:T(8,128)} %bitcast.13), custom_call_target="tpu_custom_call" | custom-call | tf_op jit(solution)/shard_map/stage_outgoing/pallas_call | solution.py:75
  3.6 6.9 %all-to-all-start = ((f32[16,392,128]{2,1,0:T(8,128)}), f32[16,392,128]{2,1,0:T(8,128)S(1)}, u32[]{:S(2)}, u32[]{:S(2)}) async-start(f32[16,392,128]{2,1,0:T(8,128)} %stage_outgoing.1), calls=%async_computation | async-start | bytes 6422528 | tf_op jit(solution)/shard_map/all_to_all | solution.py:483
  10.5 1.2 %copy-done = f32[2,128,1024]{2,1,0:T(8,128)S(1)} copy-done((f32[2,128,1024]{2,1,0:T(8,128)S(1)}, f32[2,128,1024]{2,1,0:T(8,128)}, u32[]{:S(2)}) %copy-start) | copy-done | bytes 1048600
  11.8 1.5 %keep_own.1 = f32[1536,128]{1,0:T(8,128)S(1)} custom-call(f32[2,128,1024]{2,1,0:T(8,128)S(1)} %copy-done, f32[2,384,128]{2,1,0:T(8,128)} %bitcast.7.coarse), custom_call_target="tpu_custom_call" | custom-call | flops 262144 | bytes 3145728 | tf_op jit(solution)/shard_map/keep_own/pallas_call | solution.py:122
  13.2 1.3 %collective-permute-start = (f32[1536,128]{1,0:T(8,128)S(1)}, f32[1536,128]{1,0:T(8,128)}, u32[]{:S(2)}, u32[]{:S(2)}) collective-permute-start(f32[1536,128]{1,0:T(8,128)S(1)} %keep_own.1), channel_id=1, source_target_pairs={{0,16},{16,0},{32,48},{48,32},{64,80},{80,64},{96,112},{112,96},{1... | collective-permute-start | bytes 2359304 | tf_op jit(solution)/shard_map/ppermute | solution.py:467
  14.6 3.7 %collective-permute-start.2 = (f32[2,384,128]{2,1,0:T(8,128)}, f32[2,384,128]{2,1,0:T(8,128)}, u32[]{:S(2)}, u32[]{:S(2)}) collective-permute-start(f32[2,384,128]{2,1,0:T(8,128)} %bitcast.7.coarse), channel_id=1, source_target_pairs={{0,96},{16,112},{32,0},{48,16},{64,32},{80,48},{96,64},{112,80},{1... | collective-permute-start | bytes 1179656 | tf_op jit(solution)/shard_map/ppermute | solution.py:462
  18.3 0.8 collective-permute-start.4
  19.0 0.9 %collective-permute-start.1 = (f32[1536,128]{1,0:T(8,128)}, f32[1536,128]{1,0:T(8,128)}, u32[]{:S(2)}, u32[]{:S(2)}) collective-permute-start(f32[1536,128]{1,0:T(8,128)} %collective-permute-done), channel_id=1, source_target_pairs={{0,16},{16,0},{32,48},{48,32},{64,80},{80,64},{96,112},{112,96},{1... | collective-permute-start | bytes 2359304 | tf_op jit(solution)/shard_map/ppermute | solution.py:467
  20.0 15.5 %collective-permute-done.2.refs_1_ = f32[2,384,128]{2,1,0:T(8,128)} collective-permute-done((f32[2,384,128]{2,1,0:T(8,128)}, f32[2,384,128]{2,1,0:T(8,128)}, u32[]{:S(2)}, u32[]{:S(2)}) %collective-permute-start.2) | collective-permute-done | bytes 393248 | tf_op jit(solution)/shard_map/ppermute | solution.py:462
  35.5 0.9 collective-permute-start.6
  36.4 2.6 %collective-permute-done.4.refs_3_ = f32[2,384,128]{2,1,0:T(8,128)} collective-permute-done((f32[2,384,128]{2,1,0:T(8,128)}, f32[2,384,128]{2,1,0:T(8,128)}, u32[]{:S(2)}, u32[]{:S(2)}) %collective-permute-start.4) | collective-permute-done | bytes 393248 | tf_op jit(solution)/shard_map/ppermute | solution.py:462
  39.0 0.8 collective-permute-start.8
  39.9 1.6 %collective-permute-done.8.refs_7_ = f32[2,384,128]{2,1,0:T(8,128)} collective-permute-done((f32[2,384,128]{2,1,0:T(8,128)}, f32[2,384,128]{2,1,0:T(8,128)}, u32[]{:S(2)}, u32[]{:S(2)}) %collective-permute-start.8) | collective-permute-done | bytes 393248 | tf_op jit(solution)/shard_map/ppermute | solution.py:467
  41.5 14.5 %all-to-all-done.arrived = f32[16,392,128]{2,1,0:T(8,128)S(1)} async-done(((f32[16,392,128]{2,1,0:T(8,128)}), f32[16,392,128]{2,1,0:T(8,128)S(1)}, u32[]{:S(2)}, u32[]{:S(2)}) %all-to-all-start) | async-done | bytes 3211296 | tf_op jit(solution)/shard_map/all_to_all | solution.py:483
  56.0 2.6 %block_outline.1 = (s32[8]{0:T(128)S(1)}, f32[2,384,128]{2,1,0:T(8,128)S(1)}, f32[3,8,128]{2,1,0:T(8,128)S(1)}, f32[3,8,128]{2,1,0:T(8,128)S(1)}, f32[2,3,8,8,128]{4,3,2,1,0:T(8,128)S(1)}) custom-call(s32[8]{0:T(128)S(1)} %bitcast.10, s32[8]{0:T(128)S(1)} %bitcast.12, s32[1]{0:T(128)S(6)} %add.3.owner, f32[16,392,128]{2,1,0:T(8,128)S(1)} %all-to-all-done.arrived, ...), custom_call_target="tpu_custom_call" | custom-call | tf_op jit(solution)/shard_map/block_outline/pallas_call | solution.py:257
  58.5 3.8 %collective-permute-start.9 = (f32[3,8,128]{2,1,0:T(8,128)S(1)}, f32[3,8,128]{2,1,0:T(8,128)S(1)}, u32[]{:S(2)}, u32[]{:S(2)}) collective-permute-start(f32[3,8,128]{2,1,0:T(8,128)S(1)} %get-tuple-element.17), channel_id=1, source_target_pairs={{0,1},{1,2},{2,3},{3,4},{4,5},{5,6},{6,7},{7,8},{8,9},{9,10},{10,1... | collective-permute-start | bytes 36872 | tf_op jit(solution)/shard_map/ppermute | solution.py:457
  62.4 1.9 %collective-permute-start.10 = (f32[3,8,128]{2,1,0:T(8,128)S(1)}, f32[3,8,128]{2,1,0:T(8,128)S(1)}, u32[]{:S(2)}, u32[]{:S(2)}) collective-permute-start(f32[3,8,128]{2,1,0:T(8,128)S(1)} %get-tuple-element.18), channel_id=1, source_target_pairs={{1,0},{2,1},{3,2},{4,3},{5,4},{6,5},{7,6},{8,7},{9,8},{10,9},{11,1... | collective-permute-start | bytes 36872 | tf_op jit(solution)/shard_map/ppermute | solution.py:457
  64.3 4.6 %collective-permute-done.10.from_right = f32[3,8,128]{2,1,0:T(8,128)S(1)} collective-permute-done((f32[3,8,128]{2,1,0:T(8,128)S(1)}, f32[3,8,128]{2,1,0:T(8,128)S(1)}, u32[]{:S(2)}, u32[]{:S(2)}) %collective-permute-start.10) | collective-permute-done | bytes 12320 | tf_op jit(solution)/shard_map/ppermute | solution.py:457
  68.9 0.1 edge_rows.1
  69.0 6.7 %collective-permute-start.11 = (f32[3,8,1152]{2,1,0:T(8,128)S(1)}, f32[3,8,1152]{2,1,0:T(8,128)S(1)}, u32[]{:S(2)}, u32[]{:S(2)}) collective-permute-start(f32[3,8,1152]{2,1,0:T(8,128)S(1)} %get-tuple-element.20), channel_id=1, source_target_pairs={{0,16},{16,32},{32,48},{48,64},{64,80},{80,96},{96,112},{1,17},{17... | collective-permute-start | bytes 331784 | tf_op jit(solution)/shard_map/ppermute | solution.py:457
  75.7 1.9 %collective-permute-start.12 = (f32[3,8,1152]{2,1,0:T(8,128)S(1)}, f32[3,8,1152]{2,1,0:T(8,128)S(1)}, u32[]{:S(2)}, u32[]{:S(2)}) collective-permute-start(f32[3,8,1152]{2,1,0:T(8,128)S(1)} %get-tuple-element.21), channel_id=1, source_target_pairs={{16,0},{32,16},{48,32},{64,48},{80,64},{96,80},{112,96},{17,1},{33... | collective-permute-start | bytes 331784 | tf_op jit(solution)/shard_map/ppermute | solution.py:457
  77.7 1.5 %block_interior.1 = (f32[128,1024]{1,0:T(8,128)}, f32[3,8,144,128]{3,2,1,0:T(8,128)S(1)}) custom-call(s32[8]{0:T(128)S(1)} %get-tuple-element.12.source, f32[16,392,128]{2,1,0:T(8,128)S(1)} %all-to-all-done.arrived, f32[2,384,128]{2,1,0:T(8,128)S(1)} %get-tuple-element.13.fresh, f32[2,128,1024]{2,1,0:T(8,128)S(1)} %copy-done.1), custom_call_target="tpu_custom_call" | custom-call | flops 1048576 | bytes 6291456 | tf_op jit(solution)/shard_map/block_interior/pallas_call | solution.py:311
  79.2 2.6 %collective-permute-done.12.below = f32[3,8,1152]{2,1,0:T(8,128)S(1)} collective-permute-done((f32[3,8,1152]{2,1,0:T(8,128)S(1)}, f32[3,8,1152]{2,1,0:T(8,128)S(1)}, u32[]{:S(2)}, u32[]{:S(2)}) %collective-permute-start.12) | collective-permute-done | bytes 110624 | tf_op jit(solution)/shard_map/ppermute | solution.py:457
  81.8 5.9 %jacobi_sweeps.1 = f32[2,128,1024]{2,1,0:T(8,128)} custom-call(f32[3,8,144,128]{3,2,1,0:T(8,128)S(1)} %get-tuple-element.15.inner, f32[3,144,128]{2,1,0:T(8,128)S(1)} %get-tuple-element.19.side, f32[3,8,1152]{2,1,0:T(8,128)S(1)} %collective-permute-done.11.above, f32[3,8,1152]{2,1,0:T(8,128)S(1)} %collective-permute-done.12.below), custom_call_target="tpu_custom_call" | custom-call | tf_op jit(solution)/shard_map/jacobi_sweeps/pallas_call | solution.py:437
  (18 shorter events, 0.0 us)
Async XLA Ops:
  3.6 36.2 %copy-start.3 = (s32[1,8]{1,0:T(1,128)S(1)}, s32[1,8]{1,0:T(1,128)}, u32[]{:S(2)}) copy-start(s32[1,8]{1,0:T(1,128)} %param.9) | copy-start | bytes 100
  3.6 52.4 %copy-start.2 = (s32[1,8]{1,0:T(1,128)S(1)}, s32[1,8]{1,0:T(1,128)}, u32[]{:S(2)}) copy-start(s32[1,8]{1,0:T(1,128)} %param.8) | copy-start | bytes 100
  3.6 52.3 %all-to-all-start = ((f32[16,392,128]{2,1,0:T(8,128)}), f32[16,392,128]{2,1,0:T(8,128)S(1)}, u32[]{:S(2)}, u32[]{:S(2)}) async-start(f32[16,392,128]{2,1,0:T(8,128)} %stage_outgoing.1), calls=%async_computation | async-start | bytes 6422528 | tf_op jit(solution)/shard_map/all_to_all | solution.py:483
  10.5 1.2 %copy-start = (f32[2,128,1024]{2,1,0:T(8,128)S(1)}, f32[2,128,1024]{2,1,0:T(8,128)}, u32[]{:S(2)}) copy-start(f32[2,128,1024]{2,1,0:T(8,128)} %force.3) | copy-start | bytes 3145732
  13.2 5.8 %collective-permute-start = (f32[1536,128]{1,0:T(8,128)S(1)}, f32[1536,128]{1,0:T(8,128)}, u32[]{:S(2)}, u32[]{:S(2)}) collective-permute-start(f32[1536,128]{1,0:T(8,128)S(1)} %keep_own.1), channel_id=1, source_target_pairs={{0,16},{16,0},{32,48},{48,32},{64,80},{80,64},{96,112},{112,96},{1... | collective-permute-start | bytes 2359304 | tf_op jit(solution)/shard_map/ppermute | solution.py:467
  14.6 21.0 %collective-permute-start.2 = (f32[2,384,128]{2,1,0:T(8,128)}, f32[2,384,128]{2,1,0:T(8,128)}, u32[]{:S(2)}, u32[]{:S(2)}) collective-permute-start(f32[2,384,128]{2,1,0:T(8,128)} %bitcast.7.coarse), channel_id=1, source_target_pairs={{0,96},{16,112},{32,0},{48,16},{64,32},{80,48},{96,64},{112,80},{1... | collective-permute-start | bytes 1179656 | tf_op jit(solution)/shard_map/ppermute | solution.py:462
  18.3 18.1 %collective-permute-start.3 = (f32[2,384,128]{2,1,0:T(8,128)}, f32[2,384,128]{2,1,0:T(8,128)}, u32[]{:S(2)}, u32[]{:S(2)}) collective-permute-start(f32[2,384,128]{2,1,0:T(8,128)} %bitcast.7.coarse), channel_id=1, source_target_pairs={{0,64},{16,80},{32,96},{48,112},{64,0},{80,16},{96,32},{112,48},{1... | collective-permute-start | bytes 1179656 | tf_op jit(solution)/shard_map/ppermute | solution.py:462
  18.3 20.7 %collective-permute-start.4 = (f32[2,384,128]{2,1,0:T(8,128)}, f32[2,384,128]{2,1,0:T(8,128)}, u32[]{:S(2)}, u32[]{:S(2)}) collective-permute-start(f32[2,384,128]{2,1,0:T(8,128)} %bitcast.7.coarse), channel_id=1, source_target_pairs={{0,32},{16,48},{32,64},{48,80},{64,96},{80,112},{96,0},{112,16},{1... | collective-permute-start | bytes 1179656 | tf_op jit(solution)/shard_map/ppermute | solution.py:462
  19.0 22.4 %collective-permute-start.1 = (f32[1536,128]{1,0:T(8,128)}, f32[1536,128]{1,0:T(8,128)}, u32[]{:S(2)}, u32[]{:S(2)}) collective-permute-start(f32[1536,128]{1,0:T(8,128)} %collective-permute-done), channel_id=1, source_target_pairs={{0,16},{16,0},{32,48},{48,32},{64,80},{80,64},{96,112},{112,96},{1... | collective-permute-start | bytes 2359304 | tf_op jit(solution)/shard_map/ppermute | solution.py:467
  20.0 19.9 %collective-permute-start.5 = (f32[2,384,128]{2,1,0:T(8,128)}, f32[2,384,128]{2,1,0:T(8,128)}, u32[]{:S(2)}, u32[]{:S(2)}) collective-permute-start(f32[2,384,128]{2,1,0:T(8,128)} %bitcast.7.coarse), channel_id=1, source_target_pairs={{0,16},{16,0},{32,48},{48,32},{64,80},{80,64},{96,112},{112,96},{1... | collective-permute-start | bytes 1179656 | tf_op jit(solution)/shard_map/ppermute | solution.py:467
  35.5 4.3 %collective-permute-start.6 = (f32[2,384,128]{2,1,0:T(8,128)}, f32[2,384,128]{2,1,0:T(8,128)}, u32[]{:S(2)}, u32[]{:S(2)}) collective-permute-start(f32[2,384,128]{2,1,0:T(8,128)} %collective-permute-done.2.refs_1_), channel_id=1, source_target_pairs={{0,16},{16,0},{32,48},{48,32},{64,80},{80,64},{96,112},{112,96},{1... | collective-permute-start | bytes 1179656 | tf_op jit(solution)/shard_map/ppermute | solution.py:467
  36.4 3.5 %collective-permute-start.7 = (f32[2,384,128]{2,1,0:T(8,128)}, f32[2,384,128]{2,1,0:T(8,128)}, u32[]{:S(2)}, u32[]{:S(2)}) collective-permute-start(f32[2,384,128]{2,1,0:T(8,128)} %collective-permute-done.3.refs_2_), channel_id=1, source_target_pairs={{0,16},{16,0},{32,48},{48,32},{64,80},{80,64},{96,112},{112,96},{1... | collective-permute-start | bytes 1179656 | tf_op jit(solution)/shard_map/ppermute | solution.py:467
  39.0 2.4 %collective-permute-start.8 = (f32[2,384,128]{2,1,0:T(8,128)}, f32[2,384,128]{2,1,0:T(8,128)}, u32[]{:S(2)}, u32[]{:S(2)}) collective-permute-start(f32[2,384,128]{2,1,0:T(8,128)} %collective-permute-done.4.refs_3_), channel_id=1, source_target_pairs={{0,16},{16,0},{32,48},{48,32},{64,80},{80,64},{96,112},{112,96},{1... | collective-permute-start | bytes 1179656 | tf_op jit(solution)/shard_map/ppermute | solution.py:467
  56.0 21.7 %copy-start.1 = (f32[2,128,1024]{2,1,0:T(8,128)S(1)}, f32[2,128,1024]{2,1,0:T(8,128)}, u32[]{:S(2)}) copy-start(f32[2,128,1024]{2,1,0:T(8,128)} %force.3) | copy-start | bytes 3145732
  58.5 5.8 %collective-permute-start.9 = (f32[3,8,128]{2,1,0:T(8,128)S(1)}, f32[3,8,128]{2,1,0:T(8,128)S(1)}, u32[]{:S(2)}, u32[]{:S(2)}) collective-permute-start(f32[3,8,128]{2,1,0:T(8,128)S(1)} %get-tuple-element.17), channel_id=1, source_target_pairs={{0,1},{1,2},{2,3},{3,4},{4,5},{5,6},{6,7},{7,8},{8,9},{9,10},{10,1... | collective-permute-start | bytes 36872 | tf_op jit(solution)/shard_map/ppermute | solution.py:457
  62.4 6.5 %collective-permute-start.10 = (f32[3,8,128]{2,1,0:T(8,128)S(1)}, f32[3,8,128]{2,1,0:T(8,128)S(1)}, u32[]{:S(2)}, u32[]{:S(2)}) collective-permute-start(f32[3,8,128]{2,1,0:T(8,128)S(1)} %get-tuple-element.18), channel_id=1, source_target_pairs={{1,0},{2,1},{3,2},{4,3},{5,4},{6,5},{7,6},{8,7},{9,8},{10,9},{11,1... | collective-permute-start | bytes 36872 | tf_op jit(solution)/shard_map/ppermute | solution.py:457
  69.0 10.1 %collective-permute-start.11 = (f32[3,8,1152]{2,1,0:T(8,128)S(1)}, f32[3,8,1152]{2,1,0:T(8,128)S(1)}, u32[]{:S(2)}, u32[]{:S(2)}) collective-permute-start(f32[3,8,1152]{2,1,0:T(8,128)S(1)} %get-tuple-element.20), channel_id=1, source_target_pairs={{0,16},{16,32},{32,48},{48,64},{64,80},{80,96},{96,112},{1,17},{17... | collective-permute-start | bytes 331784 | tf_op jit(solution)/shard_map/ppermute | solution.py:457
  75.7 6.1 %collective-permute-start.12 = (f32[3,8,1152]{2,1,0:T(8,128)S(1)}, f32[3,8,1152]{2,1,0:T(8,128)S(1)}, u32[]{:S(2)}, u32[]{:S(2)}) collective-permute-start(f32[3,8,1152]{2,1,0:T(8,128)S(1)} %get-tuple-element.21), channel_id=1, source_target_pairs={{16,0},{32,16},{48,32},{64,48},{80,64},{96,80},{112,96},{17,1},{33... | collective-permute-start | bytes 331784 | tf_op jit(solution)/shard_map/ppermute | solution.py:457

commit v3 on v2

--- a/solution.py
+++ b/solution.py
@@ -160,7 +160,8 @@
 
 def outline_kernel(refine, code, owner, arrived, *refs):
     pieces, refs = refs[:OWNERS], refs[OWNERS:]
-    source, fresh, left, right, rows, parent_v, note_i, force_v, picks, sems, force_sem = refs
+    source, fresh, sends, rows, parent_v, note_i, force_v, picks, sems, force_sem = refs
+    odd_column = (lax.axis_index("gy") & 1) > 0
     force_copy = pltpu.make_async_copy(pieces[0].at[pl.ds(2, 2)], force_v, force_sem)
     force_copy.start()
 
@@ -241,8 +242,9 @@
         if field > 0:
             first = first + forcing(COLS_AT + (2 * field - 2) * CELLS, CELLS)
             last = last + forcing(COLS_AT + (2 * field - 1) * CELLS, CELLS)
-        left[field] = first.T[:HALO]
-        right[field] = last.T[CELLS - HALO :]
+        left, right = first.T[:HALO], last.T[CELLS - HALO :]
+        sends[0, field] = jnp.where(odd_column, left, right)
+        sends[1, field] = jnp.where(odd_column, right, left)
         for slot in range(SLOTS):
             for edge, first in enumerate((low, low + CELLS - HALO)):
                 value = taken(slot, first, HALO)
@@ -259,12 +261,11 @@
         out_shape=(
             jax.ShapeDtypeStruct((SLOTS,), jnp.int32),
             jax.ShapeDtypeStruct((REFINED, PATCH_ROWS, CELLS), f32),
-            jax.ShapeDtypeStruct((FIELDS, HALO, CELLS), f32),
-            jax.ShapeDtypeStruct((FIELDS, HALO, CELLS), f32),
+            jax.ShapeDtypeStruct((2, FIELDS, HALO, CELLS), f32),
             jax.ShapeDtypeStruct((2, FIELDS, SLOTS, HALO, CELLS), f32),
         ),
         in_specs=[in_smem] * 3 + [in_vmem] + [in_any] * OWNERS,
-        out_specs=[in_smem] + [in_vmem] * 4,
+        out_specs=[in_smem] + [in_vmem] * 3,
         scratch_shapes=[
             pltpu.VMEM((REFINED, FIELDS, CELLS // 2, CELLS), f32),
             pltpu.VMEM((PEERS, CELLS), jnp.int32),
@@ -327,39 +328,49 @@
     )(source, arrived, fresh, force)
 
 
-def edge_kernel(rows, from_left, from_right, top, bottom, side):
+def edge_kernel(rows, first, second, sends, side):
+    odd_row, odd_column = (lax.axis_index("gx") & 1) > 0, (lax.axis_index("gy") & 1) > 0
     blank = jnp.zeros((CELLS - 2 * HALO, CELLS), jnp.float32)
     for field in range(FIELDS):
-        tile = jnp.concatenate([from_right[field], blank, from_left[field]], axis=0).T
+        one, two = first[field], second[field]
+        from_right = jnp.where(odd_column, two, one)
+        from_left = jnp.where(odd_column, one, two)
+        tile = jnp.concatenate([from_right, blank, from_left], axis=0).T
         side[field, :HALO] = tile[:HALO]
         side[field, HALO : HALO + CELLS] = tile
         side[field, HALO + CELLS :] = tile[:HALO]
-        for block in range(SLOTS):
+        for block in range(BLOCKS):
+            if block < SLOTS:
+                top, bottom = rows[0, field, block], rows[1, field, block]
+            else:
+                top, bottom = tile[:HALO], tile[CELLS - HALO :]
             at = slice(block * CELLS, (block + 1) * CELLS)
-            top[field, :, at] = rows[0, field, block]
-            bottom[field, :, at] = rows[1, field, block]
-        top[field, :, WIDTH:] = tile[:HALO]
-        bottom[field, :, WIDTH:] = tile[CELLS - HALO :]
-
-
-def edges(rows, from_left, from_right):
+            sends[0, field, :, at] = jnp.where(odd_row, top, bottom)
+            sends[1, field, :, at] = jnp.where(odd_row, bottom, top)
+
+
+def edges(rows, first, second):
     f32 = jnp.float32
     return pl.pallas_call(
         edge_kernel,
         out_shape=(
-            jax.ShapeDtypeStruct((FIELDS, HALO, EXT_COLS), f32),
-            jax.ShapeDtypeStruct((FIELDS, HALO, EXT_COLS), f32),
+            jax.ShapeDtypeStruct((2, FIELDS, HALO, EXT_COLS), f32),
             jax.ShapeDtypeStruct((FIELDS, EXT_ROWS, CELLS), f32),
         ),
         in_specs=[in_vmem] * 3,
-        out_specs=[in_vmem] * 3,
+        out_specs=[in_vmem] * 2,
         compiler_params=params(16),
         name="edge_rows",
-    )(rows, from_left, from_right)
-
-
-def sweep_kernel(inner, side, above, below, out, done_v, right, velo, faces, out_sems):
+    )(rows, first, second)
+
+
+def sweep_kernel(inner, side, first, second, out, done_v, right, velo, faces, above, below, out_sems):
     row = lax.broadcasted_iota(jnp.int32, (8, EXT_COLS), 0)
+    odd_row = (lax.axis_index("gx") & 1) > 0
+    for field in range(FIELDS):
+        one, two = first[field], second[field]
+        above[field] = jnp.where(odd_row, one, two)
+        below[field] = jnp.where(odd_row, two, one)
 
     def rows_of(t):
         return pl.ds(t, 8, stride=TILES)
@@ -431,7 +442,7 @@
             out_copy(field, block).wait()
 
 
-def sweeps(inner, side, above, below):
+def sweeps(inner, side, first, second):
     f32 = jnp.float32
     tiles = (TILES, 8, EXT_COLS)
     return pl.pallas_call(
@@ -444,17 +455,19 @@
             pltpu.VMEM((2,) + tiles, f32),
             pltpu.VMEM((2, 2) + tiles, f32),
             pltpu.VMEM((4,) + tiles, f32),
+            pltpu.VMEM((FIELDS, HALO, EXT_COLS), f32),
+            pltpu.VMEM((FIELDS, HALO, EXT_COLS), f32),
             pltpu.SemaphoreType.DMA((2, SLOTS)),
         ],
         compiler_params=params(40),
         name="jacobi_sweeps",
-    )(inner, side, above, below)
-
-
-def moved(value, axis, step):
+    )(inner, side, first, second)
+
+
+def paired(value, axis, start):
     count = lax.axis_size(axis)
-    pairs = [(i, i + step) for i in range(count) if 0 <= i + step < count]
-    return lax.ppermute(value, axis, pairs)
+    pairs = [(i, i + 1) for i in range(start, count - 1, 2)]
+    return lax.ppermute(value, axis, pairs + [(j, i) for i, j in pairs])
 
 
 def around_ring(value, axis, step):
@@ -478,24 +491,20 @@
 
 
 def body(old_state, old_dest, refine, parent_block, coarse_state, force):
-    gx = lax.axis_index("gx")
     outgoing = stage(old_dest[0], old_state.reshape(SLOTS, PATCH_ROWS, CELLS))
     arrived = lax.all_to_all(outgoing, "gy", split_axis=0, concat_axis=0, tiled=True)
     coarse = coarse_state.reshape(2, PATCH_ROWS, CELLS)
     kept = swapped(swapped(keep(force, coarse), "gx", 1), "gx", 1)
     pieces = [kept.reshape(KEPT, PATCH_ROWS, CELLS)] + column_pieces(coarse)[1:]
+    gx = lax.axis_index("gx")
     holder = parent_block[0, :1] >> 3
     owner = (((holder >> 1) - (gx >> 1)) & 3) + 4 * ((holder ^ gx) & 1)
-    source, fresh, left, right, rows = outline(
-        refine[0], parent_block[0], owner, arrived, pieces
-    )
+    source, fresh, sends, rows = outline(refine[0], parent_block[0], owner, arrived, pieces)
     depth, inner = interior(source, arrived, fresh, force)
-    from_left = moved(right, "gy", 1)
-    from_right = moved(left, "gy", -1)
-    top, bottom, side = edges(rows, from_left, from_right)
-    above = moved(bottom, "gx", 1)
-    below = moved(top, "gx", -1)
-    velocity = sweeps(inner, side, above, below)
+    first, second = paired(sends[0], "gy", 0), paired(sends[1], "gy", 1)
+    sends, side = edges(rows, first, second)
+    first, second = paired(sends[0], "gx", 0), paired(sends[1], "gx", 1)
+    velocity = sweeps(inner, side, first, second)
     return depth, velocity
 
 

time: 88.4 us -> 82.1 us (0.929)
  starting transfers between devices: 29.5 us -> 25.9 us
  waiting for transfers between devices: 41.6 us -> 38.1 us
    ppermute x4, starting transfers between devices: 14.3 us -> 10.7 us  [paired(): return lax.ppermute(value, axis, pairs + [(j, i) for i, j in pairs])]
    ppermute x4, waiting for transfers between devices: 7.23 us -> 3.95 us  [paired(): return lax.ppermute(value, axis, pairs + [(j, i) for i, j in pairs])]
  transfers between devices with their start and end apart: 14 -> 14, of which waited for: 6 -> 6; matrix products, arithmetic and copies ran while one was open for 0% -> 0% of each run, Pallas kernels for 3% -> 4%
where the time goes in v3:
time: 82.1 us; the launch traced here: 80.7 us
  waiting for transfers between devices  38.1 us (46%)
  starting transfers between devices  25.9 us (32%)
  Pallas kernels  14.6 us (18%)
  local copies, waits for them, and re-layouts  1.26 us (2%)
  between operations  0.83 us (1%)
    ppermute x3, waiting for transfers between devices, around_ring(): lax.ppermute(value, axis, [(i, (i + step) % count) for i in range(count)])  18.2 us
    all_to_all x1, waiting for transfers between devices, body(): lax.all_to_all(outgoing, 'gy', split_axis=0, concat_axis=0, tiled=True)  14.4 us
    ppermute x4, starting transfers between devices, paired(): return lax.ppermute(value, axis, pairs + [(j, i) for i, j in pairs])  10.7 us
    all_to_all x1, starting transfers between devices, body(): lax.all_to_all(outgoing, 'gy', split_axis=0, concat_axis=0, tiled=True)  6.92 us
    pallas_call x1, Pallas kernels, sweeps(): pl.pallas_call(sweep_kernel, out_shape=jax.ShapeDtypeStruct((2, CELLS, WI...  5.95 us
    ppermute x3, starting transfers between devices, around_ring(): lax.ppermute(value, axis, [(i, (i + step) % count) for i in range(count)])  4.44 us
    ppermute x4, waiting for transfers between devices, paired(): return lax.ppermute(value, axis, pairs + [(j, i) for i, j in pairs])  3.95 us
    ppermute x6, starting transfers between devices, swapped(): return lax.ppermute(value, axis, [(i, i ^ bit) for i in range(count)])  3.87 us
  transfers between devices with their start and end apart: 14, of which 6 were waited for; matrix products, arithmetic and copies ran while one was open for 0% of the time, Pallas kernels for 4%

profile of v3, /device:TPU:7, one launch (start us, length us, event | category | flops | bytes accessed | tf_op | source)
XLA Modules:
  0.0 80.7 jit_solution(1916061493515287872)
XLA Ops:
  0.6 3.0 %stage_outgoing.1 = f32[16,392,128]{2,1,0:T(8,128)} custom-call(s32[8]{0:T(128)} %bitcast.22, f32[8,384,128]{2,1,0:T(8,128)} %bitcast.21), custom_call_target="tpu_custom_call" | custom-call | tf_op jit(solution)/shard_map/stage_outgoing/pallas_call | solution.py:75
  3.6 6.9 %all-to-all-start = ((f32[16,392,128]{2,1,0:T(8,128)}), f32[16,392,128]{2,1,0:T(8,128)S(1)}, u32[]{:S(2)}, u32[]{:S(2)}) async-start(f32[16,392,128]{2,1,0:T(8,128)} %stage_outgoing.1), calls=%async_computation | async-start | bytes 6422528 | tf_op jit(solution)/shard_map/all_to_all | solution.py:495
  10.6 1.2 %copy-done = f32[2,128,1024]{2,1,0:T(8,128)S(1)} copy-done((f32[2,128,1024]{2,1,0:T(8,128)S(1)}, f32[2,128,1024]{2,1,0:T(8,128)}, u32[]{:S(2)}) %copy-start) | copy-done | bytes 1048600
  11.8 1.5 %keep_own.1 = f32[1536,128]{1,0:T(8,128)S(1)} custom-call(f32[2,128,1024]{2,1,0:T(8,128)S(1)} %copy-done, f32[2,384,128]{2,1,0:T(8,128)} %bitcast.7.coarse), custom_call_target="tpu_custom_call" | custom-call | flops 262144 | bytes 3145728 | tf_op jit(solution)/shard_map/keep_own/pallas_call | solution.py:122
  13.3 1.3 %collective-permute-start = (f32[1536,128]{1,0:T(8,128)S(1)}, f32[1536,128]{1,0:T(8,128)}, u32[]{:S(2)}, u32[]{:S(2)}) collective-permute-start(f32[1536,128]{1,0:T(8,128)S(1)} %keep_own.1), channel_id=1, source_target_pairs={{0,16},{16,0},{32,48},{48,32},{64,80},{80,64},{96,112},{112,96},{1... | collective-permute-start | bytes 2359304 | tf_op jit(solution)/shard_map/ppermute | solution.py:480
  14.6 3.7 %collective-permute-start.2 = (f32[2,384,128]{2,1,0:T(8,128)}, f32[2,384,128]{2,1,0:T(8,128)}, u32[]{:S(2)}, u32[]{:S(2)}) collective-permute-start(f32[2,384,128]{2,1,0:T(8,128)} %bitcast.7.coarse), channel_id=1, source_target_pairs={{0,96},{16,112},{32,0},{48,16},{64,32},{80,48},{96,64},{112,80},{1... | collective-permute-start | bytes 1179656 | tf_op jit(solution)/shard_map/ppermute | solution.py:475
  18.3 0.7 collective-permute-start.4
  19.0 0.9 %collective-permute-start.1 = (f32[1536,128]{1,0:T(8,128)}, f32[1536,128]{1,0:T(8,128)}, u32[]{:S(2)}, u32[]{:S(2)}) collective-permute-start(f32[1536,128]{1,0:T(8,128)} %collective-permute-done), channel_id=1, source_target_pairs={{0,16},{16,0},{32,48},{48,32},{64,80},{80,64},{96,112},{112,96},{1... | collective-permute-start | bytes 2359304 | tf_op jit(solution)/shard_map/ppermute | solution.py:480
  20.0 15.5 %collective-permute-done.2.refs_1_ = f32[2,384,128]{2,1,0:T(8,128)} collective-permute-done((f32[2,384,128]{2,1,0:T(8,128)}, f32[2,384,128]{2,1,0:T(8,128)}, u32[]{:S(2)}, u32[]{:S(2)}) %collective-permute-start.2) | collective-permute-done | bytes 393248 | tf_op jit(solution)/shard_map/ppermute | solution.py:475
  35.5 0.9 %collective-permute-start.6 = (f32[2,384,128]{2,1,0:T(8,128)}, f32[2,384,128]{2,1,0:T(8,128)}, u32[]{:S(2)}, u32[]{:S(2)}) collective-permute-start(f32[2,384,128]{2,1,0:T(8,128)} %collective-permute-done.2.refs_1_), channel_id=1, source_target_pairs={{0,16},{16,0},{32,48},{48,32},{64,80},{80,64},{96,112},{112,96},{1... | collective-permute-start | bytes 1179656 | tf_op jit(solution)/shard_map/ppermute | solution.py:480
  36.4 2.6 %collective-permute-done.4.refs_3_ = f32[2,384,128]{2,1,0:T(8,128)} collective-permute-done((f32[2,384,128]{2,1,0:T(8,128)}, f32[2,384,128]{2,1,0:T(8,128)}, u32[]{:S(2)}, u32[]{:S(2)}) %collective-permute-start.4) | collective-permute-done | bytes 393248 | tf_op jit(solution)/shard_map/ppermute | solution.py:475
  39.0 0.8 collective-permute-start.8
  39.9 1.6 %collective-permute-done.8.refs_7_ = f32[2,384,128]{2,1,0:T(8,128)} collective-permute-done((f32[2,384,128]{2,1,0:T(8,128)}, f32[2,384,128]{2,1,0:T(8,128)}, u32[]{:S(2)}, u32[]{:S(2)}) %collective-permute-start.8) | collective-permute-done | bytes 393248 | tf_op jit(solution)/shard_map/ppermute | solution.py:480
  41.5 14.4 %all-to-all-done.arrived = f32[16,392,128]{2,1,0:T(8,128)S(1)} async-done(((f32[16,392,128]{2,1,0:T(8,128)}), f32[16,392,128]{2,1,0:T(8,128)S(1)}, u32[]{:S(2)}, u32[]{:S(2)}) %all-to-all-start) | async-done | bytes 3211296 | tf_op jit(solution)/shard_map/all_to_all | solution.py:495
  55.9 2.6 %block_outline.1 = (s32[8]{0:T(128)S(1)}, f32[2,384,128]{2,1,0:T(8,128)S(1)}, f32[2,3,8,128]{3,2,1,0:T(8,128)S(1)}, f32[2,3,8,8,128]{4,3,2,1,0:T(8,128)S(1)}) custom-call(s32[8]{0:T(128)S(1)} %bitcast.18, s32[8]{0:T(128)S(1)} %bitcast.20, s32[1]{0:T(128)S(6)} %add.3.owner, f32[16,392,128]{2,1,0:T(8,128)S(1)} %all-to-all-done.arrived, ...), custom_call_target="tpu_custom_call" | custom-call | tf_op jit(solution)/shard_map/block_outline/pallas_call | solution.py:259
  58.4 0.1 collective-permute-start.9
  58.5 4.2 %collective-permute-start.10 = (f32[3,8,128]{2,1,0:T(8,128)S(1)}, f32[3,8,128]{2,1,0:T(8,128)S(1)}, u32[]{:S(2)}, u32[]{:S(2)}) collective-permute-start(f32[3,8,128]{2,1,0:T(8,128)S(1)} %get-tuple-element.20), channel_id=1, source_target_pairs={{1,2},{3,4},{5,6},{7,8},{9,10},{11,12},{13,14},{2,1},{4,3},{6,5},{... | collective-permute-start | bytes 36872 | tf_op jit(solution)/shard_map/ppermute | solution.py:470
  62.8 2.3 %collective-permute-done.10.second = f32[3,8,128]{2,1,0:T(8,128)S(1)} collective-permute-done((f32[3,8,128]{2,1,0:T(8,128)S(1)}, f32[3,8,128]{2,1,0:T(8,128)S(1)}, u32[]{:S(2)}, u32[]{:S(2)}) %collective-permute-start.10) | collective-permute-done | bytes 12320 | tf_op jit(solution)/shard_map/ppermute | solution.py:470
  65.1 0.1 edge_rows.1
  65.2 3.5 %collective-permute-start.11 = (f32[3,8,1152]{2,1,0:T(8,128)S(1)}, f32[3,8,1152]{2,1,0:T(8,128)S(1)}, u32[]{:S(2)}, u32[]{:S(2)}) collective-permute-start(f32[3,8,1152]{2,1,0:T(8,128)S(1)} %get-tuple-element.19), channel_id=1, source_target_pairs={{0,16},{32,48},{64,80},{96,112},{16,0},{48,32},{80,64},{112,96},{1... | collective-permute-start | bytes 331784 | tf_op jit(solution)/shard_map/ppermute | solution.py:470
  68.7 2.9 %collective-permute-start.12 = (f32[3,8,1152]{2,1,0:T(8,128)S(1)}, f32[3,8,1152]{2,1,0:T(8,128)S(1)}, u32[]{:S(2)}, u32[]{:S(2)}) collective-permute-start(f32[3,8,1152]{2,1,0:T(8,128)S(1)} %get-tuple-element.18), channel_id=1, source_target_pairs={{16,32},{48,64},{80,96},{32,16},{64,48},{96,80},{17,33},{49,65},{8... | collective-permute-start | bytes 331784 | tf_op jit(solution)/shard_map/ppermute | solution.py:470
  71.6 1.5 %block_interior.1 = (f32[128,1024]{1,0:T(8,128)}, f32[3,8,144,128]{3,2,1,0:T(8,128)S(1)}) custom-call(s32[8]{0:T(128)S(1)} %get-tuple-element.10.source, f32[16,392,128]{2,1,0:T(8,128)S(1)} %all-to-all-done.arrived, f32[2,384,128]{2,1,0:T(8,128)S(1)} %get-tuple-element.11.fresh, f32[2,128,1024]{2,1,0:T(8,128)S(1)} %copy-done.1), custom_call_target="tpu_custom_call" | custom-call | flops 1048576 | bytes 6291456 | tf_op jit(solution)/shard_map/block_interior/pallas_call | solution.py:312
  73.2 1.6 %collective-permute-done.12.second = f32[3,8,1152]{2,1,0:T(8,128)S(1)} collective-permute-done((f32[3,8,1152]{2,1,0:T(8,128)S(1)}, f32[3,8,1152]{2,1,0:T(8,128)S(1)}, u32[]{:S(2)}, u32[]{:S(2)}) %collective-permute-start.12) | collective-permute-done | bytes 110624 | tf_op jit(solution)/shard_map/ppermute | solution.py:470
  74.8 5.9 %jacobi_sweeps.1 = f32[2,128,1024]{2,1,0:T(8,128)} custom-call(f32[3,8,144,128]{3,2,1,0:T(8,128)S(1)} %get-tuple-element.13.inner, f32[3,144,128]{2,1,0:T(8,128)S(1)} %get-tuple-element.16.side, f32[3,8,1152]{2,1,0:T(8,128)S(1)} %collective-permute-done.11.first, f32[3,8,1152]{2,1,0:T(8,128)S(1)} %collective-permute-done.12.second), custom_call_target="tpu_custom_call" | custom-call | tf_op jit(solution)/shard_map/jacobi_sweeps/pallas_call | solution.py:448
  (20 shorter events, 0.1 us)
Async XLA Ops:
  3.6 36.2 %copy-start.3 = (s32[1,8]{1,0:T(1,128)S(1)}, s32[1,8]{1,0:T(1,128)}, u32[]{:S(2)}) copy-start(s32[1,8]{1,0:T(1,128)} %param.9) | copy-start | bytes 100
  3.6 52.2 %copy-start.2 = (s32[1,8]{1,0:T(1,128)S(1)}, s32[1,8]{1,0:T(1,128)}, u32[]{:S(2)}) copy-start(s32[1,8]{1,0:T(1,128)} %param.8) | copy-start | bytes 100
  3.6 52.2 %all-to-all-start = ((f32[16,392,128]{2,1,0:T(8,128)}), f32[16,392,128]{2,1,0:T(8,128)S(1)}, u32[]{:S(2)}, u32[]{:S(2)}) async-start(f32[16,392,128]{2,1,0:T(8,128)} %stage_outgoing.1), calls=%async_computation | async-start | bytes 6422528 | tf_op jit(solution)/shard_map/all_to_all | solution.py:495
  10.6 1.2 %copy-start = (f32[2,128,1024]{2,1,0:T(8,128)S(1)}, f32[2,128,1024]{2,1,0:T(8,128)}, u32[]{:S(2)}) copy-start(f32[2,128,1024]{2,1,0:T(8,128)} %force.3) | copy-start | bytes 3145732
  13.3 5.8 %collective-permute-start = (f32[1536,128]{1,0:T(8,128)S(1)}, f32[1536,128]{1,0:T(8,128)}, u32[]{:S(2)}, u32[]{:S(2)}) collective-permute-start(f32[1536,128]{1,0:T(8,128)S(1)} %keep_own.1), channel_id=1, source_target_pairs={{0,16},{16,0},{32,48},{48,32},{64,80},{80,64},{96,112},{112,96},{1... | collective-permute-start | bytes 2359304 | tf_op jit(solution)/shard_map/ppermute | solution.py:480
  14.6 20.9 %collective-permute-start.2 = (f32[2,384,128]{2,1,0:T(8,128)}, f32[2,384,128]{2,1,0:T(8,128)}, u32[]{:S(2)}, u32[]{:S(2)}) collective-permute-start(f32[2,384,128]{2,1,0:T(8,128)} %bitcast.7.coarse), channel_id=1, source_target_pairs={{0,96},{16,112},{32,0},{48,16},{64,32},{80,48},{96,64},{112,80},{1... | collective-permute-start | bytes 1179656 | tf_op jit(solution)/shard_map/ppermute | solution.py:475
  18.3 18.1 %collective-permute-start.3 = (f32[2,384,128]{2,1,0:T(8,128)}, f32[2,384,128]{2,1,0:T(8,128)}, u32[]{:S(2)}, u32[]{:S(2)}) collective-permute-start(f32[2,384,128]{2,1,0:T(8,128)} %bitcast.7.coarse), channel_id=1, source_target_pairs={{0,64},{16,80},{32,96},{48,112},{64,0},{80,16},{96,32},{112,48},{1... | collective-permute-start | bytes 1179656 | tf_op jit(solution)/shard_map/ppermute | solution.py:475
  18.3 20.7 %collective-permute-start.4 = (f32[2,384,128]{2,1,0:T(8,128)}, f32[2,384,128]{2,1,0:T(8,128)}, u32[]{:S(2)}, u32[]{:S(2)}) collective-permute-start(f32[2,384,128]{2,1,0:T(8,128)} %bitcast.7.coarse), channel_id=1, source_target_pairs={{0,32},{16,48},{32,64},{48,80},{64,96},{80,112},{96,0},{112,16},{1... | collective-permute-start | bytes 1179656 | tf_op jit(solution)/shard_map/ppermute | solution.py:475
  19.0 22.4 %collective-permute-start.1 = (f32[1536,128]{1,0:T(8,128)}, f32[1536,128]{1,0:T(8,128)}, u32[]{:S(2)}, u32[]{:S(2)}) collective-permute-start(f32[1536,128]{1,0:T(8,128)} %collective-permute-done), channel_id=1, source_target_pairs={{0,16},{16,0},{32,48},{48,32},{64,80},{80,64},{96,112},{112,96},{1... | collective-permute-start | bytes 2359304 | tf_op jit(solution)/shard_map/ppermute | solution.py:480
  20.0 19.9 %collective-permute-start.5 = (f32[2,384,128]{2,1,0:T(8,128)}, f32[2,384,128]{2,1,0:T(8,128)}, u32[]{:S(2)}, u32[]{:S(2)}) collective-permute-start(f32[2,384,128]{2,1,0:T(8,128)} %bitcast.7.coarse), channel_id=1, source_target_pairs={{0,16},{16,0},{32,48},{48,32},{64,80},{80,64},{96,112},{112,96},{1... | collective-permute-start | bytes 1179656 | tf_op jit(solution)/shard_map/ppermute | solution.py:480
  35.5 4.3 %collective-permute-start.6 = (f32[2,384,128]{2,1,0:T(8,128)}, f32[2,384,128]{2,1,0:T(8,128)}, u32[]{:S(2)}, u32[]{:S(2)}) collective-permute-start(f32[2,384,128]{2,1,0:T(8,128)} %collective-permute-done.2.refs_1_), channel_id=1, source_target_pairs={{0,16},{16,0},{32,48},{48,32},{64,80},{80,64},{96,112},{112,96},{1... | collective-permute-start | bytes 1179656 | tf_op jit(solution)/shard_map/ppermute | solution.py:480
  36.4 3.5 %collective-permute-start.7 = (f32[2,384,128]{2,1,0:T(8,128)}, f32[2,384,128]{2,1,0:T(8,128)}, u32[]{:S(2)}, u32[]{:S(2)}) collective-permute-start(f32[2,384,128]{2,1,0:T(8,128)} %collective-permute-done.3.refs_2_), channel_id=1, source_target_pairs={{0,16},{16,0},{32,48},{48,32},{64,80},{80,64},{96,112},{112,96},{1... | collective-permute-start | bytes 1179656 | tf_op jit(solution)/shard_map/ppermute | solution.py:480
  39.0 2.4 %collective-permute-start.8 = (f32[2,384,128]{2,1,0:T(8,128)}, f32[2,384,128]{2,1,0:T(8,128)}, u32[]{:S(2)}, u32[]{:S(2)}) collective-permute-start(f32[2,384,128]{2,1,0:T(8,128)} %collective-permute-done.4.refs_3_), channel_id=1, source_target_pairs={{0,16},{16,0},{32,48},{48,32},{64,80},{80,64},{96,112},{112,96},{1... | collective-permute-start | bytes 1179656 | tf_op jit(solution)/shard_map/ppermute | solution.py:480
  55.9 15.8 %copy-start.1 = (f32[2,128,1024]{2,1,0:T(8,128)S(1)}, f32[2,128,1024]{2,1,0:T(8,128)}, u32[]{:S(2)}) copy-start(f32[2,128,1024]{2,1,0:T(8,128)} %force.3) | copy-start | bytes 3145732
  58.4 4.3 %collective-permute-start.9 = (f32[3,8,128]{2,1,0:T(8,128)S(1)}, f32[3,8,128]{2,1,0:T(8,128)S(1)}, u32[]{:S(2)}, u32[]{:S(2)}) collective-permute-start(f32[3,8,128]{2,1,0:T(8,128)S(1)} %get-tuple-element.21), channel_id=1, source_target_pairs={{0,1},{2,3},{4,5},{6,7},{8,9},{10,11},{12,13},{14,15},{1,0},{3,2},... | collective-permute-start | bytes 36872 | tf_op jit(solution)/shard_map/ppermute | solution.py:470
  58.5 6.5 %collective-permute-start.10 = (f32[3,8,128]{2,1,0:T(8,128)S(1)}, f32[3,8,128]{2,1,0:T(8,128)S(1)}, u32[]{:S(2)}, u32[]{:S(2)}) collective-permute-start(f32[3,8,128]{2,1,0:T(8,128)S(1)} %get-tuple-element.20), channel_id=1, source_target_pairs={{1,2},{3,4},{5,6},{7,8},{9,10},{11,12},{13,14},{2,1},{4,3},{6,5},{... | collective-permute-start | bytes 36872 | tf_op jit(solution)/shard_map/ppermute | solution.py:470
  65.2 7.9 %collective-permute-start.11 = (f32[3,8,1152]{2,1,0:T(8,128)S(1)}, f32[3,8,1152]{2,1,0:T(8,128)S(1)}, u32[]{:S(2)}, u32[]{:S(2)}) collective-permute-start(f32[3,8,1152]{2,1,0:T(8,128)S(1)} %get-tuple-element.19), channel_id=1, source_target_pairs={{0,16},{32,48},{64,80},{96,112},{16,0},{48,32},{80,64},{112,96},{1... | collective-permute-start | bytes 331784 | tf_op jit(solution)/shard_map/ppermute | solution.py:470
  68.7 6.1 %collective-permute-start.12 = (f32[3,8,1152]{2,1,0:T(8,128)S(1)}, f32[3,8,1152]{2,1,0:T(8,128)S(1)}, u32[]{:S(2)}, u32[]{:S(2)}) collective-permute-start(f32[3,8,1152]{2,1,0:T(8,128)S(1)} %get-tuple-element.18), channel_id=1, source_target_pairs={{16,32},{48,64},{80,96},{32,16},{64,48},{96,80},{17,33},{49,65},{8... | collective-permute-start | bytes 331784 | tf_op jit(solution)/shard_map/ppermute | solution.py:470

commit v4 on v3

--- a/solution.py
+++ b/solution.py
@@ -36,6 +36,15 @@
     return pltpu.CompilerParams(vmem_limit_bytes=mib * MIB)
 
 
+ORDER = (0, 1, 3, 2, 10, 11, 9, 8, 4, 5, 7, 6, 14, 15, 13, 12)
+
+
+def chunk_of(device):
+    high, low = device >> 2, device & 3
+    high = ((high & 1) << 1) | (high >> 1)
+    return (high << 2) | ((low ^ (low >> 1)) ^ ((high & 1) * 3))
+
+
 def stage_kernel(dest, old, out, patch_v, note_v, in_sems, out_sems, note_sem):
     for slot in range(SLOTS):
         pltpu.make_async_copy(old.at[slot], patch_v.at[slot], in_sems.at[slot]).start()
@@ -46,13 +55,13 @@
         @pl.when(target >= 0)
         def _(target=target):
             where = lax.convert_element_type(target & (SLOTS - 1), jnp.float32)
-            note_v[target >> 3] = jnp.full((HALO, CELLS), where, jnp.float32)
+            note_v[chunk_of(target >> 3)] = jnp.full((HALO, CELLS), where, jnp.float32)
 
     notes = pltpu.make_async_copy(note_v, out.at[:, pl.ds(PATCH_ROWS, HALO)], note_sem)
     notes.start()
 
     def send(slot):
-        rows = out.at[dest[slot] >> 3, pl.ds(0, PATCH_ROWS)]
+        rows = out.at[chunk_of(dest[slot] >> 3), pl.ds(0, PATCH_ROWS)]
         return pltpu.make_async_copy(patch_v.at[slot], rows, out_sems.at[slot])
 
     for slot in range(SLOTS):
@@ -206,23 +215,25 @@
         def _(slot=slot, peer=peer):
             source[slot] = peer
 
-    def refined(number, _):
-        @pl.when(picks[number] >= 0)
-        def _():
-            for field in range(FIELDS):
-                quarter(pieces[0], number, field).wait()
-            along_rows = spread(0, 0)[:, : CELLS // 2]
-            along_cols = spread(code[picks[number]] & 1, 1)
-            for field in range(FIELDS):
-                high, low = split_two(parent_v[number, field])
-                done = dot(along_rows, high) + dot(along_rows, low)
-                high, low = split_two(done)
-                at = slice(field * CELLS, (field + 1) * CELLS)
-                fresh[number, at] = dot(high, along_cols) + dot(low, along_cols)
-
-        return 0
-
-    lax.fori_loop(0, REFINED, refined, 0)
+    along_rows = jnp.concatenate([spread(0, 0)[:, : CELLS // 2]] * 2, axis=1)
+    either = [jnp.concatenate([spread(side, 1)] * 2, axis=0) for side in range(2)]
+    @pl.when(picks[0] >= 0)
+    def _():
+        for number in range(REFINED):
+
+            @pl.when(picks[number] >= 0)
+            def _(number=number):
+                for field in range(FIELDS):
+                    quarter(pieces[0], number, field).wait()
+
+        for number in range(REFINED):
+            side = code[jnp.maximum(picks[number], 0)] & 1
+            along_cols = jnp.where(side > 0, either[1], either[0])
+            parent = jnp.concatenate([parent_v[number, field] for field in range(FIELDS)], axis=1)
+            done = dot(along_rows, jnp.concatenate(split_two(parent), axis=0))
+            fields = [done[:, field * CELLS : (field + 1) * CELLS] for field in range(FIELDS)]
+            done = jnp.concatenate(fields, axis=0)
+            fresh[number] = dot(jnp.concatenate(split_two(done), axis=1), along_cols)
 
     def taken(slot, first, size):
         origin = source[slot]
@@ -402,24 +413,34 @@
         diagonal = here + weights[0] + weights[1] + weights[2] + weights[3]
         inside = here > 0.0
         scale = jnp.where(inside, OMEGA / jnp.where(inside, diagonal, 1.0), 0.0)
-        for number, w in enumerate(weights):
-            faces[number, t] = w * scale
+        faces[0, t] = weights[1]
+        faces[1, t] = weights[3]
+        faces[2, t] = scale
         for field in range(2):
             start = spaced(field + 1, t) * scale
             right[field, t] = start
             velo[0, field, t] = start
 
-    def relaxed(now, field, t, here, others):
-        total = right[field, t] + (1.0 - OMEGA) * here
-        for number, other in enumerate(others):
-            total = total + faces[number, t] * other
-        return total
+    def relaxed(now, field):
+        u = velo.at[now, field]
+        last = faces[0, TILES - 1] * u[TILES - 1]
+        above_flux = pltpu.roll(last, 1, 0)
+        here = u[0]
+        for t in range(TILES):
+            after = u[t + 1] if t < TILES - 1 else pltpu.roll(u[0], 7, 0)
+            south, east = faces[0, t], faces[1, t]
+            flux = above_flux + south * after
+            flux = flux + east * pltpu.roll(here, EXT_COLS - 1, 1)
+            flux = flux + pltpu.roll(east * here, 1, 1)
+            yield t, right[field, t] + (1.0 - OMEGA) * here + faces[2, t] * flux
+            above_flux = south * here
+            here = after
 
     def step(s, _):
         now = s & 1
         for field in range(2):
-            for t, here, others in each_tile(lambda t: velo[now, field, t]):
-                velo[1 - now, field, t] = relaxed(now, field, t, here, others)
+            for t, total in relaxed(now, field):
+                velo[1 - now, field, t] = total
         return 0
 
     lax.fori_loop(0, SWEEPS - 2, step, 0)
@@ -431,8 +452,7 @@
 
     now = (SWEEPS - 2) % 2
     for field in range(2):
-        for t, here, others in each_tile(lambda t: velo[now, field, t]):
-            done = relaxed(now, field, t, here, others)
+        for t, done in relaxed(now, field):
             for block in range(SLOTS):
                 done_v[field, block, rows_of(t), :] = done[:, block * CELLS : (block + 1) * CELLS]
         for block in range(SLOTS):
@@ -454,7 +474,7 @@
             pltpu.VMEM((2, SLOTS, EXT_ROWS, CELLS), f32),
             pltpu.VMEM((2,) + tiles, f32),
             pltpu.VMEM((2, 2) + tiles, f32),
-            pltpu.VMEM((4,) + tiles, f32),
+            pltpu.VMEM((3,) + tiles, f32),
             pltpu.VMEM((FIELDS, HALO, EXT_COLS), f32),
             pltpu.VMEM((FIELDS, HALO, EXT_COLS), f32),
             pltpu.SemaphoreType.DMA((2, SLOTS)),
@@ -492,7 +512,9 @@
 
 def body(old_state, old_dest, refine, parent_block, coarse_state, force):
     outgoing = stage(old_dest[0], old_state.reshape(SLOTS, PATCH_ROWS, CELLS))
-    arrived = lax.all_to_all(outgoing, "gy", split_axis=0, concat_axis=0, tiled=True)
+    arrived = lax.all_to_all(
+        outgoing, "gy", split_axis=0, concat_axis=0, tiled=True, axis_index_groups=[list(ORDER)]
+    )
     coarse = coarse_state.reshape(2, PATCH_ROWS, CELLS)
     kept = swapped(swapped(keep(force, coarse), "gx", 1), "gx", 1)
     pieces = [kept.reshape(KEPT, PATCH_ROWS, CELLS)] + column_pieces(coarse)[1:]

time: 82.1 us -> 76.8 us (0.935); the launches traced: 80.7 us -> 76.7 us
  waiting for transfers between devices: 38.1 us -> 34 us
    all_to_all x1, waiting for transfers between devices: 14.4 us -> 8.34 us  [body(): lax.all_to_all(outgoing, 'gy', split_axis=0, concat_axis=0, tiled=True, a...]
    ppermute x4, waiting for transfers between devices: 3.95 us -> 5.81 us  [paired(): return lax.ppermute(value, axis, pairs + [(j, i) for i, j in pairs])]
where the time goes in v4:
time: 76.8 us; the launch traced here: 76.7 us
  waiting for transfers between devices  34 us (44%)
  starting transfers between devices  26 us (34%)
  Pallas kernels  14.6 us (19%)
  local copies, waits for them, and re-layouts  1.26 us (2%)
  between operations  0.83 us (1%)
    ppermute x3, waiting for transfers between devices, around_ring(): lax.ppermute(value, axis, [(i, (i + step) % count) for i in range(count)])  18.3 us
    ppermute x4, starting transfers between devices, paired(): return lax.ppermute(value, axis, pairs + [(j, i) for i, j in pairs])  10.9 us
    all_to_all x1, waiting for transfers between devices, body(): lax.all_to_all(outgoing, 'gy', split_axis=0, concat_axis=0, tiled=True, a...  8.34 us
    all_to_all x1, starting transfers between devices, body(): lax.all_to_all(outgoing, 'gy', split_axis=0, concat_axis=0, tiled=True, a...  6.87 us
    ppermute x4, waiting for transfers between devices, paired(): return lax.ppermute(value, axis, pairs + [(j, i) for i, j in pairs])  5.81 us
    pallas_call x1, Pallas kernels, sweeps(): pl.pallas_call(sweep_kernel, out_shape=jax.ShapeDtypeStruct((2, CELLS, WI...  5.67 us
    ppermute x3, starting transfers between devices, around_ring(): lax.ppermute(value, axis, [(i, (i + step) % count) for i in range(count)])  4.52 us
    ppermute x6, starting transfers between devices, swapped(): return lax.ppermute(value, axis, [(i, i ^ bit) for i in range(count)])  3.76 us
  transfers between devices with their start and end apart: 14, of which 6 were waited for; matrix products, arithmetic and copies ran while one was open for 0% of the time, Pallas kernels for 4%

profile of v4, /device:TPU:7, one launch (start us, length us, event | category | flops | bytes accessed | tf_op | source)
XLA Modules:
  0.0 76.7 jit_solution(16107123426592442119)
XLA Ops:
  0.6 3.0 %stage_outgoing.1 = f32[16,392,128]{2,1,0:T(8,128)} custom-call(s32[8]{0:T(128)} %bitcast.22, f32[8,384,128]{2,1,0:T(8,128)} %bitcast.21), custom_call_target="tpu_custom_call" | custom-call | tf_op jit(solution)/shard_map/stage_outgoing/pallas_call | solution.py:84
  3.7 6.9 %all-to-all-start = ((f32[16,392,128]{2,1,0:T(8,128)}), f32[16,392,128]{2,1,0:T(8,128)S(1)}, u32[]{:S(2)}, u32[]{:S(2)}) async-start(f32[16,392,128]{2,1,0:T(8,128)} %stage_outgoing.1), calls=%async_computation | async-start | bytes 6422528 | tf_op jit(solution)/shard_map/all_to_all | solution.py:515
  10.6 1.2 %copy-done = f32[2,128,1024]{2,1,0:T(8,128)S(1)} copy-done((f32[2,128,1024]{2,1,0:T(8,128)S(1)}, f32[2,128,1024]{2,1,0:T(8,128)}, u32[]{:S(2)}) %copy-start) | copy-done | bytes 1048600
  11.8 1.5 %keep_own.1 = f32[1536,128]{1,0:T(8,128)S(1)} custom-call(f32[2,128,1024]{2,1,0:T(8,128)S(1)} %copy-done, f32[2,384,128]{2,1,0:T(8,128)} %bitcast.7.coarse), custom_call_target="tpu_custom_call" | custom-call | flops 262144 | bytes 3145728 | tf_op jit(solution)/shard_map/keep_own/pallas_call | solution.py:131
  13.3 1.2 %collective-permute-start = (f32[1536,128]{1,0:T(8,128)S(1)}, f32[1536,128]{1,0:T(8,128)}, u32[]{:S(2)}, u32[]{:S(2)}) collective-permute-start(f32[1536,128]{1,0:T(8,128)S(1)} %keep_own.1), channel_id=1, source_target_pairs={{0,16},{16,0},{32,48},{48,32},{64,80},{80,64},{96,112},{112,96},{1... | collective-permute-start | bytes 2359304 | tf_op jit(solution)/shard_map/ppermute | solution.py:500
  14.5 3.8 %collective-permute-start.2 = (f32[2,384,128]{2,1,0:T(8,128)}, f32[2,384,128]{2,1,0:T(8,128)}, u32[]{:S(2)}, u32[]{:S(2)}) collective-permute-start(f32[2,384,128]{2,1,0:T(8,128)} %bitcast.7.coarse), channel_id=1, source_target_pairs={{0,96},{16,112},{32,0},{48,16},{64,32},{80,48},{96,64},{112,80},{1... | collective-permute-start | bytes 1179656 | tf_op jit(solution)/shard_map/ppermute | solution.py:495
  18.3 0.7 collective-permute-start.4
  19.0 0.9 %collective-permute-start.1 = (f32[1536,128]{1,0:T(8,128)}, f32[1536,128]{1,0:T(8,128)}, u32[]{:S(2)}, u32[]{:S(2)}) collective-permute-start(f32[1536,128]{1,0:T(8,128)} %collective-permute-done), channel_id=1, source_target_pairs={{0,16},{16,0},{32,48},{48,32},{64,80},{80,64},{96,112},{112,96},{1... | collective-permute-start | bytes 2359304 | tf_op jit(solution)/shard_map/ppermute | solution.py:500
  19.9 15.6 %collective-permute-done.2.refs_1_ = f32[2,384,128]{2,1,0:T(8,128)} collective-permute-done((f32[2,384,128]{2,1,0:T(8,128)}, f32[2,384,128]{2,1,0:T(8,128)}, u32[]{:S(2)}, u32[]{:S(2)}) %collective-permute-start.2) | collective-permute-done | bytes 393248 | tf_op jit(solution)/shard_map/ppermute | solution.py:495
  35.5 0.9 %collective-permute-start.6 = (f32[2,384,128]{2,1,0:T(8,128)}, f32[2,384,128]{2,1,0:T(8,128)}, u32[]{:S(2)}, u32[]{:S(2)}) collective-permute-start(f32[2,384,128]{2,1,0:T(8,128)} %collective-permute-done.2.refs_1_), channel_id=1, source_target_pairs={{0,16},{16,0},{32,48},{48,32},{64,80},{80,64},{96,112},{112,96},{1... | collective-permute-start | bytes 1179656 | tf_op jit(solution)/shard_map/ppermute | solution.py:500
  36.4 2.6 %collective-permute-done.4.refs_3_ = f32[2,384,128]{2,1,0:T(8,128)} collective-permute-done((f32[2,384,128]{2,1,0:T(8,128)}, f32[2,384,128]{2,1,0:T(8,128)}, u32[]{:S(2)}, u32[]{:S(2)}) %collective-permute-start.4) | collective-permute-done | bytes 393248 | tf_op jit(solution)/shard_map/ppermute | solution.py:495
  39.0 0.8 collective-permute-start.8
  39.9 1.6 %collective-permute-done.8.refs_7_ = f32[2,384,128]{2,1,0:T(8,128)} collective-permute-done((f32[2,384,128]{2,1,0:T(8,128)}, f32[2,384,128]{2,1,0:T(8,128)}, u32[]{:S(2)}, u32[]{:S(2)}) %collective-permute-start.8) | collective-permute-done | bytes 393248 | tf_op jit(solution)/shard_map/ppermute | solution.py:500
  41.5 8.3 %all-to-all-done.arrived = f32[16,392,128]{2,1,0:T(8,128)S(1)} async-done(((f32[16,392,128]{2,1,0:T(8,128)}), f32[16,392,128]{2,1,0:T(8,128)S(1)}, u32[]{:S(2)}, u32[]{:S(2)}) %all-to-all-start) | async-done | bytes 3211296 | tf_op jit(solution)/shard_map/all_to_all | solution.py:515
  49.8 2.8 %block_outline.1 = (s32[8]{0:T(128)S(1)}, f32[2,384,128]{2,1,0:T(8,128)S(1)}, f32[2,3,8,128]{3,2,1,0:T(8,128)S(1)}, f32[2,3,8,8,128]{4,3,2,1,0:T(8,128)S(1)}) custom-call(s32[8]{0:T(128)S(1)} %bitcast.18, s32[8]{0:T(128)S(1)} %bitcast.20, s32[1]{0:T(128)S(6)} %add.3.owner, f32[16,392,128]{2,1,0:T(8,128)S(1)} %all-to-all-done.arrived, ...), custom_call_target="tpu_custom_call" | custom-call | tf_op jit(solution)/shard_map/block_outline/pallas_call | solution.py:270
  52.7 1.8 %collective-permute-start.9 = (f32[3,8,128]{2,1,0:T(8,128)S(1)}, f32[3,8,128]{2,1,0:T(8,128)S(1)}, u32[]{:S(2)}, u32[]{:S(2)}) collective-permute-start(f32[3,8,128]{2,1,0:T(8,128)S(1)} %get-tuple-element.21), channel_id=1, source_target_pairs={{0,1},{2,3},{4,5},{6,7},{8,9},{10,11},{12,13},{14,15},{1,0},{3,2},... | collective-permute-start | bytes 36872 | tf_op jit(solution)/shard_map/ppermute | solution.py:490
  54.5 2.1 %collective-permute-start.10 = (f32[3,8,128]{2,1,0:T(8,128)S(1)}, f32[3,8,128]{2,1,0:T(8,128)S(1)}, u32[]{:S(2)}, u32[]{:S(2)}) collective-permute-start(f32[3,8,128]{2,1,0:T(8,128)S(1)} %get-tuple-element.20), channel_id=1, source_target_pairs={{1,2},{3,4},{5,6},{7,8},{9,10},{11,12},{13,14},{2,1},{4,3},{6,5},{... | collective-permute-start | bytes 36872 | tf_op jit(solution)/shard_map/ppermute | solution.py:490
  56.5 4.4 %collective-permute-done.10.second = f32[3,8,128]{2,1,0:T(8,128)S(1)} collective-permute-done((f32[3,8,128]{2,1,0:T(8,128)S(1)}, f32[3,8,128]{2,1,0:T(8,128)S(1)}, u32[]{:S(2)}, u32[]{:S(2)}) %collective-permute-start.10) | collective-permute-done | bytes 12320 | tf_op jit(solution)/shard_map/ppermute | solution.py:490
  61.0 0.1 edge_rows.1
  61.2 3.8 %collective-permute-start.11 = (f32[3,8,1152]{2,1,0:T(8,128)S(1)}, f32[3,8,1152]{2,1,0:T(8,128)S(1)}, u32[]{:S(2)}, u32[]{:S(2)}) collective-permute-start(f32[3,8,1152]{2,1,0:T(8,128)S(1)} %get-tuple-element.19), channel_id=1, source_target_pairs={{0,16},{32,48},{64,80},{96,112},{16,0},{48,32},{80,64},{112,96},{1... | collective-permute-start | bytes 331784 | tf_op jit(solution)/shard_map/ppermute | solution.py:490
  65.0 3.2 %collective-permute-start.12 = (f32[3,8,1152]{2,1,0:T(8,128)S(1)}, f32[3,8,1152]{2,1,0:T(8,128)S(1)}, u32[]{:S(2)}, u32[]{:S(2)}) collective-permute-start(f32[3,8,1152]{2,1,0:T(8,128)S(1)} %get-tuple-element.18), channel_id=1, source_target_pairs={{16,32},{48,64},{80,96},{32,16},{64,48},{96,80},{17,33},{49,65},{8... | collective-permute-start | bytes 331784 | tf_op jit(solution)/shard_map/ppermute | solution.py:490
  68.2 1.5 %block_interior.1 = (f32[128,1024]{1,0:T(8,128)}, f32[3,8,144,128]{3,2,1,0:T(8,128)S(1)}) custom-call(s32[8]{0:T(128)S(1)} %get-tuple-element.10.source, f32[16,392,128]{2,1,0:T(8,128)S(1)} %all-to-all-done.arrived, f32[2,384,128]{2,1,0:T(8,128)S(1)} %get-tuple-element.11.fresh, f32[2,128,1024]{2,1,0:T(8,128)S(1)} %copy-done.1), custom_call_target="tpu_custom_call" | custom-call | flops 1048576 | bytes 6291456 | tf_op jit(solution)/shard_map/block_interior/pallas_call | solution.py:323
  69.7 1.4 %collective-permute-done.12.second = f32[3,8,1152]{2,1,0:T(8,128)S(1)} collective-permute-done((f32[3,8,1152]{2,1,0:T(8,128)S(1)}, f32[3,8,1152]{2,1,0:T(8,128)S(1)}, u32[]{:S(2)}, u32[]{:S(2)}) %collective-permute-start.12) | collective-permute-done | bytes 110624 | tf_op jit(solution)/shard_map/ppermute | solution.py:490
  71.0 5.7 %jacobi_sweeps.1 = f32[2,128,1024]{2,1,0:T(8,128)} custom-call(f32[3,8,144,128]{3,2,1,0:T(8,128)S(1)} %get-tuple-element.13.inner, f32[3,144,128]{2,1,0:T(8,128)S(1)} %get-tuple-element.16.side, f32[3,8,1152]{2,1,0:T(8,128)S(1)} %collective-permute-done.11.first, f32[3,8,1152]{2,1,0:T(8,128)S(1)} %collective-permute-done.12.second), custom_call_target="tpu_custom_call" | custom-call | tf_op jit(solution)/shard_map/jacobi_sweeps/pallas_call | solution.py:468
  (20 shorter events, 0.1 us)
Async XLA Ops:
  3.7 36.1 %copy-start.3 = (s32[1,8]{1,0:T(1,128)S(1)}, s32[1,8]{1,0:T(1,128)}, u32[]{:S(2)}) copy-start(s32[1,8]{1,0:T(1,128)} %param.9) | copy-start | bytes 100
  3.7 46.2 %copy-start.2 = (s32[1,8]{1,0:T(1,128)S(1)}, s32[1,8]{1,0:T(1,128)}, u32[]{:S(2)}) copy-start(s32[1,8]{1,0:T(1,128)} %param.8) | copy-start | bytes 100
  3.7 46.2 %all-to-all-start = ((f32[16,392,128]{2,1,0:T(8,128)}), f32[16,392,128]{2,1,0:T(8,128)S(1)}, u32[]{:S(2)}, u32[]{:S(2)}) async-start(f32[16,392,128]{2,1,0:T(8,128)} %stage_outgoing.1), calls=%async_computation | async-start | bytes 6422528 | tf_op jit(solution)/shard_map/all_to_all | solution.py:515
  10.6 1.2 %copy-start = (f32[2,128,1024]{2,1,0:T(8,128)S(1)}, f32[2,128,1024]{2,1,0:T(8,128)}, u32[]{:S(2)}) copy-start(f32[2,128,1024]{2,1,0:T(8,128)} %force.3) | copy-start | bytes 3145732
  13.3 5.7 %collective-permute-start = (f32[1536,128]{1,0:T(8,128)S(1)}, f32[1536,128]{1,0:T(8,128)}, u32[]{:S(2)}, u32[]{:S(2)}) collective-permute-start(f32[1536,128]{1,0:T(8,128)S(1)} %keep_own.1), channel_id=1, source_target_pairs={{0,16},{16,0},{32,48},{48,32},{64,80},{80,64},{96,112},{112,96},{1... | collective-permute-start | bytes 2359304 | tf_op jit(solution)/shard_map/ppermute | solution.py:500
  14.5 21.0 %collective-permute-start.2 = (f32[2,384,128]{2,1,0:T(8,128)}, f32[2,384,128]{2,1,0:T(8,128)}, u32[]{:S(2)}, u32[]{:S(2)}) collective-permute-start(f32[2,384,128]{2,1,0:T(8,128)} %bitcast.7.coarse), channel_id=1, source_target_pairs={{0,96},{16,112},{32,0},{48,16},{64,32},{80,48},{96,64},{112,80},{1... | collective-permute-start | bytes 1179656 | tf_op jit(solution)/shard_map/ppermute | solution.py:495
  18.3 18.1 %collective-permute-start.3 = (f32[2,384,128]{2,1,0:T(8,128)}, f32[2,384,128]{2,1,0:T(8,128)}, u32[]{:S(2)}, u32[]{:S(2)}) collective-permute-start(f32[2,384,128]{2,1,0:T(8,128)} %bitcast.7.coarse), channel_id=1, source_target_pairs={{0,64},{16,80},{32,96},{48,112},{64,0},{80,16},{96,32},{112,48},{1... | collective-permute-start | bytes 1179656 | tf_op jit(solution)/shard_map/ppermute | solution.py:495
  18.3 20.7 %collective-permute-start.4 = (f32[2,384,128]{2,1,0:T(8,128)}, f32[2,384,128]{2,1,0:T(8,128)}, u32[]{:S(2)}, u32[]{:S(2)}) collective-permute-start(f32[2,384,128]{2,1,0:T(8,128)} %bitcast.7.coarse), channel_id=1, source_target_pairs={{0,32},{16,48},{32,64},{48,80},{64,96},{80,112},{96,0},{112,16},{1... | collective-permute-start | bytes 1179656 | tf_op jit(solution)/shard_map/ppermute | solution.py:495
  19.0 22.5 %collective-permute-start.1 = (f32[1536,128]{1,0:T(8,128)}, f32[1536,128]{1,0:T(8,128)}, u32[]{:S(2)}, u32[]{:S(2)}) collective-permute-start(f32[1536,128]{1,0:T(8,128)} %collective-permute-done), channel_id=1, source_target_pairs={{0,16},{16,0},{32,48},{48,32},{64,80},{80,64},{96,112},{112,96},{1... | collective-permute-start | bytes 2359304 | tf_op jit(solution)/shard_map/ppermute | solution.py:500
  19.9 19.9 %collective-permute-start.5 = (f32[2,384,128]{2,1,0:T(8,128)}, f32[2,384,128]{2,1,0:T(8,128)}, u32[]{:S(2)}, u32[]{:S(2)}) collective-permute-start(f32[2,384,128]{2,1,0:T(8,128)} %bitcast.7.coarse), channel_id=1, source_target_pairs={{0,16},{16,0},{32,48},{48,32},{64,80},{80,64},{96,112},{112,96},{1... | collective-permute-start | bytes 1179656 | tf_op jit(solution)/shard_map/ppermute | solution.py:500
  35.5 4.3 %collective-permute-start.6 = (f32[2,384,128]{2,1,0:T(8,128)}, f32[2,384,128]{2,1,0:T(8,128)}, u32[]{:S(2)}, u32[]{:S(2)}) collective-permute-start(f32[2,384,128]{2,1,0:T(8,128)} %collective-permute-done.2.refs_1_), channel_id=1, source_target_pairs={{0,16},{16,0},{32,48},{48,32},{64,80},{80,64},{96,112},{112,96},{1... | collective-permute-start | bytes 1179656 | tf_op jit(solution)/shard_map/ppermute | solution.py:500
  36.4 3.5 %collective-permute-start.7 = (f32[2,384,128]{2,1,0:T(8,128)}, f32[2,384,128]{2,1,0:T(8,128)}, u32[]{:S(2)}, u32[]{:S(2)}) collective-permute-start(f32[2,384,128]{2,1,0:T(8,128)} %collective-permute-done.3.refs_2_), channel_id=1, source_target_pairs={{0,16},{16,0},{32,48},{48,32},{64,80},{80,64},{96,112},{112,96},{1... | collective-permute-start | bytes 1179656 | tf_op jit(solution)/shard_map/ppermute | solution.py:500
  39.0 2.4 %collective-permute-start.8 = (f32[2,384,128]{2,1,0:T(8,128)}, f32[2,384,128]{2,1,0:T(8,128)}, u32[]{:S(2)}, u32[]{:S(2)}) collective-permute-start(f32[2,384,128]{2,1,0:T(8,128)} %collective-permute-done.4.refs_3_), channel_id=1, source_target_pairs={{0,16},{16,0},{32,48},{48,32},{64,80},{80,64},{96,112},{112,96},{1... | collective-permute-start | bytes 1179656 | tf_op jit(solution)/shard_map/ppermute | solution.py:500
  49.8 18.3 %copy-start.1 = (f32[2,128,1024]{2,1,0:T(8,128)S(1)}, f32[2,128,1024]{2,1,0:T(8,128)}, u32[]{:S(2)}) copy-start(f32[2,128,1024]{2,1,0:T(8,128)} %force.3) | copy-start | bytes 3145732
  52.7 3.9 %collective-permute-start.9 = (f32[3,8,128]{2,1,0:T(8,128)S(1)}, f32[3,8,128]{2,1,0:T(8,128)S(1)}, u32[]{:S(2)}, u32[]{:S(2)}) collective-permute-start(f32[3,8,128]{2,1,0:T(8,128)S(1)} %get-tuple-element.21), channel_id=1, source_target_pairs={{0,1},{2,3},{4,5},{6,7},{8,9},{10,11},{12,13},{14,15},{1,0},{3,2},... | collective-permute-start | bytes 36872 | tf_op jit(solution)/shard_map/ppermute | solution.py:490
  54.5 6.5 %collective-permute-start.10 = (f32[3,8,128]{2,1,0:T(8,128)S(1)}, f32[3,8,128]{2,1,0:T(8,128)S(1)}, u32[]{:S(2)}, u32[]{:S(2)}) collective-permute-start(f32[3,8,128]{2,1,0:T(8,128)S(1)} %get-tuple-element.20), channel_id=1, source_target_pairs={{1,2},{3,4},{5,6},{7,8},{9,10},{11,12},{13,14},{2,1},{4,3},{6,5},{... | collective-permute-start | bytes 36872 | tf_op jit(solution)/shard_map/ppermute | solution.py:490
  61.2 8.5 %collective-permute-start.11 = (f32[3,8,1152]{2,1,0:T(8,128)S(1)}, f32[3,8,1152]{2,1,0:T(8,128)S(1)}, u32[]{:S(2)}, u32[]{:S(2)}) collective-permute-start(f32[3,8,1152]{2,1,0:T(8,128)S(1)} %get-tuple-element.19), channel_id=1, source_target_pairs={{0,16},{32,48},{64,80},{96,112},{16,0},{48,32},{80,64},{112,96},{1... | collective-permute-start | bytes 331784 | tf_op jit(solution)/shard_map/ppermute | solution.py:490
  65.0 6.1 %collective-permute-start.12 = (f32[3,8,1152]{2,1,0:T(8,128)S(1)}, f32[3,8,1152]{2,1,0:T(8,128)S(1)}, u32[]{:S(2)}, u32[]{:S(2)}) collective-permute-start(f32[3,8,1152]{2,1,0:T(8,128)S(1)} %get-tuple-element.18), channel_id=1, source_target_pairs={{16,32},{48,64},{80,96},{32,16},{64,48},{96,80},{17,33},{49,65},{8... | collective-permute-start | bytes 331784 | tf_op jit(solution)/shard_map/ppermute | solution.py:490

commit v5 on v4

--- a/solution.py
+++ b/solution.py
@@ -339,7 +339,7 @@
     )(source, arrived, fresh, force)
 
 
-def edge_kernel(rows, first, second, sends, side):
+def edge_kernel(rows, second, first, sends, side):
     odd_row, odd_column = (lax.axis_index("gx") & 1) > 0, (lax.axis_index("gy") & 1) > 0
     blank = jnp.zeros((CELLS - 2 * HALO, CELLS), jnp.float32)
     for field in range(FIELDS):
@@ -360,7 +360,7 @@
             sends[1, field, :, at] = jnp.where(odd_row, bottom, top)
 
 
-def edges(rows, first, second):
+def edges(rows, second, first):
     f32 = jnp.float32
     return pl.pallas_call(
         edge_kernel,
@@ -372,10 +372,10 @@
         out_specs=[in_vmem] * 2,
         compiler_params=params(16),
         name="edge_rows",
-    )(rows, first, second)
-
-
-def sweep_kernel(inner, side, first, second, out, done_v, right, velo, faces, above, below, out_sems):
+    )(rows, second, first)
+
+
+def sweep_kernel(inner, side, second, first, out, done_v, right, velo, faces, above, below, out_sems):
     row = lax.broadcasted_iota(jnp.int32, (8, EXT_COLS), 0)
     odd_row = (lax.axis_index("gx") & 1) > 0
     for field in range(FIELDS):
@@ -462,7 +462,7 @@
             out_copy(field, block).wait()
 
 
-def sweeps(inner, side, first, second):
+def sweeps(inner, side, second, first):
     f32 = jnp.float32
     tiles = (TILES, 8, EXT_COLS)
     return pl.pallas_call(
@@ -481,7 +481,7 @@
         ],
         compiler_params=params(40),
         name="jacobi_sweeps",
-    )(inner, side, first, second)
+    )(inner, side, second, first)
 
 
 def paired(value, axis, start):
@@ -523,10 +523,12 @@
     owner = (((holder >> 1) - (gx >> 1)) & 3) + 4 * ((holder ^ gx) & 1)
     source, fresh, sends, rows = outline(refine[0], parent_block[0], owner, arrived, pieces)
     depth, inner = interior(source, arrived, fresh, force)
-    first, second = paired(sends[0], "gy", 0), paired(sends[1], "gy", 1)
-    sends, side = edges(rows, first, second)
-    first, second = paired(sends[0], "gx", 0), paired(sends[1], "gx", 1)
-    velocity = sweeps(inner, side, first, second)
+    second = paired(sends[1], "gy", 1)
+    first = paired(sends[0], "gy", 0)
+    sends, side = edges(rows, second, first)
+    second = paired(sends[1], "gx", 1)
+    first = paired(sends[0], "gx", 0)
+    velocity = sweeps(inner, side, second, first)
     return depth, velocity
 
 

time: 76.8 us -> 76.1 us (level)
  the two profiles are of different devices: /device:TPU:7 before, /device:TPU:81 now
where the time goes in v5:
time: 76.1 us; the launch traced here: 76 us
  waiting for transfers between devices  35.5 us (47%)
  starting transfers between devices  24.2 us (32%)
  Pallas kernels  14.3 us (19%)
  local copies, waits for them, and re-layouts  1.26 us (2%)
  between operations  0.83 us (1%)
    ppermute x3, waiting for transfers between devices, around_ring(): lax.ppermute(value, axis, [(i, (i + step) % count) for i in range(count)])  14.9 us
    all_to_all x1, waiting for transfers between devices, body(): lax.all_to_all(outgoing, 'gy', split_axis=0, concat_axis=0, tiled=True, a...  13.6 us
    ppermute x4, starting transfers between devices, paired(): return lax.ppermute(value, axis, pairs + [(j, i) for i, j in pairs])  9.1 us
    all_to_all x1, starting transfers between devices, body(): lax.all_to_all(outgoing, 'gy', split_axis=0, concat_axis=0, tiled=True, a...  6.81 us
    pallas_call x1, Pallas kernels, sweeps(): pl.pallas_call(sweep_kernel, out_shape=jax.ShapeDtypeStruct((2, CELLS, WI...  5.67 us
    ppermute x4, waiting for transfers between devices, paired(): return lax.ppermute(value, axis, pairs + [(j, i) for i, j in pairs])  5.34 us
    ppermute x6, starting transfers between devices, swapped(): return lax.ppermute(value, axis, [(i, i ^ bit) for i in range(count)])  5.21 us
    ppermute x3, starting transfers between devices, around_ring(): lax.ppermute(value, axis, [(i, (i + step) % count) for i in range(count)])  3.07 us
  transfers between devices with their start and end apart: 14, of which 7 were waited for; matrix products, arithmetic and copies ran while one was open for 0% of the time, Pallas kernels for 4%

profile of v5, /device:TPU:81, one launch (start us, length us, event | category | flops | bytes accessed | tf_op | source)
XLA Modules:
  0.0 76.0 jit_solution(16377670387205570048)
XLA Ops:
  0.6 2.9 %stage_outgoing.1 = f32[16,392,128]{2,1,0:T(8,128)} custom-call(s32[8]{0:T(128)} %bitcast.22, f32[8,384,128]{2,1,0:T(8,128)} %bitcast.21), custom_call_target="tpu_custom_call" | custom-call | tf_op jit(solution)/shard_map/stage_outgoing/pallas_call | solution.py:84
  3.6 6.8 %all-to-all-start = ((f32[16,392,128]{2,1,0:T(8,128)}), f32[16,392,128]{2,1,0:T(8,128)S(1)}, u32[]{:S(2)}, u32[]{:S(2)}) async-start(f32[16,392,128]{2,1,0:T(8,128)} %stage_outgoing.1), calls=%async_computation | async-start | bytes 6422528 | tf_op jit(solution)/shard_map/all_to_all | solution.py:515
  10.4 1.2 %copy-done = f32[2,128,1024]{2,1,0:T(8,128)S(1)} copy-done((f32[2,128,1024]{2,1,0:T(8,128)S(1)}, f32[2,128,1024]{2,1,0:T(8,128)}, u32[]{:S(2)}) %copy-start) | copy-done | bytes 1048600
  11.6 1.5 %keep_own.1 = f32[1536,128]{1,0:T(8,128)S(1)} custom-call(f32[2,128,1024]{2,1,0:T(8,128)S(1)} %copy-done, f32[2,384,128]{2,1,0:T(8,128)} %bitcast.7.coarse), custom_call_target="tpu_custom_call" | custom-call | flops 262144 | bytes 3145728 | tf_op jit(solution)/shard_map/keep_own/pallas_call | solution.py:131
  13.1 1.3 %collective-permute-start = (f32[1536,128]{1,0:T(8,128)S(1)}, f32[1536,128]{1,0:T(8,128)}, u32[]{:S(2)}, u32[]{:S(2)}) collective-permute-start(f32[1536,128]{1,0:T(8,128)S(1)} %keep_own.1), channel_id=1, source_target_pairs={{0,16},{16,0},{32,48},{48,32},{64,80},{80,64},{96,112},{112,96},{1... | collective-permute-start | bytes 2359304 | tf_op jit(solution)/shard_map/ppermute | solution.py:500
  14.4 3.1 %collective-permute-start.3 = (f32[2,384,128]{2,1,0:T(8,128)}, f32[2,384,128]{2,1,0:T(8,128)}, u32[]{:S(2)}, u32[]{:S(2)}) collective-permute-start(f32[2,384,128]{2,1,0:T(8,128)} %bitcast.7.coarse), channel_id=1, source_target_pairs={{0,64},{16,80},{32,96},{48,112},{64,0},{80,16},{96,32},{112,48},{1... | collective-permute-start | bytes 1179656 | tf_op jit(solution)/shard_map/ppermute | solution.py:495
  17.5 0.6 collective-permute-start.1
  18.1 0.1 collective-permute-start.5
  18.2 7.2 %collective-permute-done.2.refs_1_ = f32[2,384,128]{2,1,0:T(8,128)} collective-permute-done((f32[2,384,128]{2,1,0:T(8,128)}, f32[2,384,128]{2,1,0:T(8,128)}, u32[]{:S(2)}, u32[]{:S(2)}) %collective-permute-start.2) | collective-permute-done | bytes 393248 | tf_op jit(solution)/shard_map/ppermute | solution.py:495
  25.4 1.3 %collective-permute-start.6 = (f32[2,384,128]{2,1,0:T(8,128)}, f32[2,384,128]{2,1,0:T(8,128)}, u32[]{:S(2)}, u32[]{:S(2)}) collective-permute-start(f32[2,384,128]{2,1,0:T(8,128)} %collective-permute-done.2.refs_1_), channel_id=1, source_target_pairs={{0,16},{16,0},{32,48},{48,32},{64,80},{80,64},{96,112},{112,96},{1... | collective-permute-start | bytes 1179656 | tf_op jit(solution)/shard_map/ppermute | solution.py:500
  26.7 0.3 collective-permute-done.3.refs_2_
  27.0 1.4 %collective-permute-start.7 = (f32[2,384,128]{2,1,0:T(8,128)}, f32[2,384,128]{2,1,0:T(8,128)}, u32[]{:S(2)}, u32[]{:S(2)}) collective-permute-start(f32[2,384,128]{2,1,0:T(8,128)} %collective-permute-done.3.refs_2_), channel_id=1, source_target_pairs={{0,16},{16,0},{32,48},{48,32},{64,80},{80,64},{96,112},{112,96},{1... | collective-permute-start | bytes 1179656 | tf_op jit(solution)/shard_map/ppermute | solution.py:500
  28.4 7.4 %collective-permute-done.4.refs_3_ = f32[2,384,128]{2,1,0:T(8,128)} collective-permute-done((f32[2,384,128]{2,1,0:T(8,128)}, f32[2,384,128]{2,1,0:T(8,128)}, u32[]{:S(2)}, u32[]{:S(2)}) %collective-permute-start.4) | collective-permute-done | bytes 393248 | tf_op jit(solution)/shard_map/ppermute | solution.py:495
  35.8 0.5 collective-permute-start.8
  36.4 1.6 %collective-permute-done.8.refs_7_ = f32[2,384,128]{2,1,0:T(8,128)} collective-permute-done((f32[2,384,128]{2,1,0:T(8,128)}, f32[2,384,128]{2,1,0:T(8,128)}, u32[]{:S(2)}, u32[]{:S(2)}) %collective-permute-start.8) | collective-permute-done | bytes 393248 | tf_op jit(solution)/shard_map/ppermute | solution.py:500
  38.0 13.6 %all-to-all-done.arrived = f32[16,392,128]{2,1,0:T(8,128)S(1)} async-done(((f32[16,392,128]{2,1,0:T(8,128)}), f32[16,392,128]{2,1,0:T(8,128)S(1)}, u32[]{:S(2)}, u32[]{:S(2)}) %all-to-all-start) | async-done | bytes 3211296 | tf_op jit(solution)/shard_map/all_to_all | solution.py:515
  51.6 2.6 %block_outline.1 = (s32[8]{0:T(128)S(1)}, f32[2,384,128]{2,1,0:T(8,128)S(1)}, f32[2,3,8,128]{3,2,1,0:T(8,128)S(1)}, f32[2,3,8,8,128]{4,3,2,1,0:T(8,128)S(1)}) custom-call(s32[8]{0:T(128)S(1)} %bitcast.18, s32[8]{0:T(128)S(1)} %bitcast.20, s32[1]{0:T(128)S(6)} %add.3.owner, f32[16,392,128]{2,1,0:T(8,128)S(1)} %all-to-all-done.arrived, ...), custom_call_target="tpu_custom_call" | custom-call | tf_op jit(solution)/shard_map/block_outline/pallas_call | solution.py:270
  54.2 1.9 %collective-permute-start.9 = (f32[3,8,128]{2,1,0:T(8,128)S(1)}, f32[3,8,128]{2,1,0:T(8,128)S(1)}, u32[]{:S(2)}, u32[]{:S(2)}) collective-permute-start(f32[3,8,128]{2,1,0:T(8,128)S(1)} %get-tuple-element.21), channel_id=1, source_target_pairs={{1,2},{3,4},{5,6},{7,8},{9,10},{11,12},{13,14},{2,1},{4,3},{6,5},{... | collective-permute-start | bytes 36872 | tf_op jit(solution)/shard_map/ppermute | solution.py:490
  56.2 4.5 %collective-permute-done.9.second = f32[3,8,128]{2,1,0:T(8,128)S(1)} collective-permute-done((f32[3,8,128]{2,1,0:T(8,128)S(1)}, f32[3,8,128]{2,1,0:T(8,128)S(1)}, u32[]{:S(2)}, u32[]{:S(2)}) %collective-permute-start.9) | collective-permute-done | bytes 12320 | tf_op jit(solution)/shard_map/ppermute | solution.py:490
  60.7 0.1 edge_rows.1
  60.9 7.0 %collective-permute-start.11 = (f32[3,8,1152]{2,1,0:T(8,128)S(1)}, f32[3,8,1152]{2,1,0:T(8,128)S(1)}, u32[]{:S(2)}, u32[]{:S(2)}) collective-permute-start(f32[3,8,1152]{2,1,0:T(8,128)S(1)} %get-tuple-element.19), channel_id=1, source_target_pairs={{16,32},{48,64},{80,96},{32,16},{64,48},{96,80},{17,33},{49,65},{8... | collective-permute-start | bytes 331784 | tf_op jit(solution)/shard_map/ppermute | solution.py:490
  68.0 1.5 %block_interior.1 = (f32[128,1024]{1,0:T(8,128)}, f32[3,8,144,128]{3,2,1,0:T(8,128)S(1)}) custom-call(s32[8]{0:T(128)S(1)} %get-tuple-element.10.source, f32[16,392,128]{2,1,0:T(8,128)S(1)} %all-to-all-done.arrived, f32[2,384,128]{2,1,0:T(8,128)S(1)} %get-tuple-element.11.fresh, f32[2,128,1024]{2,1,0:T(8,128)S(1)} %copy-done.1), custom_call_target="tpu_custom_call" | custom-call | flops 1048576 | bytes 6291456 | tf_op jit(solution)/shard_map/block_interior/pallas_call | solution.py:323
  69.5 0.8 %collective-permute-done.11.second = f32[3,8,1152]{2,1,0:T(8,128)S(1)} collective-permute-done((f32[3,8,1152]{2,1,0:T(8,128)S(1)}, f32[3,8,1152]{2,1,0:T(8,128)S(1)}, u32[]{:S(2)}, u32[]{:S(2)}) %collective-permute-start.11) | collective-permute-done | bytes 110624 | tf_op jit(solution)/shard_map/ppermute | solution.py:490
  70.3 5.7 %jacobi_sweeps.1 = f32[2,128,1024]{2,1,0:T(8,128)} custom-call(f32[3,8,144,128]{3,2,1,0:T(8,128)S(1)} %get-tuple-element.13.inner, f32[3,144,128]{2,1,0:T(8,128)S(1)} %get-tuple-element.16.side, f32[3,8,1152]{2,1,0:T(8,128)S(1)} %collective-permute-done.11.second, f32[3,8,1152]{2,1,0:T(8,128)S(1)} %collective-permute-done.12.first), custom_call_target="tpu_custom_call" | custom-call | tf_op jit(solution)/shard_map/jacobi_sweeps/pallas_call | solution.py:468
  (20 shorter events, 0.2 us)
Async XLA Ops:
  3.6 32.7 %copy-start.3 = (s32[1,8]{1,0:T(1,128)S(1)}, s32[1,8]{1,0:T(1,128)}, u32[]{:S(2)}) copy-start(s32[1,8]{1,0:T(1,128)} %param.9) | copy-start | bytes 100
  3.6 48.0 %copy-start.2 = (s32[1,8]{1,0:T(1,128)S(1)}, s32[1,8]{1,0:T(1,128)}, u32[]{:S(2)}) copy-start(s32[1,8]{1,0:T(1,128)} %param.8) | copy-start | bytes 100
  3.6 48.0 %all-to-all-start = ((f32[16,392,128]{2,1,0:T(8,128)}), f32[16,392,128]{2,1,0:T(8,128)S(1)}, u32[]{:S(2)}, u32[]{:S(2)}) async-start(f32[16,392,128]{2,1,0:T(8,128)} %stage_outgoing.1), calls=%async_computation | async-start | bytes 6422528 | tf_op jit(solution)/shard_map/all_to_all | solution.py:515
  10.4 1.2 %copy-start = (f32[2,128,1024]{2,1,0:T(8,128)S(1)}, f32[2,128,1024]{2,1,0:T(8,128)}, u32[]{:S(2)}) copy-start(f32[2,128,1024]{2,1,0:T(8,128)} %force.3) | copy-start | bytes 3145732
  13.1 4.3 %collective-permute-start = (f32[1536,128]{1,0:T(8,128)S(1)}, f32[1536,128]{1,0:T(8,128)}, u32[]{:S(2)}, u32[]{:S(2)}) collective-permute-start(f32[1536,128]{1,0:T(8,128)S(1)} %keep_own.1), channel_id=1, source_target_pairs={{0,16},{16,0},{32,48},{48,32},{64,80},{80,64},{96,112},{112,96},{1... | collective-permute-start | bytes 2359304 | tf_op jit(solution)/shard_map/ppermute | solution.py:500
  14.4 11.0 %collective-permute-start.2 = (f32[2,384,128]{2,1,0:T(8,128)}, f32[2,384,128]{2,1,0:T(8,128)}, u32[]{:S(2)}, u32[]{:S(2)}) collective-permute-start(f32[2,384,128]{2,1,0:T(8,128)} %bitcast.7.coarse), channel_id=1, source_target_pairs={{0,96},{16,112},{32,0},{48,16},{64,32},{80,48},{96,64},{112,80},{1... | collective-permute-start | bytes 1179656 | tf_op jit(solution)/shard_map/ppermute | solution.py:495
  14.4 12.6 %collective-permute-start.3 = (f32[2,384,128]{2,1,0:T(8,128)}, f32[2,384,128]{2,1,0:T(8,128)}, u32[]{:S(2)}, u32[]{:S(2)}) collective-permute-start(f32[2,384,128]{2,1,0:T(8,128)} %bitcast.7.coarse), channel_id=1, source_target_pairs={{0,64},{16,80},{32,96},{48,112},{64,0},{80,16},{96,32},{112,48},{1... | collective-permute-start | bytes 1179656 | tf_op jit(solution)/shard_map/ppermute | solution.py:495
  17.5 18.3 %collective-permute-start.4 = (f32[2,384,128]{2,1,0:T(8,128)}, f32[2,384,128]{2,1,0:T(8,128)}, u32[]{:S(2)}, u32[]{:S(2)}) collective-permute-start(f32[2,384,128]{2,1,0:T(8,128)} %bitcast.7.coarse), channel_id=1, source_target_pairs={{0,32},{16,48},{32,64},{48,80},{64,96},{80,112},{96,0},{112,16},{1... | collective-permute-start | bytes 1179656 | tf_op jit(solution)/shard_map/ppermute | solution.py:495
  17.5 20.5 %collective-permute-start.1 = (f32[1536,128]{1,0:T(8,128)}, f32[1536,128]{1,0:T(8,128)}, u32[]{:S(2)}, u32[]{:S(2)}) collective-permute-start(f32[1536,128]{1,0:T(8,128)} %collective-permute-done), channel_id=1, source_target_pairs={{0,16},{16,0},{32,48},{48,32},{64,80},{80,64},{96,112},{112,96},{1... | collective-permute-start | bytes 2359304 | tf_op jit(solution)/shard_map/ppermute | solution.py:500
  18.1 18.3 %collective-permute-start.5 = (f32[2,384,128]{2,1,0:T(8,128)}, f32[2,384,128]{2,1,0:T(8,128)}, u32[]{:S(2)}, u32[]{:S(2)}) collective-permute-start(f32[2,384,128]{2,1,0:T(8,128)} %bitcast.7.coarse), channel_id=1, source_target_pairs={{0,16},{16,0},{32,48},{48,32},{64,80},{80,64},{96,112},{112,96},{1... | collective-permute-start | bytes 1179656 | tf_op jit(solution)/shard_map/ppermute | solution.py:500
  25.4 11.0 %collective-permute-start.6 = (f32[2,384,128]{2,1,0:T(8,128)}, f32[2,384,128]{2,1,0:T(8,128)}, u32[]{:S(2)}, u32[]{:S(2)}) collective-permute-start(f32[2,384,128]{2,1,0:T(8,128)} %collective-permute-done.2.refs_1_), channel_id=1, source_target_pairs={{0,16},{16,0},{32,48},{48,32},{64,80},{80,64},{96,112},{112,96},{1... | collective-permute-start | bytes 1179656 | tf_op jit(solution)/shard_map/ppermute | solution.py:500
  27.0 9.4 %collective-permute-start.7 = (f32[2,384,128]{2,1,0:T(8,128)}, f32[2,384,128]{2,1,0:T(8,128)}, u32[]{:S(2)}, u32[]{:S(2)}) collective-permute-start(f32[2,384,128]{2,1,0:T(8,128)} %collective-permute-done.3.refs_2_), channel_id=1, source_target_pairs={{0,16},{16,0},{32,48},{48,32},{64,80},{80,64},{96,112},{112,96},{1... | collective-permute-start | bytes 1179656 | tf_op jit(solution)/shard_map/ppermute | solution.py:500
  35.8 2.2 %collective-permute-start.8 = (f32[2,384,128]{2,1,0:T(8,128)}, f32[2,384,128]{2,1,0:T(8,128)}, u32[]{:S(2)}, u32[]{:S(2)}) collective-permute-start(f32[2,384,128]{2,1,0:T(8,128)} %collective-permute-done.4.refs_3_), channel_id=1, source_target_pairs={{0,16},{16,0},{32,48},{48,32},{64,80},{80,64},{96,112},{112,96},{1... | collective-permute-start | bytes 1179656 | tf_op jit(solution)/shard_map/ppermute | solution.py:500
  51.6 16.4 %copy-start.1 = (f32[2,128,1024]{2,1,0:T(8,128)S(1)}, f32[2,128,1024]{2,1,0:T(8,128)}, u32[]{:S(2)}) copy-start(f32[2,128,1024]{2,1,0:T(8,128)} %force.3) | copy-start | bytes 3145732
  54.2 6.5 %collective-permute-start.9 = (f32[3,8,128]{2,1,0:T(8,128)S(1)}, f32[3,8,128]{2,1,0:T(8,128)S(1)}, u32[]{:S(2)}, u32[]{:S(2)}) collective-permute-start(f32[3,8,128]{2,1,0:T(8,128)S(1)} %get-tuple-element.21), channel_id=1, source_target_pairs={{1,2},{3,4},{5,6},{7,8},{9,10},{11,12},{13,14},{2,1},{4,3},{6,5},{... | collective-permute-start | bytes 36872 | tf_op jit(solution)/shard_map/ppermute | solution.py:490
  56.1 4.6 %collective-permute-start.10 = (f32[3,8,128]{2,1,0:T(8,128)S(1)}, f32[3,8,128]{2,1,0:T(8,128)S(1)}, u32[]{:S(2)}, u32[]{:S(2)}) collective-permute-start(f32[3,8,128]{2,1,0:T(8,128)S(1)} %get-tuple-element.20), channel_id=1, source_target_pairs={{0,1},{2,3},{4,5},{6,7},{8,9},{10,11},{12,13},{14,15},{1,0},{3,2},... | collective-permute-start | bytes 36872 | tf_op jit(solution)/shard_map/ppermute | solution.py:490
  60.9 9.4 %collective-permute-start.11 = (f32[3,8,1152]{2,1,0:T(8,128)S(1)}, f32[3,8,1152]{2,1,0:T(8,128)S(1)}, u32[]{:S(2)}, u32[]{:S(2)}) collective-permute-start(f32[3,8,1152]{2,1,0:T(8,128)S(1)} %get-tuple-element.19), channel_id=1, source_target_pairs={{16,32},{48,64},{80,96},{32,16},{64,48},{96,80},{17,33},{49,65},{8... | collective-permute-start | bytes 331784 | tf_op jit(solution)/shard_map/ppermute | solution.py:490
  67.9 2.4 %collective-permute-start.12 = (f32[3,8,1152]{2,1,0:T(8,128)S(1)}, f32[3,8,1152]{2,1,0:T(8,128)S(1)}, u32[]{:S(2)}, u32[]{:S(2)}) collective-permute-start(f32[3,8,1152]{2,1,0:T(8,128)S(1)} %get-tuple-element.18), channel_id=1, source_target_pairs={{0,16},{32,48},{64,80},{96,112},{16,0},{48,32},{80,64},{112,96},{1... | collective-permute-start | bytes 331784 | tf_op jit(solution)/shard_map/ppermute | solution.py:490

commit v6 on v5

--- a/solution.py
+++ b/solution.py
@@ -36,13 +36,14 @@
     return pltpu.CompilerParams(vmem_limit_bytes=mib * MIB)
 
 
-ORDER = (0, 1, 3, 2, 10, 11, 9, 8, 4, 5, 7, 6, 14, 15, 13, 12)
+ORDER = (13, 15, 14, 6, 7, 5, 4, 8, 9, 11, 10, 2, 3, 1, 0, 12)
 
 
 def chunk_of(device):
-    high, low = device >> 2, device & 3
-    high = ((high & 1) << 1) | (high >> 1)
-    return (high << 2) | ((low ^ (low >> 1)) ^ ((high & 1) * 3))
+    place = jnp.int32(0)
+    for number, other in enumerate(ORDER):
+        place = jnp.where(device == other, number, place)
+    return place
 
 
 def stage_kernel(dest, old, out, patch_v, note_v, in_sems, out_sems, note_sem):

time: 76.1 us -> 74.4 us (0.978)
  the two profiles are of different devices: /device:TPU:81 before, /device:TPU:7 now
where the time goes in v6:
time: 74.4 us; the launch traced here: 73.8 us
  waiting for transfers between devices  30 us (40%)
  starting transfers between devices  27 us (36%)
  Pallas kernels  14.6 us (20%)
  local copies, waits for them, and re-layouts  1.26 us (2%)
  between operations  0.83 us (1%)
    ppermute x3, waiting for transfers between devices, around_ring(): lax.ppermute(value, axis, [(i, (i + step) % count) for i in range(count)])  18.3 us
    ppermute x4, starting transfers between devices, paired(): return lax.ppermute(value, axis, pairs + [(j, i) for i, j in pairs])  11.3 us
    all_to_all x1, starting transfers between devices, body(): lax.all_to_all(outgoing, 'gy', split_axis=0, concat_axis=0, tiled=True, a...  7.41 us
    all_to_all x1, waiting for transfers between devices, body(): lax.all_to_all(outgoing, 'gy', split_axis=0, concat_axis=0, tiled=True, a...  6.5 us
    pallas_call x1, Pallas kernels, sweeps(): pl.pallas_call(sweep_kernel, out_shape=jax.ShapeDtypeStruct((2, CELLS, WI...  5.67 us
    ppermute x3, starting transfers between devices, around_ring(): lax.ppermute(value, axis, [(i, (i + step) % count) for i in range(count)])  4.48 us
    ppermute x6, starting transfers between devices, swapped(): return lax.ppermute(value, axis, [(i, i ^ bit) for i in range(count)])  3.81 us
    ppermute x4, waiting for transfers between devices, paired(): return lax.ppermute(value, axis, pairs + [(j, i) for i, j in pairs])  3.64 us
  transfers between devices with their start and end apart: 14, of which 7 were waited for; matrix products, arithmetic and copies ran while one was open for 0% of the time, Pallas kernels for 4%

profile of v6, /device:TPU:7, one launch (start us, length us, event | category | flops | bytes accessed | tf_op | source)
XLA Modules:
  0.0 73.8 jit_solution(407411787409036848)
XLA Ops:
  0.6 3.0 %stage_outgoing.1 = f32[16,392,128]{2,1,0:T(8,128)} custom-call(s32[8]{0:T(128)} %bitcast.22, f32[8,384,128]{2,1,0:T(8,128)} %bitcast.21), custom_call_target="tpu_custom_call" | custom-call | tf_op jit(solution)/shard_map/stage_outgoing/pallas_call | solution.py:85
  3.7 7.4 %all-to-all-start = ((f32[16,392,128]{2,1,0:T(8,128)}), f32[16,392,128]{2,1,0:T(8,128)S(1)}, u32[]{:S(2)}, u32[]{:S(2)}) async-start(f32[16,392,128]{2,1,0:T(8,128)} %stage_outgoing.1), calls=%async_computation | async-start | bytes 6422528 | tf_op jit(solution)/shard_map/all_to_all | solution.py:516
  11.1 1.2 %copy-done = f32[2,128,1024]{2,1,0:T(8,128)S(1)} copy-done((f32[2,128,1024]{2,1,0:T(8,128)S(1)}, f32[2,128,1024]{2,1,0:T(8,128)}, u32[]{:S(2)}) %copy-start) | copy-done | bytes 1048600
  12.3 1.5 %keep_own.1 = f32[1536,128]{1,0:T(8,128)S(1)} custom-call(f32[2,128,1024]{2,1,0:T(8,128)S(1)} %copy-done, f32[2,384,128]{2,1,0:T(8,128)} %bitcast.7.coarse), custom_call_target="tpu_custom_call" | custom-call | flops 262144 | bytes 3145728 | tf_op jit(solution)/shard_map/keep_own/pallas_call | solution.py:132
  13.8 1.3 %collective-permute-start = (f32[1536,128]{1,0:T(8,128)S(1)}, f32[1536,128]{1,0:T(8,128)}, u32[]{:S(2)}, u32[]{:S(2)}) collective-permute-start(f32[1536,128]{1,0:T(8,128)S(1)} %keep_own.1), channel_id=1, source_target_pairs={{0,16},{16,0},{32,48},{48,32},{64,80},{80,64},{96,112},{112,96},{1... | collective-permute-start | bytes 2359304 | tf_op jit(solution)/shard_map/ppermute | solution.py:501
  15.1 3.8 %collective-permute-start.2 = (f32[2,384,128]{2,1,0:T(8,128)}, f32[2,384,128]{2,1,0:T(8,128)}, u32[]{:S(2)}, u32[]{:S(2)}) collective-permute-start(f32[2,384,128]{2,1,0:T(8,128)} %bitcast.7.coarse), channel_id=1, source_target_pairs={{0,96},{16,112},{32,0},{48,16},{64,32},{80,48},{96,64},{112,80},{1... | collective-permute-start | bytes 1179656 | tf_op jit(solution)/shard_map/ppermute | solution.py:496
  18.9 0.7 collective-permute-start.4
  19.5 0.9 %collective-permute-start.1 = (f32[1536,128]{1,0:T(8,128)}, f32[1536,128]{1,0:T(8,128)}, u32[]{:S(2)}, u32[]{:S(2)}) collective-permute-start(f32[1536,128]{1,0:T(8,128)} %collective-permute-done), channel_id=1, source_target_pairs={{0,16},{16,0},{32,48},{48,32},{64,80},{80,64},{96,112},{112,96},{1... | collective-permute-start | bytes 2359304 | tf_op jit(solution)/shard_map/ppermute | solution.py:501
  20.5 15.6 %collective-permute-done.2.refs_1_ = f32[2,384,128]{2,1,0:T(8,128)} collective-permute-done((f32[2,384,128]{2,1,0:T(8,128)}, f32[2,384,128]{2,1,0:T(8,128)}, u32[]{:S(2)}, u32[]{:S(2)}) %collective-permute-start.2) | collective-permute-done | bytes 393248 | tf_op jit(solution)/shard_map/ppermute | solution.py:496
  36.1 0.9 %collective-permute-start.6 = (f32[2,384,128]{2,1,0:T(8,128)}, f32[2,384,128]{2,1,0:T(8,128)}, u32[]{:S(2)}, u32[]{:S(2)}) collective-permute-start(f32[2,384,128]{2,1,0:T(8,128)} %collective-permute-done.2.refs_1_), channel_id=1, source_target_pairs={{0,16},{16,0},{32,48},{48,32},{64,80},{80,64},{96,112},{112,96},{1... | collective-permute-start | bytes 1179656 | tf_op jit(solution)/shard_map/ppermute | solution.py:501
  36.9 2.6 %collective-permute-done.4.refs_3_ = f32[2,384,128]{2,1,0:T(8,128)} collective-permute-done((f32[2,384,128]{2,1,0:T(8,128)}, f32[2,384,128]{2,1,0:T(8,128)}, u32[]{:S(2)}, u32[]{:S(2)}) %collective-permute-start.4) | collective-permute-done | bytes 393248 | tf_op jit(solution)/shard_map/ppermute | solution.py:496
  39.6 0.8 %collective-permute-start.8 = (f32[2,384,128]{2,1,0:T(8,128)}, f32[2,384,128]{2,1,0:T(8,128)}, u32[]{:S(2)}, u32[]{:S(2)}) collective-permute-start(f32[2,384,128]{2,1,0:T(8,128)} %collective-permute-done.4.refs_3_), channel_id=1, source_target_pairs={{0,16},{16,0},{32,48},{48,32},{64,80},{80,64},{96,112},{112,96},{1... | collective-permute-start | bytes 1179656 | tf_op jit(solution)/shard_map/ppermute | solution.py:501
  40.4 1.6 %collective-permute-done.8.refs_7_ = f32[2,384,128]{2,1,0:T(8,128)} collective-permute-done((f32[2,384,128]{2,1,0:T(8,128)}, f32[2,384,128]{2,1,0:T(8,128)}, u32[]{:S(2)}, u32[]{:S(2)}) %collective-permute-start.8) | collective-permute-done | bytes 393248 | tf_op jit(solution)/shard_map/ppermute | solution.py:501
  42.0 6.5 %all-to-all-done.arrived = f32[16,392,128]{2,1,0:T(8,128)S(1)} async-done(((f32[16,392,128]{2,1,0:T(8,128)}), f32[16,392,128]{2,1,0:T(8,128)S(1)}, u32[]{:S(2)}, u32[]{:S(2)}) %all-to-all-start) | async-done | bytes 3211296 | tf_op jit(solution)/shard_map/all_to_all | solution.py:516
  48.6 2.9 %block_outline.1 = (s32[8]{0:T(128)S(1)}, f32[2,384,128]{2,1,0:T(8,128)S(1)}, f32[2,3,8,128]{3,2,1,0:T(8,128)S(1)}, f32[2,3,8,8,128]{4,3,2,1,0:T(8,128)S(1)}) custom-call(s32[8]{0:T(128)S(1)} %bitcast.18, s32[8]{0:T(128)S(1)} %bitcast.20, s32[1]{0:T(128)S(6)} %add.3.owner, f32[16,392,128]{2,1,0:T(8,128)S(1)} %all-to-all-done.arrived, ...), custom_call_target="tpu_custom_call" | custom-call | tf_op jit(solution)/shard_map/block_outline/pallas_call | solution.py:271
  51.4 5.5 %collective-permute-start.9 = (f32[3,8,128]{2,1,0:T(8,128)S(1)}, f32[3,8,128]{2,1,0:T(8,128)S(1)}, u32[]{:S(2)}, u32[]{:S(2)}) collective-permute-start(f32[3,8,128]{2,1,0:T(8,128)S(1)} %get-tuple-element.21), channel_id=1, source_target_pairs={{1,2},{3,4},{5,6},{7,8},{9,10},{11,12},{13,14},{2,1},{4,3},{6,5},{... | collective-permute-start | bytes 36872 | tf_op jit(solution)/shard_map/ppermute | solution.py:491
  57.1 1.0 %collective-permute-done.9.second = f32[3,8,128]{2,1,0:T(8,128)S(1)} collective-permute-done((f32[3,8,128]{2,1,0:T(8,128)S(1)}, f32[3,8,128]{2,1,0:T(8,128)S(1)}, u32[]{:S(2)}, u32[]{:S(2)}) %collective-permute-start.9) | collective-permute-done | bytes 12320 | tf_op jit(solution)/shard_map/ppermute | solution.py:491
  58.0 1.9 %collective-permute-done.10.first = f32[3,8,128]{2,1,0:T(8,128)S(1)} collective-permute-done((f32[3,8,128]{2,1,0:T(8,128)S(1)}, f32[3,8,128]{2,1,0:T(8,128)S(1)}, u32[]{:S(2)}, u32[]{:S(2)}) %collective-permute-start.10) | collective-permute-done | bytes 12320 | tf_op jit(solution)/shard_map/ppermute | solution.py:491
  59.9 0.1 edge_rows.1
  60.1 5.6 %collective-permute-start.11 = (f32[3,8,1152]{2,1,0:T(8,128)S(1)}, f32[3,8,1152]{2,1,0:T(8,128)S(1)}, u32[]{:S(2)}, u32[]{:S(2)}) collective-permute-start(f32[3,8,1152]{2,1,0:T(8,128)S(1)} %get-tuple-element.19), channel_id=1, source_target_pairs={{16,32},{48,64},{80,96},{32,16},{64,48},{96,80},{17,33},{49,65},{8... | collective-permute-start | bytes 331784 | tf_op jit(solution)/shard_map/ppermute | solution.py:491
  65.7 0.1 collective-permute-start.12
  65.8 1.5 %block_interior.1 = (f32[128,1024]{1,0:T(8,128)}, f32[3,8,144,128]{3,2,1,0:T(8,128)S(1)}) custom-call(s32[8]{0:T(128)S(1)} %get-tuple-element.10.source, f32[16,392,128]{2,1,0:T(8,128)S(1)} %all-to-all-done.arrived, f32[2,384,128]{2,1,0:T(8,128)S(1)} %get-tuple-element.11.fresh, f32[2,128,1024]{2,1,0:T(8,128)S(1)} %copy-done.1), custom_call_target="tpu_custom_call" | custom-call | flops 1048576 | bytes 6291456 | tf_op jit(solution)/shard_map/block_interior/pallas_call | solution.py:324
  67.3 0.8 %collective-permute-done.11.second = f32[3,8,1152]{2,1,0:T(8,128)S(1)} collective-permute-done((f32[3,8,1152]{2,1,0:T(8,128)S(1)}, f32[3,8,1152]{2,1,0:T(8,128)S(1)}, u32[]{:S(2)}, u32[]{:S(2)}) %collective-permute-start.11) | collective-permute-done | bytes 110624 | tf_op jit(solution)/shard_map/ppermute | solution.py:491
  68.1 5.7 %jacobi_sweeps.1 = f32[2,128,1024]{2,1,0:T(8,128)} custom-call(f32[3,8,144,128]{3,2,1,0:T(8,128)S(1)} %get-tuple-element.13.inner, f32[3,144,128]{2,1,0:T(8,128)S(1)} %get-tuple-element.16.side, f32[3,8,1152]{2,1,0:T(8,128)S(1)} %collective-permute-done.11.second, f32[3,8,1152]{2,1,0:T(8,128)S(1)} %collective-permute-done.12.first), custom_call_target="tpu_custom_call" | custom-call | tf_op jit(solution)/shard_map/jacobi_sweeps/pallas_call | solution.py:469
  (20 shorter events, 0.2 us)
Async XLA Ops:
  3.6 36.7 %copy-start.3 = (s32[1,8]{1,0:T(1,128)S(1)}, s32[1,8]{1,0:T(1,128)}, u32[]{:S(2)}) copy-start(s32[1,8]{1,0:T(1,128)} %param.9) | copy-start | bytes 100
  3.6 44.9 %copy-start.2 = (s32[1,8]{1,0:T(1,128)S(1)}, s32[1,8]{1,0:T(1,128)}, u32[]{:S(2)}) copy-start(s32[1,8]{1,0:T(1,128)} %param.8) | copy-start | bytes 100
  3.7 44.9 %all-to-all-start = ((f32[16,392,128]{2,1,0:T(8,128)}), f32[16,392,128]{2,1,0:T(8,128)S(1)}, u32[]{:S(2)}, u32[]{:S(2)}) async-start(f32[16,392,128]{2,1,0:T(8,128)} %stage_outgoing.1), calls=%async_computation | async-start | bytes 6422528 | tf_op jit(solution)/shard_map/all_to_all | solution.py:516
  11.1 1.2 %copy-start = (f32[2,128,1024]{2,1,0:T(8,128)S(1)}, f32[2,128,1024]{2,1,0:T(8,128)}, u32[]{:S(2)}) copy-start(f32[2,128,1024]{2,1,0:T(8,128)} %force.3) | copy-start | bytes 3145732
  13.8 5.8 %collective-permute-start = (f32[1536,128]{1,0:T(8,128)S(1)}, f32[1536,128]{1,0:T(8,128)}, u32[]{:S(2)}, u32[]{:S(2)}) collective-permute-start(f32[1536,128]{1,0:T(8,128)S(1)} %keep_own.1), channel_id=1, source_target_pairs={{0,16},{16,0},{32,48},{48,32},{64,80},{80,64},{96,112},{112,96},{1... | collective-permute-start | bytes 2359304 | tf_op jit(solution)/shard_map/ppermute | solution.py:501
  15.1 21.0 %collective-permute-start.2 = (f32[2,384,128]{2,1,0:T(8,128)}, f32[2,384,128]{2,1,0:T(8,128)}, u32[]{:S(2)}, u32[]{:S(2)}) collective-permute-start(f32[2,384,128]{2,1,0:T(8,128)} %bitcast.7.coarse), channel_id=1, source_target_pairs={{0,96},{16,112},{32,0},{48,16},{64,32},{80,48},{96,64},{112,80},{1... | collective-permute-start | bytes 1179656 | tf_op jit(solution)/shard_map/ppermute | solution.py:496
  18.9 18.1 %collective-permute-start.3 = (f32[2,384,128]{2,1,0:T(8,128)}, f32[2,384,128]{2,1,0:T(8,128)}, u32[]{:S(2)}, u32[]{:S(2)}) collective-permute-start(f32[2,384,128]{2,1,0:T(8,128)} %bitcast.7.coarse), channel_id=1, source_target_pairs={{0,64},{16,80},{32,96},{48,112},{64,0},{80,16},{96,32},{112,48},{1... | collective-permute-start | bytes 1179656 | tf_op jit(solution)/shard_map/ppermute | solution.py:496
  18.9 20.7 %collective-permute-start.4 = (f32[2,384,128]{2,1,0:T(8,128)}, f32[2,384,128]{2,1,0:T(8,128)}, u32[]{:S(2)}, u32[]{:S(2)}) collective-permute-start(f32[2,384,128]{2,1,0:T(8,128)} %bitcast.7.coarse), channel_id=1, source_target_pairs={{0,32},{16,48},{32,64},{48,80},{64,96},{80,112},{96,0},{112,16},{1... | collective-permute-start | bytes 1179656 | tf_op jit(solution)/shard_map/ppermute | solution.py:496
  19.5 22.5 %collective-permute-start.1 = (f32[1536,128]{1,0:T(8,128)}, f32[1536,128]{1,0:T(8,128)}, u32[]{:S(2)}, u32[]{:S(2)}) collective-permute-start(f32[1536,128]{1,0:T(8,128)} %collective-permute-done), channel_id=1, source_target_pairs={{0,16},{16,0},{32,48},{48,32},{64,80},{80,64},{96,112},{112,96},{1... | collective-permute-start | bytes 2359304 | tf_op jit(solution)/shard_map/ppermute | solution.py:501
  20.5 19.9 %collective-permute-start.5 = (f32[2,384,128]{2,1,0:T(8,128)}, f32[2,384,128]{2,1,0:T(8,128)}, u32[]{:S(2)}, u32[]{:S(2)}) collective-permute-start(f32[2,384,128]{2,1,0:T(8,128)} %bitcast.7.coarse), channel_id=1, source_target_pairs={{0,16},{16,0},{32,48},{48,32},{64,80},{80,64},{96,112},{112,96},{1... | collective-permute-start | bytes 1179656 | tf_op jit(solution)/shard_map/ppermute | solution.py:501
  36.1 4.3 %collective-permute-start.6 = (f32[2,384,128]{2,1,0:T(8,128)}, f32[2,384,128]{2,1,0:T(8,128)}, u32[]{:S(2)}, u32[]{:S(2)}) collective-permute-start(f32[2,384,128]{2,1,0:T(8,128)} %collective-permute-done.2.refs_1_), channel_id=1, source_target_pairs={{0,16},{16,0},{32,48},{48,32},{64,80},{80,64},{96,112},{112,96},{1... | collective-permute-start | bytes 1179656 | tf_op jit(solution)/shard_map/ppermute | solution.py:501
  36.9 3.5 %collective-permute-start.7 = (f32[2,384,128]{2,1,0:T(8,128)}, f32[2,384,128]{2,1,0:T(8,128)}, u32[]{:S(2)}, u32[]{:S(2)}) collective-permute-start(f32[2,384,128]{2,1,0:T(8,128)} %collective-permute-done.3.refs_2_), channel_id=1, source_target_pairs={{0,16},{16,0},{32,48},{48,32},{64,80},{80,64},{96,112},{112,96},{1... | collective-permute-start | bytes 1179656 | tf_op jit(solution)/shard_map/ppermute | solution.py:501
  39.6 2.4 %collective-permute-start.8 = (f32[2,384,128]{2,1,0:T(8,128)}, f32[2,384,128]{2,1,0:T(8,128)}, u32[]{:S(2)}, u32[]{:S(2)}) collective-permute-start(f32[2,384,128]{2,1,0:T(8,128)} %collective-permute-done.4.refs_3_), channel_id=1, source_target_pairs={{0,16},{16,0},{32,48},{48,32},{64,80},{80,64},{96,112},{112,96},{1... | collective-permute-start | bytes 1179656 | tf_op jit(solution)/shard_map/ppermute | solution.py:501
  48.6 17.2 %copy-start.1 = (f32[2,128,1024]{2,1,0:T(8,128)S(1)}, f32[2,128,1024]{2,1,0:T(8,128)}, u32[]{:S(2)}) copy-start(f32[2,128,1024]{2,1,0:T(8,128)} %force.3) | copy-start | bytes 3145732
  51.4 6.6 %collective-permute-start.9 = (f32[3,8,128]{2,1,0:T(8,128)S(1)}, f32[3,8,128]{2,1,0:T(8,128)S(1)}, u32[]{:S(2)}, u32[]{:S(2)}) collective-permute-start(f32[3,8,128]{2,1,0:T(8,128)S(1)} %get-tuple-element.21), channel_id=1, source_target_pairs={{1,2},{3,4},{5,6},{7,8},{9,10},{11,12},{13,14},{2,1},{4,3},{6,5},{... | collective-permute-start | bytes 36872 | tf_op jit(solution)/shard_map/ppermute | solution.py:491
  57.0 2.9 %collective-permute-start.10 = (f32[3,8,128]{2,1,0:T(8,128)S(1)}, f32[3,8,128]{2,1,0:T(8,128)S(1)}, u32[]{:S(2)}, u32[]{:S(2)}) collective-permute-start(f32[3,8,128]{2,1,0:T(8,128)S(1)} %get-tuple-element.20), channel_id=1, source_target_pairs={{0,1},{2,3},{4,5},{6,7},{8,9},{10,11},{12,13},{14,15},{1,0},{3,2},... | collective-permute-start | bytes 36872 | tf_op jit(solution)/shard_map/ppermute | solution.py:491
  60.1 8.1 %collective-permute-start.11 = (f32[3,8,1152]{2,1,0:T(8,128)S(1)}, f32[3,8,1152]{2,1,0:T(8,128)S(1)}, u32[]{:S(2)}, u32[]{:S(2)}) collective-permute-start(f32[3,8,1152]{2,1,0:T(8,128)S(1)} %get-tuple-element.19), channel_id=1, source_target_pairs={{16,32},{48,64},{80,96},{32,16},{64,48},{96,80},{17,33},{49,65},{8... | collective-permute-start | bytes 331784 | tf_op jit(solution)/shard_map/ppermute | solution.py:491
  65.7 2.4 %collective-permute-start.12 = (f32[3,8,1152]{2,1,0:T(8,128)S(1)}, f32[3,8,1152]{2,1,0:T(8,128)S(1)}, u32[]{:S(2)}, u32[]{:S(2)}) collective-permute-start(f32[3,8,1152]{2,1,0:T(8,128)S(1)} %get-tuple-element.18), channel_id=1, source_target_pairs={{0,16},{32,48},{64,80},{96,112},{16,0},{48,32},{80,64},{112,96},{1... | collective-permute-start | bytes 331784 | tf_op jit(solution)/shard_map/ppermute | solution.py:491

commit v7 on v6

--- a/solution.py
+++ b/solution.py
@@ -452,12 +452,13 @@
         return pltpu.make_async_copy(source, out.at[field, :, cols], out_sems.at[field, block])
 
     now = (SWEEPS - 2) % 2
-    for field in range(2):
-        for t, done in relaxed(now, field):
-            for block in range(SLOTS):
-                done_v[field, block, rows_of(t), :] = done[:, block * CELLS : (block + 1) * CELLS]
-        for block in range(SLOTS):
-            out_copy(field, block).start()
+    for blocks in (range(SLOTS // 2), range(SLOTS // 2, SLOTS)):
+        for field in range(2):
+            for t, done in relaxed(now, field):
+                for block in blocks:
+                    done_v[field, block, rows_of(t), :] = done[:, block * CELLS : (block + 1) * CELLS]
+            for block in blocks:
+                out_copy(field, block).start()
     for field in range(2):
         for block in range(SLOTS):
             out_copy(field, block).wait()

time: 74.4 us -> 74.5 us (level)
  no operation moved by 1% of the time
where the time goes in v7:
time: 74.5 us; the launch traced here: 73.5 us
  waiting for transfers between devices  30 us (40%)
  starting transfers between devices  27 us (36%)
  Pallas kernels  14.3 us (19%)
  local copies, waits for them, and re-layouts  1.26 us (2%)
  between operations  0.83 us (1%)
    ppermute x3, waiting for transfers between devices, around_ring(): lax.ppermute(value, axis, [(i, (i + step) % count) for i in range(count)])  18.1 us
    ppermute x4, starting transfers between devices, paired(): return lax.ppermute(value, axis, pairs + [(j, i) for i, j in pairs])  11.3 us
    all_to_all x1, starting transfers between devices, body(): lax.all_to_all(outgoing, 'gy', split_axis=0, concat_axis=0, tiled=True, a...  7.51 us
    all_to_all x1, waiting for transfers between devices, body(): lax.all_to_all(outgoing, 'gy', split_axis=0, concat_axis=0, tiled=True, a...  6.64 us
    pallas_call x1, Pallas kernels, sweeps(): pl.pallas_call(sweep_kernel, out_shape=jax.ShapeDtypeStruct((2, CELLS, WI...  5.66 us
    ppermute x3, starting transfers between devices, around_ring(): lax.ppermute(value, axis, [(i, (i + step) % count) for i in range(count)])  4.43 us
    ppermute x6, starting transfers between devices, swapped(): return lax.ppermute(value, axis, [(i, i ^ bit) for i in range(count)])  3.84 us
    ppermute x4, waiting for transfers between devices, paired(): return lax.ppermute(value, axis, pairs + [(j, i) for i, j in pairs])  3.64 us
  transfers between devices with their start and end apart: 14, of which 7 were waited for; matrix products, arithmetic and copies ran while one was open for 0% of the time, Pallas kernels for 4%

profile of v7, /device:TPU:7, one launch (start us, length us, event | category | flops | bytes accessed | tf_op | source)
XLA Modules:
  0.0 73.5 jit_solution(15346119083769162146)
XLA Ops:
  0.6 2.9 %stage_outgoing.1 = f32[16,392,128]{2,1,0:T(8,128)} custom-call(s32[8]{0:T(128)} %bitcast.22, f32[8,384,128]{2,1,0:T(8,128)} %bitcast.21), custom_call_target="tpu_custom_call" | custom-call | tf_op jit(solution)/shard_map/stage_outgoing/pallas_call | solution.py:85
  3.6 7.5 %all-to-all-start = ((f32[16,392,128]{2,1,0:T(8,128)}), f32[16,392,128]{2,1,0:T(8,128)S(1)}, u32[]{:S(2)}, u32[]{:S(2)}) async-start(f32[16,392,128]{2,1,0:T(8,128)} %stage_outgoing.1), calls=%async_computation | async-start | bytes 6422528 | tf_op jit(solution)/shard_map/all_to_all | solution.py:517
  11.1 1.2 %copy-done = f32[2,128,1024]{2,1,0:T(8,128)S(1)} copy-done((f32[2,128,1024]{2,1,0:T(8,128)S(1)}, f32[2,128,1024]{2,1,0:T(8,128)}, u32[]{:S(2)}) %copy-start) | copy-done | bytes 1048600
  12.3 1.5 %keep_own.1 = f32[1536,128]{1,0:T(8,128)S(1)} custom-call(f32[2,128,1024]{2,1,0:T(8,128)S(1)} %copy-done, f32[2,384,128]{2,1,0:T(8,128)} %bitcast.7.coarse), custom_call_target="tpu_custom_call" | custom-call | flops 262144 | bytes 3145728 | tf_op jit(solution)/shard_map/keep_own/pallas_call | solution.py:132
  13.8 1.3 %collective-permute-start = (f32[1536,128]{1,0:T(8,128)S(1)}, f32[1536,128]{1,0:T(8,128)}, u32[]{:S(2)}, u32[]{:S(2)}) collective-permute-start(f32[1536,128]{1,0:T(8,128)S(1)} %keep_own.1), channel_id=1, source_target_pairs={{0,16},{16,0},{32,48},{48,32},{64,80},{80,64},{96,112},{112,96},{1... | collective-permute-start | bytes 2359304 | tf_op jit(solution)/shard_map/ppermute | solution.py:502
  15.1 3.6 %collective-permute-start.2 = (f32[2,384,128]{2,1,0:T(8,128)}, f32[2,384,128]{2,1,0:T(8,128)}, u32[]{:S(2)}, u32[]{:S(2)}) collective-permute-start(f32[2,384,128]{2,1,0:T(8,128)} %bitcast.7.coarse), channel_id=1, source_target_pairs={{0,96},{16,112},{32,0},{48,16},{64,32},{80,48},{96,64},{112,80},{1... | collective-permute-start | bytes 1179656 | tf_op jit(solution)/shard_map/ppermute | solution.py:497
  18.7 0.8 %collective-permute-start.4 = (f32[2,384,128]{2,1,0:T(8,128)}, f32[2,384,128]{2,1,0:T(8,128)}, u32[]{:S(2)}, u32[]{:S(2)}) collective-permute-start(f32[2,384,128]{2,1,0:T(8,128)} %bitcast.7.coarse), channel_id=1, source_target_pairs={{0,32},{16,48},{32,64},{48,80},{64,96},{80,112},{96,0},{112,16},{1... | collective-permute-start | bytes 1179656 | tf_op jit(solution)/shard_map/ppermute | solution.py:497
  19.5 0.9 %collective-permute-start.1 = (f32[1536,128]{1,0:T(8,128)}, f32[1536,128]{1,0:T(8,128)}, u32[]{:S(2)}, u32[]{:S(2)}) collective-permute-start(f32[1536,128]{1,0:T(8,128)} %collective-permute-done), channel_id=1, source_target_pairs={{0,16},{16,0},{32,48},{48,32},{64,80},{80,64},{96,112},{112,96},{1... | collective-permute-start | bytes 2359304 | tf_op jit(solution)/shard_map/ppermute | solution.py:502
  20.4 15.5 %collective-permute-done.2.refs_1_ = f32[2,384,128]{2,1,0:T(8,128)} collective-permute-done((f32[2,384,128]{2,1,0:T(8,128)}, f32[2,384,128]{2,1,0:T(8,128)}, u32[]{:S(2)}, u32[]{:S(2)}) %collective-permute-start.2) | collective-permute-done | bytes 393248 | tf_op jit(solution)/shard_map/ppermute | solution.py:497
  35.9 0.9 %collective-permute-start.6 = (f32[2,384,128]{2,1,0:T(8,128)}, f32[2,384,128]{2,1,0:T(8,128)}, u32[]{:S(2)}, u32[]{:S(2)}) collective-permute-start(f32[2,384,128]{2,1,0:T(8,128)} %collective-permute-done.2.refs_1_), channel_id=1, source_target_pairs={{0,16},{16,0},{32,48},{48,32},{64,80},{80,64},{96,112},{112,96},{1... | collective-permute-start | bytes 1179656 | tf_op jit(solution)/shard_map/ppermute | solution.py:502
  36.8 2.6 %collective-permute-done.4.refs_3_ = f32[2,384,128]{2,1,0:T(8,128)} collective-permute-done((f32[2,384,128]{2,1,0:T(8,128)}, f32[2,384,128]{2,1,0:T(8,128)}, u32[]{:S(2)}, u32[]{:S(2)}) %collective-permute-start.4) | collective-permute-done | bytes 393248 | tf_op jit(solution)/shard_map/ppermute | solution.py:497
  39.4 0.8 %collective-permute-start.8 = (f32[2,384,128]{2,1,0:T(8,128)}, f32[2,384,128]{2,1,0:T(8,128)}, u32[]{:S(2)}, u32[]{:S(2)}) collective-permute-start(f32[2,384,128]{2,1,0:T(8,128)} %collective-permute-done.4.refs_3_), channel_id=1, source_target_pairs={{0,16},{16,0},{32,48},{48,32},{64,80},{80,64},{96,112},{112,96},{1... | collective-permute-start | bytes 1179656 | tf_op jit(solution)/shard_map/ppermute | solution.py:502
  40.3 1.6 %collective-permute-done.8.refs_7_ = f32[2,384,128]{2,1,0:T(8,128)} collective-permute-done((f32[2,384,128]{2,1,0:T(8,128)}, f32[2,384,128]{2,1,0:T(8,128)}, u32[]{:S(2)}, u32[]{:S(2)}) %collective-permute-start.8) | collective-permute-done | bytes 393248 | tf_op jit(solution)/shard_map/ppermute | solution.py:502
  41.9 6.6 %all-to-all-done.arrived = f32[16,392,128]{2,1,0:T(8,128)S(1)} async-done(((f32[16,392,128]{2,1,0:T(8,128)}), f32[16,392,128]{2,1,0:T(8,128)S(1)}, u32[]{:S(2)}, u32[]{:S(2)}) %all-to-all-start) | async-done | bytes 3211296 | tf_op jit(solution)/shard_map/all_to_all | solution.py:517
  48.5 2.7 %block_outline.1 = (s32[8]{0:T(128)S(1)}, f32[2,384,128]{2,1,0:T(8,128)S(1)}, f32[2,3,8,128]{3,2,1,0:T(8,128)S(1)}, f32[2,3,8,8,128]{4,3,2,1,0:T(8,128)S(1)}) custom-call(s32[8]{0:T(128)S(1)} %bitcast.18, s32[8]{0:T(128)S(1)} %bitcast.20, s32[1]{0:T(128)S(6)} %add.3.owner, f32[16,392,128]{2,1,0:T(8,128)S(1)} %all-to-all-done.arrived, ...), custom_call_target="tpu_custom_call" | custom-call | tf_op jit(solution)/shard_map/block_outline/pallas_call | solution.py:271
  51.2 5.9 %collective-permute-start.9 = (f32[3,8,128]{2,1,0:T(8,128)S(1)}, f32[3,8,128]{2,1,0:T(8,128)S(1)}, u32[]{:S(2)}, u32[]{:S(2)}) collective-permute-start(f32[3,8,128]{2,1,0:T(8,128)S(1)} %get-tuple-element.21), channel_id=1, source_target_pairs={{1,2},{3,4},{5,6},{7,8},{9,10},{11,12},{13,14},{2,1},{4,3},{6,5},{... | collective-permute-start | bytes 36872 | tf_op jit(solution)/shard_map/ppermute | solution.py:492
  57.1 0.1 collective-permute-start.10
  57.2 1.0 %collective-permute-done.9.second = f32[3,8,128]{2,1,0:T(8,128)S(1)} collective-permute-done((f32[3,8,128]{2,1,0:T(8,128)S(1)}, f32[3,8,128]{2,1,0:T(8,128)S(1)}, u32[]{:S(2)}, u32[]{:S(2)}) %collective-permute-start.9) | collective-permute-done | bytes 12320 | tf_op jit(solution)/shard_map/ppermute | solution.py:492
  58.1 1.9 %collective-permute-done.10.first = f32[3,8,128]{2,1,0:T(8,128)S(1)} collective-permute-done((f32[3,8,128]{2,1,0:T(8,128)S(1)}, f32[3,8,128]{2,1,0:T(8,128)S(1)}, u32[]{:S(2)}, u32[]{:S(2)}) %collective-permute-start.10) | collective-permute-done | bytes 12320 | tf_op jit(solution)/shard_map/ppermute | solution.py:492
  60.0 0.1 edge_rows.1
  60.2 5.2 %collective-permute-start.11 = (f32[3,8,1152]{2,1,0:T(8,128)S(1)}, f32[3,8,1152]{2,1,0:T(8,128)S(1)}, u32[]{:S(2)}, u32[]{:S(2)}) collective-permute-start(f32[3,8,1152]{2,1,0:T(8,128)S(1)} %get-tuple-element.19), channel_id=1, source_target_pairs={{16,32},{48,64},{80,96},{32,16},{64,48},{96,80},{17,33},{49,65},{8... | collective-permute-start | bytes 331784 | tf_op jit(solution)/shard_map/ppermute | solution.py:492
  65.5 1.5 %block_interior.1 = (f32[128,1024]{1,0:T(8,128)}, f32[3,8,144,128]{3,2,1,0:T(8,128)S(1)}) custom-call(s32[8]{0:T(128)S(1)} %get-tuple-element.10.source, f32[16,392,128]{2,1,0:T(8,128)S(1)} %all-to-all-done.arrived, f32[2,384,128]{2,1,0:T(8,128)S(1)} %get-tuple-element.11.fresh, f32[2,128,1024]{2,1,0:T(8,128)S(1)} %copy-done.1), custom_call_target="tpu_custom_call" | custom-call | flops 1048576 | bytes 6291456 | tf_op jit(solution)/shard_map/block_interior/pallas_call | solution.py:324
  67.0 0.8 %collective-permute-done.11.second = f32[3,8,1152]{2,1,0:T(8,128)S(1)} collective-permute-done((f32[3,8,1152]{2,1,0:T(8,128)S(1)}, f32[3,8,1152]{2,1,0:T(8,128)S(1)}, u32[]{:S(2)}, u32[]{:S(2)}) %collective-permute-start.11) | collective-permute-done | bytes 110624 | tf_op jit(solution)/shard_map/ppermute | solution.py:492
  67.8 5.7 %jacobi_sweeps.1 = f32[2,128,1024]{2,1,0:T(8,128)} custom-call(f32[3,8,144,128]{3,2,1,0:T(8,128)S(1)} %get-tuple-element.13.inner, f32[3,144,128]{2,1,0:T(8,128)S(1)} %get-tuple-element.16.side, f32[3,8,1152]{2,1,0:T(8,128)S(1)} %collective-permute-done.11.second, f32[3,8,1152]{2,1,0:T(8,128)S(1)} %collective-permute-done.12.first), custom_call_target="tpu_custom_call" | custom-call | tf_op jit(solution)/shard_map/jacobi_sweeps/pallas_call | solution.py:470
  (20 shorter events, 0.2 us)
Async XLA Ops:
  3.5 36.6 %copy-start.3 = (s32[1,8]{1,0:T(1,128)S(1)}, s32[1,8]{1,0:T(1,128)}, u32[]{:S(2)}) copy-start(s32[1,8]{1,0:T(1,128)} %param.9) | copy-start | bytes 100
  3.6 45.0 %copy-start.2 = (s32[1,8]{1,0:T(1,128)S(1)}, s32[1,8]{1,0:T(1,128)}, u32[]{:S(2)}) copy-start(s32[1,8]{1,0:T(1,128)} %param.8) | copy-start | bytes 100
  3.6 45.0 %all-to-all-start = ((f32[16,392,128]{2,1,0:T(8,128)}), f32[16,392,128]{2,1,0:T(8,128)S(1)}, u32[]{:S(2)}, u32[]{:S(2)}) async-start(f32[16,392,128]{2,1,0:T(8,128)} %stage_outgoing.1), calls=%async_computation | async-start | bytes 6422528 | tf_op jit(solution)/shard_map/all_to_all | solution.py:517
  11.1 1.2 %copy-start = (f32[2,128,1024]{2,1,0:T(8,128)S(1)}, f32[2,128,1024]{2,1,0:T(8,128)}, u32[]{:S(2)}) copy-start(f32[2,128,1024]{2,1,0:T(8,128)} %force.3) | copy-start | bytes 3145732
  13.8 5.7 %collective-permute-start = (f32[1536,128]{1,0:T(8,128)S(1)}, f32[1536,128]{1,0:T(8,128)}, u32[]{:S(2)}, u32[]{:S(2)}) collective-permute-start(f32[1536,128]{1,0:T(8,128)S(1)} %keep_own.1), channel_id=1, source_target_pairs={{0,16},{16,0},{32,48},{48,32},{64,80},{80,64},{96,112},{112,96},{1... | collective-permute-start | bytes 2359304 | tf_op jit(solution)/shard_map/ppermute | solution.py:502
  15.1 20.8 %collective-permute-start.2 = (f32[2,384,128]{2,1,0:T(8,128)}, f32[2,384,128]{2,1,0:T(8,128)}, u32[]{:S(2)}, u32[]{:S(2)}) collective-permute-start(f32[2,384,128]{2,1,0:T(8,128)} %bitcast.7.coarse), channel_id=1, source_target_pairs={{0,96},{16,112},{32,0},{48,16},{64,32},{80,48},{96,64},{112,80},{1... | collective-permute-start | bytes 1179656 | tf_op jit(solution)/shard_map/ppermute | solution.py:497
  18.7 18.1 %collective-permute-start.3 = (f32[2,384,128]{2,1,0:T(8,128)}, f32[2,384,128]{2,1,0:T(8,128)}, u32[]{:S(2)}, u32[]{:S(2)}) collective-permute-start(f32[2,384,128]{2,1,0:T(8,128)} %bitcast.7.coarse), channel_id=1, source_target_pairs={{0,64},{16,80},{32,96},{48,112},{64,0},{80,16},{96,32},{112,48},{1... | collective-permute-start | bytes 1179656 | tf_op jit(solution)/shard_map/ppermute | solution.py:497
  18.7 20.7 %collective-permute-start.4 = (f32[2,384,128]{2,1,0:T(8,128)}, f32[2,384,128]{2,1,0:T(8,128)}, u32[]{:S(2)}, u32[]{:S(2)}) collective-permute-start(f32[2,384,128]{2,1,0:T(8,128)} %bitcast.7.coarse), channel_id=1, source_target_pairs={{0,32},{16,48},{32,64},{48,80},{64,96},{80,112},{96,0},{112,16},{1... | collective-permute-start | bytes 1179656 | tf_op jit(solution)/shard_map/ppermute | solution.py:497
  19.5 22.3 %collective-permute-start.1 = (f32[1536,128]{1,0:T(8,128)}, f32[1536,128]{1,0:T(8,128)}, u32[]{:S(2)}, u32[]{:S(2)}) collective-permute-start(f32[1536,128]{1,0:T(8,128)} %collective-permute-done), channel_id=1, source_target_pairs={{0,16},{16,0},{32,48},{48,32},{64,80},{80,64},{96,112},{112,96},{1... | collective-permute-start | bytes 2359304 | tf_op jit(solution)/shard_map/ppermute | solution.py:502
  20.4 19.8 %collective-permute-start.5 = (f32[2,384,128]{2,1,0:T(8,128)}, f32[2,384,128]{2,1,0:T(8,128)}, u32[]{:S(2)}, u32[]{:S(2)}) collective-permute-start(f32[2,384,128]{2,1,0:T(8,128)} %bitcast.7.coarse), channel_id=1, source_target_pairs={{0,16},{16,0},{32,48},{48,32},{64,80},{80,64},{96,112},{112,96},{1... | collective-permute-start | bytes 1179656 | tf_op jit(solution)/shard_map/ppermute | solution.py:502
  35.9 4.3 %collective-permute-start.6 = (f32[2,384,128]{2,1,0:T(8,128)}, f32[2,384,128]{2,1,0:T(8,128)}, u32[]{:S(2)}, u32[]{:S(2)}) collective-permute-start(f32[2,384,128]{2,1,0:T(8,128)} %collective-permute-done.2.refs_1_), channel_id=1, source_target_pairs={{0,16},{16,0},{32,48},{48,32},{64,80},{80,64},{96,112},{112,96},{1... | collective-permute-start | bytes 1179656 | tf_op jit(solution)/shard_map/ppermute | solution.py:502
  36.8 3.5 %collective-permute-start.7 = (f32[2,384,128]{2,1,0:T(8,128)}, f32[2,384,128]{2,1,0:T(8,128)}, u32[]{:S(2)}, u32[]{:S(2)}) collective-permute-start(f32[2,384,128]{2,1,0:T(8,128)} %collective-permute-done.3.refs_2_), channel_id=1, source_target_pairs={{0,16},{16,0},{32,48},{48,32},{64,80},{80,64},{96,112},{112,96},{1... | collective-permute-start | bytes 1179656 | tf_op jit(solution)/shard_map/ppermute | solution.py:502
  39.4 2.5 %collective-permute-start.8 = (f32[2,384,128]{2,1,0:T(8,128)}, f32[2,384,128]{2,1,0:T(8,128)}, u32[]{:S(2)}, u32[]{:S(2)}) collective-permute-start(f32[2,384,128]{2,1,0:T(8,128)} %collective-permute-done.4.refs_3_), channel_id=1, source_target_pairs={{0,16},{16,0},{32,48},{48,32},{64,80},{80,64},{96,112},{112,96},{1... | collective-permute-start | bytes 1179656 | tf_op jit(solution)/shard_map/ppermute | solution.py:502
  48.5 17.0 %copy-start.1 = (f32[2,128,1024]{2,1,0:T(8,128)S(1)}, f32[2,128,1024]{2,1,0:T(8,128)}, u32[]{:S(2)}) copy-start(f32[2,128,1024]{2,1,0:T(8,128)} %force.3) | copy-start | bytes 3145732
  51.2 6.9 %collective-permute-start.9 = (f32[3,8,128]{2,1,0:T(8,128)S(1)}, f32[3,8,128]{2,1,0:T(8,128)S(1)}, u32[]{:S(2)}, u32[]{:S(2)}) collective-permute-start(f32[3,8,128]{2,1,0:T(8,128)S(1)} %get-tuple-element.21), channel_id=1, source_target_pairs={{1,2},{3,4},{5,6},{7,8},{9,10},{11,12},{13,14},{2,1},{4,3},{6,5},{... | collective-permute-start | bytes 36872 | tf_op jit(solution)/shard_map/ppermute | solution.py:492
  57.1 2.9 %collective-permute-start.10 = (f32[3,8,128]{2,1,0:T(8,128)S(1)}, f32[3,8,128]{2,1,0:T(8,128)S(1)}, u32[]{:S(2)}, u32[]{:S(2)}) collective-permute-start(f32[3,8,128]{2,1,0:T(8,128)S(1)} %get-tuple-element.20), channel_id=1, source_target_pairs={{0,1},{2,3},{4,5},{6,7},{8,9},{10,11},{12,13},{14,15},{1,0},{3,2},... | collective-permute-start | bytes 36872 | tf_op jit(solution)/shard_map/ppermute | solution.py:492
  60.2 7.7 %collective-permute-start.11 = (f32[3,8,1152]{2,1,0:T(8,128)S(1)}, f32[3,8,1152]{2,1,0:T(8,128)S(1)}, u32[]{:S(2)}, u32[]{:S(2)}) collective-permute-start(f32[3,8,1152]{2,1,0:T(8,128)S(1)} %get-tuple-element.19), channel_id=1, source_target_pairs={{16,32},{48,64},{80,96},{32,16},{64,48},{96,80},{17,33},{49,65},{8... | collective-permute-start | bytes 331784 | tf_op jit(solution)/shard_map/ppermute | solution.py:492
  65.4 2.4 %collective-permute-start.12 = (f32[3,8,1152]{2,1,0:T(8,128)S(1)}, f32[3,8,1152]{2,1,0:T(8,128)S(1)}, u32[]{:S(2)}, u32[]{:S(2)}) collective-permute-start(f32[3,8,1152]{2,1,0:T(8,128)S(1)} %get-tuple-element.18), channel_id=1, source_target_pairs={{0,16},{32,48},{64,80},{96,112},{16,0},{48,32},{80,64},{112,96},{1... | collective-permute-start | bytes 331784 | tf_op jit(solution)/shard_map/ppermute | solution.py:492
